TPU v7x, 32 devices: a whole 2x2x4 slice. The times are simulated.
32 devices in a mesh: groups: 2 (over y), workers: 4 (over z), team: 2 (over x), sub: 2 (over core).
Axes of the slice: x: 2, y: 2, z: 4, core: 2. Of those that a mesh axis runs over, the one named last changes fastest.
Arguments:
- embeddings: bfloat16 [8192, 1024], P(('groups', 'workers', 'team', 'sub')), parts along dimension 0, may hold values from -6 to 6
- owner_ids: int32 [8192, 1], P(('groups', 'workers', 'team', 'sub')), parts along dimension 0, may hold values from 0 to 3; in each aligned block of 256 rows (0 to 255, 256 to 511, ...) at most 160 rows name the same one
- clusters: int32 [8192], P(('groups', 'workers', 'team', 'sub')), parts along dimension 0, may hold values from 0 to 15
- priority: int32 [8192], P(('groups', 'workers', 'team', 'sub')), parts along dimension 0, may hold values from 0 to 4095, each once
Outputs:
- max_similarity: float32 [8192], P(('groups', 'workers', 'team', 'sub')), parts along dimension 0
There are 2 independent parts, one for each index of `groups`. A program takes and returns all parts, laid end to end along the dimension named above; each array names one. Nothing has to cross between parts.
Inputs may be any that keep to these rules, and one draw needn't show every extreme that they name: `owner_ids`: in the rows of one device no worker is named by more than 160 rows, a bound that some block reaches of them. `priority`: within one part every value appears exactly once.
All inputs are finite; a program needn't handle non-finite values.
Results may differ from a plain program's by a relative error of at most 0.0009.
Values may be sent and summed in bfloat16 or wider, within the bound.
No kernel may reach another device: no remote copies, remote signals or barrier semaphores. Data moves between devices by JAX's collectives and lax.ppermute only.
A program may use at most 64 MiB of HBM per device.

v0:
```python
import jax
import jax.numpy as jnp
from jax import lax
from jax.sharding import PartitionSpec as P


def earlier_max(scores, qclus, qprio, kclus, kprio, axis):
    mask = (
        (qclus[:, None] == kclus[None, :])
        & (kprio[None, :] < qprio[:, None])
        & (kclus[None, :] >= 0)
    )
    return jnp.max(jnp.where(mask, scores, jnp.float32(-1.0)), axis=axis)


def similar(left, right):
    return lax.dot_general(
        left, right, (((1,), (1,)), ((), ())), preferred_element_type=jnp.float32
    )


def on_device(embeddings, owner_ids, clusters, priority):
    rows_dev, width = embeddings.shape
    n_work = lax.axis_size("workers")
    cap = max(2, 5 * rows_dev // (2 * n_work))
    slots = n_work * cap
    values = embeddings.astype(jnp.float32)
    normed = (values * lax.rsqrt(jnp.sum(values * values, axis=1, keepdims=True) + 1e-06)).astype(
        jnp.bfloat16
    )
    owner = owner_ids[:, 0]
    onehot = (owner[:, None] == jnp.arange(n_work, dtype=jnp.int32)[None, :]).astype(jnp.int32)
    before = jnp.cumsum(onehot, axis=0) - onehot
    rank = jnp.sum(before * onehot, axis=1)
    slot = owner * cap + rank
    send_rows = jnp.zeros((slots, width), jnp.bfloat16).at[slot].set(normed)
    send_clus = jnp.full((slots,), -1, jnp.int32).at[slot].set(clusters)
    send_prio = jnp.zeros((slots,), jnp.int32).at[slot].set(priority)
    got_rows, got_clus, got_prio = (
        lax.all_to_all(
            send_rows.reshape(n_work, cap, width),
            "workers",
            split_axis=0,
            concat_axis=0,
            tiled=True,
        ),
        lax.all_to_all(
            send_clus.reshape(n_work, cap), "workers", split_axis=0, concat_axis=0, tiled=True
        ),
        lax.all_to_all(
            send_prio.reshape(n_work, cap), "workers", split_axis=0, concat_axis=0, tiled=True
        ),
    )
    got_rows = got_rows.reshape(slots, width)
    got_clus = got_clus.reshape(slots)
    got_prio = got_prio.reshape(slots)
    start_best = jnp.full((slots,), -1.0, jnp.float32)
    key_rows = lax.all_gather(got_rows, ("team", "sub"), axis=0, tiled=True)
    key_clus = lax.all_gather(got_clus, ("team", "sub"), axis=0, tiled=True)
    key_prio = lax.all_gather(got_prio, ("team", "sub"), axis=0, tiled=True)
    scores = similar(got_rows, key_rows)
    best = jnp.maximum(start_best, earlier_max(scores, got_clus, got_prio, key_clus, key_prio, 1))
    returned = lax.all_to_all(
        best.reshape(n_work, cap), "workers", split_axis=0, concat_axis=0, tiled=True
    ).reshape(slots)
    return returned[slot]


def solution(mesh):
    placed = (
        P(("groups", "workers", "team", "sub"), None),
        P(("groups", "workers", "team", "sub"), None),
        P(("groups", "workers", "team", "sub")),
        P(("groups", "workers", "team", "sub")),
    )
    return jax.shard_map(
        on_device,
        mesh=mesh,
        in_specs=placed,
        out_specs=P(("groups", "workers", "team", "sub")),
        check_vma=False,
    )
```

profile of v0, /device:TPU:0, one launch (start us, length us, event | category | flops | bytes accessed | tf_op | source)
XLA Modules:
  0.0 118.2 jit_solution(4265124096970569698)
XLA Ops:
  6.5 1.2 %fusion = f32[256]{0:T(256)S(1)} fusion(bf16[256,1024]{1,0:T(8,128)(2,1)} %param.4), kind=kLoop, calls=%fused_computation.7 | loop fusion | flops 786176 | bytes 525312 | tf_op jit(solution)/shard_map/reduce_sum | solution.py:28
  7.8 0.7 compare_convert_fusion
  8.5 1.2 %reduce-window.6 = s32[4,2,128]{2,1,0:T(2,128)S(1)} reduce-window(s32[4,2,128]{2,1,0:T(2,128)S(1)} %compare_convert_fusion, s32[]{:T(128)} %constant.11.clone.1), window={size=1x1x128 pad=0_0x0_0x127_0}, to_apply=%region_0.0 | reduce-window | flops 130048 | bytes 8196 | tf_op jit(solution)/shard_map/reduce-window
  9.7 0.1 slice.10
  9.7 0.1 copy.11
  9.9 0.1 copy.12
  10.0 0.1 add_bitcast_fusion
  10.1 0.7 fusion.8
  10.8 0.7 compare_select_fusion
  11.4 2.6 %scatter_custom_fusion.2 = bf16[640,1024]{1,0:T(8,128)(2,1)S(1)} fusion(s32[256]{0:T(256)S(1)} %bitcast.35, bf16[]{:T(256)} %constant.13.clone.1, bf16[256,1024]{1,0:T(8,128)(2,1)} %param.4, f32[256]{0:T(256)S(1)} %add_rsqrt_fusion), kind=kCustom, calls=%fused_computation.9 | custom fusion | flops 786432 | bytes 1836034 | tf_op jit(solution)/shard_map/scatter | solution.py:36
  14.0 37.6 %all_to_all.29 = bf16[4,160,1024]{2,1,0:T(8,128)(2,1)} all-to-all(bf16[4,160,1024]{2,1,0:T(8,128)(2,1)S(1)} %bitcast.32), channel_id=1, replica_groups=mesh['groups'=2,'workers'=4,'team'=2,'sub'=2] {'workers'}, dimensions={0} | all-to-all | bytes 2621440 | tf_op jit(solution)/shard_map/all_to_all | solution.py:40
  51.6 1.6 %scatter_custom_fusion = s32[640]{0:T(1024)S(1)} fusion(s32[256]{0:T(256)S(1)} %bitcast.36, s32[256]{0:T(256)} %param.6, s32[]{:T(128)} %constant.9.clone.1), kind=kCustom, calls=%fused_computation.25 | custom fusion | bytes 3072 | tf_op jit(solution)/shard_map/scatter | solution.py:37
  53.2 0.7 all_to_all.19
  53.9 3.2 %all-to-all-start = ((s32[4,1,160]{2,1,0:T(1,128)}), s32[4,1,160]{2,1,0:T(1,128)S(1)}, u32[]{:S(2)}, u32[]{:S(2)}) async-start(s32[4,1,160]{2,1,0:T(1,128)} %all_to_all.19), calls=%async_computation | async-start | bytes 8192 | tf_op jit(solution)/shard_map/all_to_all | solution.py:47
  57.1 1.6 %scatter_custom_fusion.1 = s32[640]{0:T(1024)S(1)} fusion(s32[256]{0:T(256)S(1)} %bitcast.37, s32[256]{0:T(256)} %param.7, s32[]{:T(128)} %constant.11.clone.1), kind=kCustom, calls=%fused_computation.23 | custom fusion | bytes 3072 | tf_op jit(solution)/shard_map/scatter | solution.py:38
  58.7 0.7 all_to_all.21
  59.3 3.1 %all-to-all-done = s32[4,1,160]{2,1,0:T(1,128)S(1)} async-done(((s32[4,1,160]{2,1,0:T(1,128)}), s32[4,1,160]{2,1,0:T(1,128)S(1)}, u32[]{:S(2)}, u32[]{:S(2)}) %all-to-all-start) | async-done | bytes 2592 | tf_op jit(solution)/shard_map/all_to_all | solution.py:47
  62.5 3.2 %all-to-all-start.1 = ((s32[4,1,160]{2,1,0:T(1,128)}), s32[4,1,160]{2,1,0:T(1,128)S(1)}, u32[]{:S(2)}, u32[]{:S(2)}) async-start(s32[4,1,160]{2,1,0:T(1,128)} %all_to_all.21), calls=%async_computation.1 | async-start | bytes 8192 | tf_op jit(solution)/shard_map/all_to_all | solution.py:50
  65.8 0.1 reshape.108
  65.8 0.1 eq.48
  65.9 5.3 %all-to-all-done.1 = s32[4,1,160]{2,1,0:T(1,128)S(1)} async-done(((s32[4,1,160]{2,1,0:T(1,128)}), s32[4,1,160]{2,1,0:T(1,128)S(1)}, u32[]{:S(2)}, u32[]{:S(2)}) %all-to-all-start.1) | async-done | bytes 2592 | tf_op jit(solution)/shard_map/all_to_all | solution.py:50
  71.3 0.1 reshape.110
  71.4 0.1 reshape.72
  71.5 5.2 %all-gather = s32[4,1,640]{2,1,0:T(1,128)S(1)} all-gather(s32[1,1,640]{2,1,0:T(1,128)S(1)} %reshape.108), channel_id=1, replica_groups=mesh['groups'=2,'workers'=4,'team'=2,'sub'=2] {'team','sub'}, dimensions={0}, use_global_device_ids=true | all-gather | bytes 12800 | tf_op jit(solution)/shard_map/all_gather | solution.py:59
  76.7 5.2 %all-gather.1 = s32[4,1,640]{2,1,0:T(1,128)S(1)} all-gather(s32[1,1,640]{2,1,0:T(1,128)S(1)} %reshape.110), channel_id=1, replica_groups=mesh['groups'=2,'workers'=4,'team'=2,'sub'=2] {'team','sub'}, dimensions={0}, use_global_device_ids=true | all-gather | bytes 12800 | tf_op jit(solution)/shard_map/all_gather | solution.py:60
  81.9 9.5 %all-gather.4.cloned.1.call-done = bf16[2560,1024]{1,0:T(8,128)(2,1)} async-done(((bf16[640,1024]{1,0:T(8,128)(2,1)}), bf16[2560,1024]{1,0:T(8,128)(2,1)}) %all-gather.4.cloned.1.call-update) | async-done | bytes 5242896 | tf_op jit(solution)/shard_map/all_gather | solution.py:58
  91.5 7.0 %select_reduce_fusion = f32[640]{0:T(1024)S(1)} fusion(bf16[640,1024]{1,0:T(8,128)(2,1)} %bitcast.31, bf16[2560,1024]{1,0:T(8,128)(2,1)} %all-gather.4.cloned.1.call-done, s32[2560]{0:T(1024)S(1)} %reshape.111, s32[2560]{0:T(1024)S(1)} %reshape.109, s32[640]{0:T(1024)S(1)} %reshape.72, s32[640]{0:T(1024)S(1)} %eq.48, ...), kind=kOutput, calls=%fused_computation.4 | convolution fusion | flops 3365273088 | bytes 6584320 | tf_op jit(solution)/shard_map/dot_general | solution.py:17
  98.5 0.7 max_broadcast_in_dim.15
  99.2 4.6 %all-to-all-start.3 = ((f32[4,1,160]{2,1,0:T(1,128)}), f32[4,1,160]{2,1,0:T(1,128)S(1)}, u32[]{:S(2)}, u32[]{:S(2)}) async-start(f32[4,1,160]{2,1,0:T(1,128)} %max_broadcast_in_dim.15), calls=%async_computation.3 | async-start | bytes 8192 | tf_op jit(solution)/shard_map/all_to_all | solution.py:63
  103.8 5.6 %all-to-all-done.3 = f32[4,1,160]{2,1,0:T(1,128)S(1)} async-done(((f32[4,1,160]{2,1,0:T(1,128)}), f32[4,1,160]{2,1,0:T(1,128)S(1)}, u32[]{:S(2)}, u32[]{:S(2)}) %all-to-all-start.3) | async-done | bytes 2592 | tf_op jit(solution)/shard_map/all_to_all | solution.py:63
  109.4 0.1 reshape.75
  109.5 1.9 %gather_fusion = f32[256]{0:T(256)} fusion(f32[640]{0:T(1024)S(1)} %reshape.75, s32[1024]{0:T(1024)S(1)} %pad_clamp_fusion), kind=kCustom, calls=%fused_computation | custom fusion | bytes 3072 | tf_op jit(solution)/shard_map/gather | solution.py:66
  (15 shorter events, 0.3 us)
Async XLA Ops:
  6.5 84.9 %all-gather.4.cloned.1.call-start = ((), (), s32[]{:S(2)}) async-start(), calls=%async_computation.4 | async-start | bytes 6553600 | tf_op jit(solution)/shard_map/all_gather | solution.py:58
  53.9 8.6 %all-to-all-start = ((s32[4,1,160]{2,1,0:T(1,128)}), s32[4,1,160]{2,1,0:T(1,128)S(1)}, u32[]{:S(2)}, u32[]{:S(2)}) async-start(s32[4,1,160]{2,1,0:T(1,128)} %all_to_all.19), calls=%async_computation | async-start | bytes 8192 | tf_op jit(solution)/shard_map/all_to_all | solution.py:47
  62.5 8.8 %all-to-all-start.1 = ((s32[4,1,160]{2,1,0:T(1,128)}), s32[4,1,160]{2,1,0:T(1,128)S(1)}, u32[]{:S(2)}, u32[]{:S(2)}) async-start(s32[4,1,160]{2,1,0:T(1,128)} %all_to_all.21), calls=%async_computation.1 | async-start | bytes 8192 | tf_op jit(solution)/shard_map/all_to_all | solution.py:50
  99.2 10.2 %all-to-all-start.3 = ((f32[4,1,160]{2,1,0:T(1,128)}), f32[4,1,160]{2,1,0:T(1,128)S(1)}, u32[]{:S(2)}, u32[]{:S(2)}) async-start(f32[4,1,160]{2,1,0:T(1,128)} %max_broadcast_in_dim.15), calls=%async_computation.3 | async-start | bytes 8192 | tf_op jit(solution)/shard_map/all_to_all | solution.py:63
Sparse Core Ops, SparseCore 0:
  51.7 39.6 all-gather.3
where the time goes:
time: 119 us; the launch traced here: 118 us
  blocking collectives  47.9 us (40%)
  waiting for transfers between devices  23.6 us (20%)
  between operations  13.5 us (11%)
  starting transfers between devices  11.1 us (9%)
  local copies, waits for them, and re-layouts  7.79 us (7%)
  other arithmetic  7.36 us (6%)
  matrix products  7.03 us (6%)
    all_to_all x1, blocking collectives, on_device(): lax.all_to_all(send_rows.reshape(n_work, cap, width), 'workers', split_ax...  37.6 us
    all_gather x1, waiting for transfers between devices, on_device(): key_rows = lax.all_gather(got_rows, ('team', 'sub'), axis=0, tiled=True)  9.53 us
    dot_general x1, matrix products, similar(): lax.dot_general(left, right, (((1,), (1,)), ((), ())), preferred_element_...  7.03 us
    all_to_all x1, waiting for transfers between devices, on_device(): lax.all_to_all(best.reshape(n_work, cap), 'workers', split_axis=0, concat...  5.57 us
    all_to_all x1, waiting for transfers between devices, on_device(): lax.all_to_all(send_prio.reshape(n_work, cap), 'workers', split_axis=0, c...  5.35 us
    all_gather x1, blocking collectives, on_device(): key_prio = lax.all_gather(got_prio, ('team', 'sub'), axis=0, tiled=True)  5.18 us
    all_gather x1, blocking collectives, on_device(): key_clus = lax.all_gather(got_clus, ('team', 'sub'), axis=0, tiled=True)  5.17 us
    all_to_all x1, starting transfers between devices, on_device(): lax.all_to_all(best.reshape(n_work, cap), 'workers', split_axis=0, concat...  4.59 us
  transfers between devices with their start and end apart: 4, of which 4 were waited for; matrix products, arithmetic and copies ran while one was open for 3% of the time, Pallas kernels for 0%

commit v1 on v0

v1 whole, which is shorter than its diff:
```python
import functools

import jax
import jax.numpy as jnp
from jax import lax
from jax.experimental import pallas as pl
from jax.experimental.pallas import tpu as pltpu
from jax.sharding import PartitionSpec as P

KC = 16
VMEM = pl.BlockSpec(memory_space=pltpu.VMEM)


def normalise(raw):
    values = raw.astype(jnp.float32)
    total = jnp.sum(values * values, axis=1, keepdims=True)
    return (values * lax.rsqrt(total + 1e-06)).astype(jnp.bfloat16)


def code_of(owner, cluster, high, low):
    return ((owner * KC + cluster) * 256 + high) * 256 + low


def payload_code(ref, rows):
    meta = ref[rows : rows + 16, :].astype(jnp.float32)[0:1, :].astype(jnp.int32)
    return code_of(*[meta[:, i * rows : (i + 1) * rows] for i in range(4)])


def as_column(row):
    return jnp.broadcast_to(row, (128, row.shape[1])).T


def fold_rows(best):
    return jnp.max(best.T, axis=0, keepdims=True)


def prepare_kernel(rows, emb, owner, cluster, priority, payload, meta):
    payload[0:rows, :] = normalise(emb[...])
    own = owner[...] + 1
    high = priority[...] // 256
    low = priority[...] % 256
    line = jnp.concatenate([own, cluster[...], high, low], axis=1).astype(jnp.float32)
    width = payload.shape[1]
    first = lax.broadcasted_iota(jnp.int32, (16, width), 0) == 0
    payload[rows : rows + 16, :] = jnp.where(
        first, jnp.broadcast_to(line, (16, width)), 0.0
    ).astype(jnp.bfloat16)
    meta[...] = jnp.concatenate(
        [own, cluster[...], priority[...], jnp.zeros((5, rows), jnp.int32)], axis=0
    )


def scores_of(left, right):
    return lax.dot_general(
        left, right, (((1,), (1,)), ((), ())), preferred_element_type=jnp.float32
    )


def own_kernel(rows, n_plane, *refs):
    plane, best = refs[:n_plane], refs[n_plane]
    mine = plane[0][0:rows, :]
    column = as_column(payload_code(plane[0], rows))
    found = jnp.full((rows, 128), -1.0, jnp.float32)
    for block in plane:
        scores = scores_of(mine, block[0:rows, :])
        code = payload_code(block, rows)
        for at in range(0, rows, 128):
            other = code[:, at : at + 128]
            earlier = ((column ^ other) < 65536) & (column > other)
            found = jnp.maximum(found, jnp.where(earlier, scores[:, at : at + 128], -1.0))
    best[...] = fold_rows(found)


def meet_kernel(rows, n_plane, raw, *refs):
    plane = refs[:n_plane]
    if raw:
        came, came_meta, back, kept = refs[n_plane:]
        queries = normalise(came[...])
        owner, cluster, priority = [came_meta[i : i + 1, :] for i in range(3)]
        code = code_of(owner, cluster, priority // 256, priority % 256)
    else:
        came, back, kept = refs[n_plane:]
        queries = came[0:rows, :]
        code = payload_code(came, rows)
    column = as_column(code)
    found = jnp.full((rows, 128), -1.0, jnp.float32)
    for index, block in enumerate(plane):
        scores = scores_of(queries, block[0:rows, :])
        code = payload_code(block, rows)
        for at in range(0, rows, 128):
            other = code[:, at : at + 128]
            shared = jnp.where((column ^ other) < 65536, scores[:, at : at + 128], -1.0)
            later = column > other
            found = jnp.maximum(found, jnp.where(later, shared, -1.0))
            kept[index : index + 1, at : at + 128] = jnp.max(
                jnp.where(later, -1.0, shared), axis=0, keepdims=True
            )
    back[...] = fold_rows(found)


def params():
    return pltpu.CompilerParams(vmem_limit_bytes=40 * 1024 * 1024)


def rounds_of(n):
    half = n // 2
    line = [p // 2 + (p % 2) * half for p in range(2 * half)] + list(range(2 * half, n))
    turns = []
    for step in range(1, (n - 1) // 2 + 1):
        turns.append([(line[p], line[(p + step) % n]) for p in range(n)])
    if n % 2 == 0:
        pairs = [(line[p], line[p + half]) for p in range(half)]
        turns.append([(a, b) if i % 2 == 0 else (b, a) for i, (a, b) in enumerate(pairs)])
    return turns


def shift(n, step):
    return [(i, (i + step) % n) for i in range(n)]


def on_device(embeddings, owner_ids, clusters, priority):
    rows, width = embeddings.shape
    n_work, n_team, n_sub = [lax.axis_size(a) for a in ("workers", "team", "sub")]
    n_plane = n_team * n_sub
    turns = rounds_of(n_work)
    first = lax.ppermute(embeddings, "workers", turns[0]) if turns else None

    payload, meta = pl.pallas_call(
        functools.partial(prepare_kernel, rows),
        out_shape=(
            jax.ShapeDtypeStruct((rows + 16, width), jnp.bfloat16),
            jax.ShapeDtypeStruct((8, rows), jnp.int32),
        ),
        in_specs=[VMEM] * 4,
        out_specs=(VMEM, VMEM),
        compiler_params=params(),
        name="prepare",
    )(
        embeddings,
        owner_ids.reshape(1, rows),
        clusters.reshape(1, rows),
        priority.reshape(1, rows),
    )
    came_meta = lax.ppermute(meta, "workers", turns[0]) if turns else None

    by_team = [payload] + [
        lax.ppermute(payload, "team", shift(n_team, step)) for step in range(1, n_team)
    ]
    plane = []
    for block in by_team:
        plane.append(block)
        for step in range(1, n_sub):
            plane.append(lax.ppermute(block, "sub", shift(n_sub, step)))

    best = pl.pallas_call(
        functools.partial(own_kernel, rows, n_plane),
        out_shape=jax.ShapeDtypeStruct((1, rows), jnp.float32),
        in_specs=[VMEM] * n_plane,
        out_specs=VMEM,
        compiler_params=params(),
        name="own",
    )(*plane)

    kept = jnp.full((n_plane, rows), -1.0, jnp.float32)
    for index in list(range(1, len(turns))) + list(range(min(1, len(turns)))):
        turn = turns[index]
        raw = index == 0
        came = (first, came_meta) if raw else (lax.ppermute(payload, "workers", turn),)
        back, part = pl.pallas_call(
            functools.partial(meet_kernel, rows, n_plane, raw),
            out_shape=(
                jax.ShapeDtypeStruct((1, rows), jnp.float32),
                jax.ShapeDtypeStruct((n_plane, rows), jnp.float32),
            ),
            in_specs=[VMEM] * (n_plane + len(came)),
            out_specs=(VMEM, VMEM),
            compiler_params=params(),
            name="meet",
        )(*plane, *came)
        kept = jnp.maximum(kept, part)
        got = lax.ppermute(back, "workers", [(b, a) for a, b in turn])
        if len(turn) < n_work:
            here = lax.axis_index("workers")
            sent = functools.reduce(jnp.logical_or, [here == a for a, _ in turn])
            got = jnp.where(sent, got, -1.0)
        best = jnp.maximum(best, got)

    kept = kept.reshape(n_team, n_sub, rows)
    ends = kept[:, 0]
    for step in range(1, n_sub):
        ends = jnp.maximum(ends, lax.ppermute(kept[:, step], "sub", shift(n_sub, -step)))
    total = ends[0:1]
    for step in range(1, n_team):
        total = jnp.maximum(
            total, lax.ppermute(ends[step : step + 1], "team", shift(n_team, -step))
        )
    return jnp.maximum(best, total).reshape(rows)


def solution(mesh):
    placed = (
        P(("groups", "workers", "team", "sub"), None),
        P(("groups", "workers", "team", "sub"), None),
        P(("groups", "workers", "team", "sub")),
        P(("groups", "workers", "team", "sub")),
    )
    return jax.shard_map(
        on_device,
        mesh=mesh,
        in_specs=placed,
        out_specs=P(("groups", "workers", "team", "sub")),
        check_vma=False,
    )
```

time: 119 us -> 55.6 us (0.47)
  blocking collectives: 47.9 us -> 0 us
  starting transfers between devices: 11.1 us -> 25.5 us
  between operations: 13.5 us -> 0.11 us
  matrix products: 7.03 us -> 0 us
  other arithmetic: 7.36 us -> 0.58 us
  local copies, waits for them, and re-layouts: 7.79 us -> 1.78 us
  Pallas kernels: 0 us -> 3.12 us
    all_to_all x1 -> x0, blocking collectives: 37.6 us -> none  [on_device(): lax.all_to_all(send_rows.reshape(n_work, cap, width), 'workers', split_ax...]
    ppermute x0 -> x10, starting transfers between devices: none -> 25.5 us  [the longest x2 14.1 us: on_device(): got = lax.ppermute(back, 'workers', [(b, a) for a, b in turn])]
    ppermute x0 -> x10, waiting for transfers between devices: none -> 24.4 us  [the longest x1 13.5 us: on_device(): came_meta = lax.ppermute(meta, 'workers', turns[0]) if turns else None]
    all_to_all x3 -> x0, waiting for transfers between devices: 14.1 us -> none  [the longest x1 5.57 us: on_device(): lax.all_to_all(best.reshape(n_work, cap), 'workers', split_axis=0, concat...]
    all_to_all x3 -> x0, starting transfers between devices: 11.1 us -> none  [the longest x1 4.59 us: on_device(): lax.all_to_all(best.reshape(n_work, cap), 'workers', split_axis=0, concat...]
    all_gather x2 -> x0, blocking collectives: 10.4 us -> none  [the longest x1 5.18 us: on_device(): key_prio = lax.all_gather(got_prio, ('team', 'sub'), axis=0, tiled=True)]
    all_gather x1 -> x0, waiting for transfers between devices: 9.53 us -> none  [on_device(): key_rows = lax.all_gather(got_rows, ('team', 'sub'), axis=0, tiled=True)]
    dot_general x1 -> x0, matrix products: 7.03 us -> none  [similar(): lax.dot_general(left, right, (((1,), (1,)), ((), ())), preferred_element_...]
  transfers between devices with their start and end apart: 4 -> 10, of which waited for: 4 -> 4; matrix products, arithmetic and copies ran while one was open for 3% -> 0% of each run, Pallas kernels for 0% -> 3%
where the time goes in v1:
time: 55.6 us; the launch traced here: 55.4 us
  starting transfers between devices  25.5 us (46%)
  waiting for transfers between devices  24.4 us (44%)
  Pallas kernels  3.12 us (6%)
  local copies, waits for them, and re-layouts  1.78 us (3%)
  other arithmetic  0.58 us (1%)
    ppermute x2, starting transfers between devices, on_device(): got = lax.ppermute(back, 'workers', [(b, a) for a, b in turn])  14.1 us
    ppermute x1, waiting for transfers between devices, on_device(): came_meta = lax.ppermute(meta, 'workers', turns[0]) if turns else None  13.5 us
    ppermute x1, waiting for transfers between devices, on_device(): lax.ppermute(payload, 'team', shift(n_team, step))  9.11 us
    ppermute x1, starting transfers between devices, on_device(): lax.ppermute(payload, 'workers', turn)  3.5 us
    ppermute x1, starting transfers between devices, on_device(): lax.ppermute(payload, 'team', shift(n_team, step))  3 us
    ppermute x1, starting transfers between devices, on_device(): first = lax.ppermute(embeddings, 'workers', turns[0]) if turns else None  2.84 us
    pallas_call x2, Pallas kernels, on_device(): pl.pallas_call(functools.partial(meet_kernel, rows, n_plane, raw), out_sh...  2.04 us
    unnamed x11, local copies, waits for them, and re-layouts  1.76 us
  transfers between devices with their start and end apart: 10, of which 4 were waited for; matrix products, arithmetic and copies ran while one was open for 0% of the time, Pallas kernels for 3%

profile of v1, /device:TPU:0, one launch (start us, length us, event | category | flops | bytes accessed | tf_op | source)
XLA Modules:
  0.0 55.4 jit_solution(14795564757146063781)
XLA Ops:
  0.0 0.0 copy-start.3
  0.0 0.0 copy-start.4
  0.0 0.7 %copy-done.3 = s32[256]{0:T(256)S(1)} copy-done((s32[256]{0:T(256)S(1)}, s32[256]{0:T(256)}, u32[]{:S(2)}) %copy-start.3) | copy-done | bytes 1048
  0.7 0.0 copy-done.4
  0.7 0.0 copy-done.2
  0.7 1.0 %copy-done = bf16[256,1024]{1,0:T(8,128)(2,1)S(1)} copy-done((bf16[256,1024]{1,0:T(8,128)(2,1)S(1)}, bf16[256,1024]{1,0:T(8,128)(2,1)}, u32[]{:S(2)}) %copy-start) | copy-done | bytes 524312
  1.8 0.2 prepare.1
  1.9 3.0 %collective-permute-start.1 = (bf16[272,1024]{1,0:T(8,128)(2,1)S(1)}, bf16[272,1024]{1,0:T(8,128)(2,1)S(1)}, u32[]{:S(2)}, u32[]{:S(2)}) collective-permute-start(bf16[272,1024]{1,0:T(8,128)(2,1)S(1)} %get-tuple-element.11.refs_0_), channel_id=1, source_target_pairs={{0,2},{2,0},{1,3},{3,1},{4,6},{6,4},{5,7},{7,5},{8,10},{10,8},{9,1... | collective-permute-start | bytes 1671176 | tf_op jit(solution)/shard_map/ppermute | solution.py:147
  5.0 0.0 collective-permute-start
  5.0 3.5 %collective-permute-start.3 = (bf16[272,1024]{1,0:T(8,128)(2,1)S(1)}, bf16[272,1024]{1,0:T(8,128)(2,1)S(1)}, u32[]{:S(2)}, u32[]{:S(2)}) collective-permute-start(bf16[272,1024]{1,0:T(8,128)(2,1)S(1)} %get-tuple-element.11.refs_0_), channel_id=1, source_target_pairs={{0,4},{12,8},{1,5},{13,9},{2,6},{14,10},{3,7},{15,11},{16,20},{28,... | collective-permute-start | bytes 1671176 | tf_op jit(solution)/shard_map/ppermute | solution.py:168
  8.5 9.1 %collective-permute-done.1.refs_2_ = bf16[272,1024]{1,0:T(8,128)(2,1)S(1)} collective-permute-done((bf16[272,1024]{1,0:T(8,128)(2,1)S(1)}, bf16[272,1024]{1,0:T(8,128)(2,1)S(1)}, u32[]{:S(2)}, u32[]{:S(2)}) %collective-permute-start.1) | collective-permute-done | bytes 557088 | tf_op jit(solution)/shard_map/ppermute | solution.py:147
  17.6 0.0 collective-permute-start.2
  17.6 0.0 copy-done.1
  17.6 2.8 %collective-permute-start.5 = (bf16[256,1024]{1,0:T(8,128)(2,1)S(1)}, bf16[256,1024]{1,0:T(8,128)(2,1)S(1)}, u32[]{:S(2)}, u32[]{:S(2)}) collective-permute-start(bf16[256,1024]{1,0:T(8,128)(2,1)S(1)} %copy-done.1), channel_id=1, source_target_pairs={{0,8},{8,4},{4,12},{12,0},{1,9},{9,5},{5,13},{13,1},{2,10},{10,6},... | collective-permute-start | bytes 1572872 | tf_op jit(solution)/shard_map/ppermute | solution.py:126
  20.4 0.4 collective-permute-start.6
  20.9 0.0 collective-permute-done.refs_1_
  20.9 0.1 collective-permute-done.3.refs_4_
  21.0 0.0 collective-permute-done.2.refs_3_
  21.0 1.0 %meet.2 = (f32[1,256]{1,0:T(1,128)S(1)}, f32[4,256]{1,0:T(4,128)S(1)}) custom-call(bf16[272,1024]{1,0:T(8,128)(2,1)S(1)} %get-tuple-element.11.refs_0_, bf16[272,1024]{1,0:T(8,128)(2,1)S(1)} %collective-permute-done.refs_1_, bf16[272,1024]{1,0:T(8,128)(2,1)S(1)} %collective-permute-done.1.refs_2_, bf16[272,1024]{1,0:T(8,128)(2,1)S(1)} %collective-permute-done.2.refs_3_, ...), custom_call_target="tpu_custom_call" | custom-call | tf_op jit(solution)/shard_map/meet/pallas_call | solution.py:169
  22.0 13.5 %collective-permute-done.6.refs_5_ = s32[8,256]{1,0:T(8,128)S(1)} collective-permute-done((s32[8,256]{1,0:T(8,128)S(1)}, s32[8,256]{1,0:T(8,128)S(1)}, u32[]{:S(2)}, u32[]{:S(2)}) %collective-permute-start.6) | collective-permute-done | bytes 8224 | tf_op jit(solution)/shard_map/ppermute | solution.py:144
  35.4 0.0 collective-permute-done.5.refs_4_
  35.4 1.1 %meet.3 = (f32[1,256]{1,0:T(1,128)S(1)}, f32[4,256]{1,0:T(4,128)S(1)}) custom-call(bf16[272,1024]{1,0:T(8,128)(2,1)S(1)} %get-tuple-element.11.refs_0_, bf16[272,1024]{1,0:T(8,128)(2,1)S(1)} %collective-permute-done.refs_1_, bf16[272,1024]{1,0:T(8,128)(2,1)S(1)} %collective-permute-done.1.refs_2_, bf16[272,1024]{1,0:T(8,128)(2,1)S(1)} %collective-permute-done.2.refs_3_, ...), custom_call_target="tpu_custom_call" | custom-call | tf_op jit(solution)/shard_map/meet/pallas_call | solution.py:169
  36.5 0.1 collective-permute-start.8
  36.6 12.8 %collective-permute-start.7 = (f32[1,256]{1,0:T(1,128)S(1)}, f32[1,256]{1,0:T(1,128)S(1)}, u32[]{:S(2)}, u32[]{:S(2)}) collective-permute-start(f32[1,256]{1,0:T(1,128)S(1)} %get-tuple-element.14), channel_id=1, source_target_pairs={{8,0},{4,8},{12,4},{0,12},{9,1},{5,9},{13,5},{1,13},{10,2},{6,10},... | collective-permute-start | bytes 3080 | tf_op jit(solution)/shard_map/ppermute | solution.py:181
  49.4 1.3 %collective-permute-start.4 = (f32[1,256]{1,0:T(1,128)S(1)}, f32[1,256]{1,0:T(1,128)S(1)}, u32[]{:S(2)}, u32[]{:S(2)}) collective-permute-start(f32[1,256]{1,0:T(1,128)S(1)} %get-tuple-element.12), channel_id=1, source_target_pairs={{4,0},{8,12},{5,1},{9,13},{6,2},{10,14},{7,3},{11,15},{20,16},{24,... | collective-permute-start | bytes 3080 | tf_op jit(solution)/shard_map/ppermute | solution.py:181
  50.7 0.0 collective-permute-done.8
  50.7 1.6 %collective-permute-start.9 = (f32[1,256]{1,0:T(1,128)S(1)}, f32[1,256]{1,0:T(1,128)S(1)}, u32[]{:S(2)}, u32[]{:S(2)}) collective-permute-start(f32[1,256]{1,0:T(1,128)S(1)} %slice.19), channel_id=1, source_target_pairs={{0,2},{2,0},{1,3},{3,1},{4,6},{6,4},{5,7},{7,5},{8,10},{10,8},{9,1... | collective-permute-start | bytes 3080 | tf_op jit(solution)/shard_map/ppermute | solution.py:195
  52.3 0.9 %own.1 = f32[1,256]{1,0:T(1,128)S(1)} custom-call(bf16[272,1024]{1,0:T(8,128)(2,1)S(1)} %get-tuple-element.11.refs_0_, bf16[272,1024]{1,0:T(8,128)(2,1)S(1)} %collective-permute-done.refs_1_, bf16[272,1024]{1,0:T(8,128)(2,1)S(1)} %collective-permute-done.1.refs_2_, bf16[272,1024]{1,0:T(8,128)(2,1)S(1)} %collective-permute-done.2.refs_3_), custom_call_target="tpu_custom_call" | custom-call | tf_op jit(solution)/shard_map/own/pallas_call | solution.py:155
  53.2 0.0 collective-permute-done.7
  53.2 1.7 %collective-permute-done.4 = f32[1,256]{1,0:T(1,128)S(1)} collective-permute-done((f32[1,256]{1,0:T(1,128)S(1)}, f32[1,256]{1,0:T(1,128)S(1)}, u32[]{:S(2)}, u32[]{:S(2)}) %collective-permute-start.4) | collective-permute-done | bytes 1056 | tf_op jit(solution)/shard_map/ppermute | solution.py:181
  54.9 0.0 collective-permute-done.9
  54.9 0.6 %fusion.3 = f32[1,256]{1,0:T(1,128)} fusion(f32[1,256]{1,0:T(1,128)S(1)} %collective-permute-done.7, f32[1,256]{1,0:T(1,128)S(1)} %own.1, f32[1,256]{1,0:T(1,128)S(1)} %collective-permute-done.4, pred[]{:T(512)S(6)} %or.3, f32[1,256]{1,0:T(1,128)S(1)} %collective-permute-done.9, f32[2,256]{1,0:T(2,128)S(1)} %fusion), kind=kLoop, calls=%fused_computation.7 | loop fusion | flops 1280 | bytes 6145 | tf_op jit(solution)/shard_map/max | solution.py:197
  (9 shorter events, 0.0 us)
Async XLA Ops:
  0.0 0.7 %copy-start.3 = (s32[256]{0:T(256)S(1)}, s32[256]{0:T(256)}, u32[]{:S(2)}) copy-start(s32[256]{0:T(256)} %param.6) | copy-start | bytes 3076
  0.0 0.7 %copy-start.4 = (s32[256]{0:T(256)S(1)}, s32[256]{0:T(256)}, u32[]{:S(2)}) copy-start(s32[256]{0:T(256)} %param.7) | copy-start | bytes 3076
  0.0 0.7 %copy-start.2 = (s32[256,1]{0,1:T(1,128)S(1)}, s32[256,1]{0,1:T(1,128)}, u32[]{:S(2)}) copy-start(s32[256,1]{0,1:T(1,128)} %param.5) | copy-start | bytes 3076
  0.7 1.0 %copy-start = (bf16[256,1024]{1,0:T(8,128)(2,1)S(1)}, bf16[256,1024]{1,0:T(8,128)(2,1)}, u32[]{:S(2)}) copy-start(bf16[256,1024]{1,0:T(8,128)(2,1)} %emb.1) | copy-start | bytes 1572868
  1.8 15.8 %copy-start.1 = (bf16[256,1024]{1,0:T(8,128)(2,1)S(1)}, bf16[256,1024]{1,0:T(8,128)(2,1)}, u32[]{:S(2)}) copy-start(bf16[256,1024]{1,0:T(8,128)(2,1)} %emb.1) | copy-start | bytes 1572868
  1.9 15.6 %collective-permute-start.1 = (bf16[272,1024]{1,0:T(8,128)(2,1)S(1)}, bf16[272,1024]{1,0:T(8,128)(2,1)S(1)}, u32[]{:S(2)}, u32[]{:S(2)}) collective-permute-start(bf16[272,1024]{1,0:T(8,128)(2,1)S(1)} %get-tuple-element.11.refs_0_), channel_id=1, source_target_pairs={{0,2},{2,0},{1,3},{3,1},{4,6},{6,4},{5,7},{7,5},{8,10},{10,8},{9,1... | collective-permute-start | bytes 1671176 | tf_op jit(solution)/shard_map/ppermute | solution.py:147
  5.0 15.9 %collective-permute-start = (bf16[272,1024]{1,0:T(8,128)(2,1)S(1)}, bf16[272,1024]{1,0:T(8,128)(2,1)S(1)}, u32[]{:S(2)}, u32[]{:S(2)}) collective-permute-start(bf16[272,1024]{1,0:T(8,128)(2,1)S(1)} %get-tuple-element.11.refs_0_), channel_id=1, source_target_pairs={{0,1},{1,0},{2,3},{3,2},{4,5},{5,4},{6,7},{7,6},{8,9},{9,8},{10,11... | collective-permute-start | bytes 1671176 | tf_op jit(solution)/shard_map/ppermute | solution.py:153
  5.0 16.0 %collective-permute-start.3 = (bf16[272,1024]{1,0:T(8,128)(2,1)S(1)}, bf16[272,1024]{1,0:T(8,128)(2,1)S(1)}, u32[]{:S(2)}, u32[]{:S(2)}) collective-permute-start(bf16[272,1024]{1,0:T(8,128)(2,1)S(1)} %get-tuple-element.11.refs_0_), channel_id=1, source_target_pairs={{0,4},{12,8},{1,5},{13,9},{2,6},{14,10},{3,7},{15,11},{16,20},{28,... | collective-permute-start | bytes 1671176 | tf_op jit(solution)/shard_map/ppermute | solution.py:168
  17.6 3.4 %collective-permute-start.2 = (bf16[272,1024]{1,0:T(8,128)(2,1)S(1)}, bf16[272,1024]{1,0:T(8,128)(2,1)S(1)}, u32[]{:S(2)}, u32[]{:S(2)}) collective-permute-start(bf16[272,1024]{1,0:T(8,128)(2,1)S(1)} %collective-permute-done.1.refs_2_), channel_id=1, source_target_pairs={{0,1},{1,0},{2,3},{3,2},{4,5},{5,4},{6,7},{7,6},{8,9},{9,8},{10,11... | collective-permute-start | bytes 1671176 | tf_op jit(solution)/shard_map/ppermute | solution.py:153
  17.6 17.8 %collective-permute-start.5 = (bf16[256,1024]{1,0:T(8,128)(2,1)S(1)}, bf16[256,1024]{1,0:T(8,128)(2,1)S(1)}, u32[]{:S(2)}, u32[]{:S(2)}) collective-permute-start(bf16[256,1024]{1,0:T(8,128)(2,1)S(1)} %copy-done.1), channel_id=1, source_target_pairs={{0,8},{8,4},{4,12},{12,0},{1,9},{9,5},{5,13},{13,1},{2,10},{10,6},... | collective-permute-start | bytes 1572872 | tf_op jit(solution)/shard_map/ppermute | solution.py:126
  20.4 15.0 %collective-permute-start.6 = (s32[8,256]{1,0:T(8,128)S(1)}, s32[8,256]{1,0:T(8,128)S(1)}, u32[]{:S(2)}, u32[]{:S(2)}) collective-permute-start(s32[8,256]{1,0:T(8,128)S(1)} %get-tuple-element.13), channel_id=1, source_target_pairs={{0,8},{8,4},{4,12},{12,0},{1,9},{9,5},{5,13},{13,1},{2,10},{10,6},... | collective-permute-start | bytes 24584 | tf_op jit(solution)/shard_map/ppermute | solution.py:144
  36.5 14.2 %collective-permute-start.8 = (f32[2,256]{1,0:T(2,128)S(1)}, f32[2,256]{1,0:T(2,128)S(1)}, u32[]{:S(2)}, u32[]{:S(2)}) collective-permute-start(f32[2,256]{1,0:T(2,128)S(1)} %bitcast.14), channel_id=1, source_target_pairs={{0,1},{1,0},{2,3},{3,2},{4,5},{5,4},{6,7},{7,6},{8,9},{9,8},{10,11... | collective-permute-start | bytes 6152 | tf_op jit(solution)/shard_map/ppermute | solution.py:191
  36.6 16.6 %collective-permute-start.7 = (f32[1,256]{1,0:T(1,128)S(1)}, f32[1,256]{1,0:T(1,128)S(1)}, u32[]{:S(2)}, u32[]{:S(2)}) collective-permute-start(f32[1,256]{1,0:T(1,128)S(1)} %get-tuple-element.14), channel_id=1, source_target_pairs={{8,0},{4,8},{12,4},{0,12},{9,1},{5,9},{13,5},{1,13},{10,2},{6,10},... | collective-permute-start | bytes 3080 | tf_op jit(solution)/shard_map/ppermute | solution.py:181
  49.4 5.5 %collective-permute-start.4 = (f32[1,256]{1,0:T(1,128)S(1)}, f32[1,256]{1,0:T(1,128)S(1)}, u32[]{:S(2)}, u32[]{:S(2)}) collective-permute-start(f32[1,256]{1,0:T(1,128)S(1)} %get-tuple-element.12), channel_id=1, source_target_pairs={{4,0},{8,12},{5,1},{9,13},{6,2},{10,14},{7,3},{11,15},{20,16},{24,... | collective-permute-start | bytes 3080 | tf_op jit(solution)/shard_map/ppermute | solution.py:181
  50.7 4.1 %collective-permute-start.9 = (f32[1,256]{1,0:T(1,128)S(1)}, f32[1,256]{1,0:T(1,128)S(1)}, u32[]{:S(2)}, u32[]{:S(2)}) collective-permute-start(f32[1,256]{1,0:T(1,128)S(1)} %slice.19), channel_id=1, source_target_pairs={{0,2},{2,0},{1,3},{3,1},{4,6},{6,4},{5,7},{7,5},{8,10},{10,8},{9,1... | collective-permute-start | bytes 3080 | tf_op jit(solution)/shard_map/ppermute | solution.py:195

commit v2 on v0

v2 whole, which is shorter than its diff:
```python
import functools

import jax
import jax.numpy as jnp
from jax import lax
from jax.experimental import pallas as pl
from jax.experimental.pallas import tpu as pltpu
from jax.sharding import PartitionSpec as P

KC = 16
EXTRA = 16
VMEM = pl.BlockSpec(memory_space=pltpu.VMEM)


def normalise(raw):
    values = raw.astype(jnp.float32)
    total = jnp.sum(values * values, axis=1, keepdims=True)
    return (values * lax.rsqrt(total + 1e-06)).astype(jnp.bfloat16)


def code_of(owner, cluster, high, low):
    return ((owner * KC + cluster) * 256 + high) * 256 + low


def code_in(ids):
    place = ids[2:3, :]
    return code_of(ids[0:1, :], ids[1:2, :], place // 256, place % 256)


def code_at(block, rows):
    last = block[rows : rows + EXTRA, :].astype(jnp.float32)[0:1, :].astype(jnp.int32)
    return code_of(*[last[:, i * rows : (i + 1) * rows] for i in range(4)])


def as_column(row):
    return jnp.broadcast_to(row, (128, row.shape[1])).T


def fold_rows(best):
    return jnp.max(best.T, axis=0, keepdims=True)


def scores_of(left, right):
    return lax.dot_general(
        left, right, (((1,), (1,)), ((), ())), preferred_element_type=jnp.float32
    )


def pack_kernel(rows, raw, ids, block):
    width = block.shape[1]
    place = ids[2:3, :]
    line = [ids[0:1, :], ids[1:2, :], place // 256, place % 256]
    line += [jnp.zeros((1, width - 4 * rows), jnp.int32)] if width > 4 * rows else []
    line = jnp.concatenate(line, axis=1).astype(jnp.float32)
    first = lax.broadcasted_iota(jnp.int32, (EXTRA, width), 0) == 0
    last = jnp.where(first, jnp.broadcast_to(line, (EXTRA, width)), 0.0)
    block[0:rows, :] = normalise(raw[...])
    block[rows : rows + EXTRA, :] = last.astype(jnp.bfloat16)


def own_kernel(rows, *refs):
    blocks, (plane, codes, kept) = refs[:-3], refs[-3:]
    mine = blocks[0][0:rows, :]
    column = as_column(code_at(blocks[0], rows))
    found = jnp.full((rows, 128), -1.0, jnp.float32)
    for index, block in enumerate(blocks):
        here = block[0:rows, :]
        code = code_at(block, rows)
        plane[index * rows : (index + 1) * rows, :] = here
        codes[index : index + 1, :] = code
        scores = scores_of(mine, here)
        for at in range(0, rows, 128):
            other = code[:, at : at + 128]
            earlier = ((column ^ other) < 65536) & (column > other)
            found = jnp.maximum(found, jnp.where(earlier, scores[:, at : at + 128], -1.0))
    kept[...] = jnp.full(kept.shape, -1.0, jnp.float32)
    kept[0:1, :] = fold_rows(found)


def meet_kernel(rows, n_plane, has_far, has_near, *refs):
    (plane, codes, part), refs = refs[:3], list(refs[3:])
    if has_far:
        far, far_ids = refs.pop(0), refs.pop(0)
        far_rows, far_column = normalise(far[...]), as_column(code_in(far_ids))
        found = jnp.full((rows, 128), -1.0, jnp.float32)
    if has_near:
        near, near_ids = refs.pop(0), refs.pop(0)
        near_rows, near_column = normalise(near[...]), as_column(code_in(near_ids))
    kept = refs.pop(0)
    for index in range(n_plane):
        here = plane[index * rows : (index + 1) * rows, :]
        far_scores = scores_of(far_rows, here) if has_far else None
        near_scores = scores_of(near_rows, here) if has_near else None
        for at in range(0, rows, 128):
            lanes = slice(at, at + 128)
            other = codes[index : index + 1, lanes]
            keep = jnp.full((rows, 128), -1.0, jnp.float32)
            if has_far:
                shared = jnp.where((far_column ^ other) < 65536, far_scores[:, lanes], -1.0)
                later = far_column > other
                found = jnp.maximum(found, jnp.where(later, shared, -1.0))
                keep = jnp.where(later, -1.0, shared)
            if has_near:
                earlier = ((near_column ^ other) < 65536) & (near_column < other)
                keep = jnp.maximum(keep, jnp.where(earlier, near_scores[:, lanes], -1.0))
            kept[index : index + 1, lanes] = jnp.maximum(
                part[index : index + 1, lanes], jnp.max(keep, axis=0, keepdims=True)
            )
    if has_far:
        (back,) = refs
        back[...] = fold_rows(found)


def kernel(body, name, out_shape, args):
    return pl.pallas_call(
        body,
        out_shape=out_shape,
        in_specs=[VMEM] * len(args),
        out_specs=(VMEM,) * len(out_shape),
        compiler_params=pltpu.CompilerParams(vmem_limit_bytes=40 * 1024 * 1024),
        name=name,
    )(*args)


def shift(n, step):
    return [(i, (i + step) % n) for i in range(n)]


def turns_of(n):
    half = n // 2
    line = [p // 2 + p % 2 * half for p in range(2 * half)] + list(range(2 * half, n))
    turns = [[(line[p], line[(p + step) % n]) for p in range(n)] for step in range(1, half + 1)]
    far = turns[: (n - 1) // 2]
    return far, turns[-1] if n % 2 == 0 else None


def on_device(embeddings, owner_ids, clusters, priority):
    rows, width = embeddings.shape
    n_work, n_team, n_sub = [lax.axis_size(a) for a in ("workers", "team", "sub")]
    n_plane = n_team * n_sub
    struct = jax.ShapeDtypeStruct
    far_turns, near_turn = turns_of(n_work)

    far = [lax.ppermute(embeddings, "workers", turn) for turn in far_turns]
    near = lax.ppermute(embeddings, "workers", near_turn) if near_turn else None
    ids = jnp.concatenate(
        [owner_ids.reshape(1, rows), clusters.reshape(1, rows), priority.reshape(1, rows)], axis=0
    )
    far_ids = [lax.ppermute(ids, "workers", turn) for turn in far_turns]
    near_ids = lax.ppermute(ids, "workers", near_turn) if near_turn else None

    def gather():
        (block,) = kernel(
            functools.partial(pack_kernel, rows),
            "pack",
            (struct((rows + EXTRA, width), jnp.bfloat16),),
            (embeddings, ids),
        )
        blocks = []
        for dt in range(n_team):
            first = lax.ppermute(block, "team", shift(n_team, dt)) if dt else block
            blocks.append(first)
            for ds in range(1, n_sub):
                blocks.append(lax.ppermute(first, "sub", shift(n_sub, ds)))
        return tuple(blocks)

    blocks = lax.cond(
        lax.axis_index("groups") < lax.axis_size("groups"),
        gather,
        lambda: (jnp.zeros((rows + EXTRA, width), jnp.bfloat16),) * n_plane,
    )
    plane, codes, kept = kernel(
        functools.partial(own_kernel, rows),
        "own",
        (
            struct((n_plane * rows, width), jnp.bfloat16),
            struct((n_plane, rows), jnp.int32),
            struct((n_plane, rows), jnp.float32),
        ),
        blocks,
    )

    answers = []
    for index in range(max(len(far), 1)):
        has_far, has_near = index < len(far), index == 0 and near is not None
        if not has_far and not has_near:
            break
        came = (far[index], far_ids[index]) if has_far else ()
        came += (near, near_ids) if has_near else ()
        out = (struct((n_plane, rows), jnp.float32),)
        out += (struct((1, rows), jnp.float32),) if has_far else ()
        kept, *back = kernel(
            functools.partial(meet_kernel, rows, n_plane, has_far, has_near),
            "meet",
            out,
            (plane, codes, kept, *came),
        )
        if has_far:
            home = [(b, a) for a, b in far_turns[index]]
            answers.append(lax.ppermute(back[0], "workers", home))

    kept = kept.reshape(n_team, n_sub, rows)
    ends = kept[:, 0]
    for ds in range(1, n_sub):
        ends = jnp.maximum(ends, lax.ppermute(kept[:, ds], "sub", shift(n_sub, -ds)))
    best = ends[0:1]
    for dt in range(1, n_team):
        best = jnp.maximum(best, lax.ppermute(ends[dt : dt + 1], "team", shift(n_team, -dt)))
    for answer in answers:
        best = jnp.maximum(best, answer)
    return best.reshape(rows)


def solution(mesh):
    placed = (
        P(("groups", "workers", "team", "sub"), None),
        P(("groups", "workers", "team", "sub"), None),
        P(("groups", "workers", "team", "sub")),
        P(("groups", "workers", "team", "sub")),
    )
    return jax.shard_map(
        on_device,
        mesh=mesh,
        in_specs=placed,
        out_specs=P(("groups", "workers", "team", "sub")),
        check_vma=False,
    )
```

time: 119 us -> 38.2 us (0.32)
  blocking collectives: 47.9 us -> 0 us
  between operations: 13.5 us -> 0.04 us
  local copies, waits for them, and re-layouts: 7.79 us -> 0.03 us
  matrix products: 7.03 us -> 0 us
  Pallas kernels: 0 us -> 6.18 us
  other arithmetic: 7.36 us -> 1.29 us
  waiting for transfers between devices: 23.6 us -> 17.6 us
  starting transfers between devices: 11.1 us -> 12.8 us
    all_to_all x1 -> x0, blocking collectives: 37.6 us -> none  [on_device(): lax.all_to_all(send_rows.reshape(n_work, cap, width), 'workers', split_ax...]
    ppermute x0 -> x10, waiting for transfers between devices: none -> 17.6 us  [the longest x1 12.4 us: gather(): first = lax.ppermute(block, 'team', shift(n_team, dt)) if dt else block]
    all_to_all x3 -> x0, waiting for transfers between devices: 14.1 us -> none  [the longest x1 5.57 us: on_device(): lax.all_to_all(best.reshape(n_work, cap), 'workers', split_axis=0, concat...]
    ppermute x0 -> x10, starting transfers between devices: none -> 12.8 us  [the longest x1 4.04 us: on_device(): far = [lax.ppermute(embeddings, 'workers', turn) for turn in far_turns]]
    all_to_all x3 -> x0, starting transfers between devices: 11.1 us -> none  [the longest x1 4.59 us: on_device(): lax.all_to_all(best.reshape(n_work, cap), 'workers', split_axis=0, concat...]
    all_gather x2 -> x0, blocking collectives: 10.4 us -> none  [the longest x1 5.18 us: on_device(): key_prio = lax.all_gather(got_prio, ('team', 'sub'), axis=0, tiled=True)]
    all_gather x1 -> x0, waiting for transfers between devices: 9.53 us -> none  [on_device(): key_rows = lax.all_gather(got_rows, ('team', 'sub'), axis=0, tiled=True)]
    dot_general x1 -> x0, matrix products: 7.03 us -> none  [similar(): lax.dot_general(left, right, (((1,), (1,)), ((), ())), preferred_element_...]
  transfers between devices with their start and end apart: 4 -> 10, of which waited for: 4 -> 4; matrix products, arithmetic and copies ran while one was open for 3% -> 2% of each run, Pallas kernels for 0% -> 12%
where the time goes in v2:
time: 38.2 us; the launch traced here: 38 us
  waiting for transfers between devices  17.6 us (46%)
  starting transfers between devices  12.8 us (34%)
  Pallas kernels  6.18 us (16%)
  other arithmetic  1.29 us (3%)
    ppermute x1, waiting for transfers between devices, gather(): first = lax.ppermute(block, 'team', shift(n_team, dt)) if dt else block  12.4 us
    pallas_call x3, Pallas kernels, kernel(): pl.pallas_call(body, out_shape=out_shape, in_specs=[VMEM] * len(args), ou...  6.18 us
    ppermute x1, starting transfers between devices, on_device(): far = [lax.ppermute(embeddings, 'workers', turn) for turn in far_turns]  4.04 us
    ppermute x1, starting transfers between devices, on_device(): answers.append(lax.ppermute(back[0], 'workers', home))  3.29 us
    ppermute x2, waiting for transfers between devices, gather(): blocks.append(lax.ppermute(first, 'sub', shift(n_sub, ds)))  2.3 us
    ppermute x1, waiting for transfers between devices, on_device(): lax.ppermute(ends[dt:dt + 1], 'team', shift(n_team, -dt))  2.08 us
    ppermute x1, starting transfers between devices, gather(): first = lax.ppermute(block, 'team', shift(n_team, dt)) if dt else block  1.7 us
    ppermute x1, starting transfers between devices, on_device(): near = lax.ppermute(embeddings, 'workers', near_turn) if near_turn else None  1.58 us
  transfers between devices with their start and end apart: 10, of which 4 were waited for; matrix products, arithmetic and copies ran while one was open for 2% of the time, Pallas kernels for 12%

profile of v2, /device:TPU:0, one launch (start us, length us, event | category | flops | bytes accessed | tf_op | source)
XLA Modules:
  0.0 38.0 jit_solution(6278358642760158817)
XLA Ops:
  0.0 4.0 %collective-permute-start.3 = (bf16[256,1024]{1,0:T(8,128)(2,1)}, bf16[256,1024]{1,0:T(8,128)(2,1)S(1)}, u32[]{:S(2)}, u32[]{:S(2)}) collective-permute-start(bf16[256,1024]{1,0:T(8,128)(2,1)} %param.6), channel_id=1, source_target_pairs={{0,8},{8,4},{4,12},{12,0},{1,9},{9,5},{5,13},{13,1},{2,10},{10,6},... | collective-permute-start | bytes 1572872 | tf_op jit(solution)/shard_map/ppermute | solution.py:144
  4.0 1.6 %collective-permute-start.5 = (bf16[256,1024]{1,0:T(8,128)(2,1)}, bf16[256,1024]{1,0:T(8,128)(2,1)S(1)}, u32[]{:S(2)}, u32[]{:S(2)}) collective-permute-start(bf16[256,1024]{1,0:T(8,128)(2,1)} %param.6), channel_id=1, source_target_pairs={{0,4},{8,12},{4,0},{12,8},{1,5},{9,13},{5,1},{13,9},{2,6},{10,14},... | collective-permute-start | bytes 1572872 | tf_op jit(solution)/shard_map/ppermute | solution.py:145
  5.6 0.7 %pad_add_fusion = s32[3,256]{1,0:T(4,128)S(1)} fusion(s32[1,256]{1,0:T(1,128)} %bitcast.12, s32[1,256]{1,0:T(1,128)} %bitcast.13, s32[1,256]{1,0:T(1,128)} %bitcast.14), kind=kLoop, calls=%fused_computation | loop fusion | flops 1536 | bytes 6144 | tf_op jit(solution)/shard_map/concatenate | solution.py:146
  6.3 0.0 collective-permute-start.4
  6.3 18.5 %conditional.1 = (bf16[272,1024]{1,0:T(8,128)(2,1)}, bf16[272,1024]{1,0:T(8,128)(2,1)}, bf16[272,1024]{1,0:T(8,128)(2,1)}, bf16[272,1024]{1,0:T(8,128)(2,1)}) conditional(s32[]{:T(128)} %convert_element_type.3, () %tuple.13, (bf16[256,1024]{1,0:T(8,128)(2,1)}, s32[3,256]{1,0:T(4,128)S(1)}) %tuple.14), branch_computations={%region_0.0_spmd, %region_1.0_spmd} | conditional | bytes 6684824 | solution.py:167
  6.3 2.0 %pack.1 = bf16[272,1024]{1,0:T(8,128)(2,1)} custom-call(bf16[256,1024]{1,0:T(8,128)(2,1)} %get-tuple-element.9.raw, s32[3,256]{1,0:T(4,128)S(1)} %get-tuple-element.10.ids), custom_call_target="tpu_custom_call" | custom-call | tf_op jit(solution)/shard_map/cond/branch_1_fun/pack/pallas_call | solution.py:115
  8.4 1.7 %collective-permute-start.1 = (bf16[272,1024]{1,0:T(8,128)(2,1)}, bf16[272,1024]{1,0:T(8,128)(2,1)}, u32[]{:S(2)}, u32[]{:S(2)}) collective-permute-start(bf16[272,1024]{1,0:T(8,128)(2,1)} %pack.1), channel_id=1, source_target_pairs={{0,2},{2,0},{1,3},{3,1},{4,6},{6,4},{5,7},{7,5},{8,10},{10,8},{9,1... | collective-permute-start | bytes 1671176 | tf_op jit(solution)/shard_map/cond/branch_1_fun/ppermute | solution.py:161
  10.1 0.0 collective-permute-start
  10.1 12.4 %collective-permute-done.1 = bf16[272,1024]{1,0:T(8,128)(2,1)} collective-permute-done((bf16[272,1024]{1,0:T(8,128)(2,1)}, bf16[272,1024]{1,0:T(8,128)(2,1)}, u32[]{:S(2)}, u32[]{:S(2)}) %collective-permute-start.1) | collective-permute-done | bytes 557088 | tf_op jit(solution)/shard_map/cond/branch_1_fun/ppermute | solution.py:161
  22.5 0.0 collective-permute-start.2
  22.5 0.0 collective-permute-done
  22.5 2.3 %collective-permute-done.2 = bf16[272,1024]{1,0:T(8,128)(2,1)} collective-permute-done((bf16[272,1024]{1,0:T(8,128)(2,1)}, bf16[272,1024]{1,0:T(8,128)(2,1)}, u32[]{:S(2)}, u32[]{:S(2)}) %collective-permute-start.2) | collective-permute-done | bytes 557088 | tf_op jit(solution)/shard_map/cond/branch_1_fun/ppermute | solution.py:164
  24.8 0.6 %collective-permute-start.6 = (s32[3,256]{1,0:T(4,128)S(1)}, s32[3,256]{1,0:T(4,128)S(1)}, u32[]{:S(2)}, u32[]{:S(2)}) collective-permute-start(s32[3,256]{1,0:T(4,128)S(1)} %pad_add_fusion), channel_id=1, source_target_pairs={{0,4},{8,12},{4,0},{12,8},{1,5},{9,13},{5,1},{13,9},{2,6},{10,14},... | collective-permute-start | bytes 9224 | tf_op jit(solution)/shard_map/ppermute | solution.py:150
  25.4 2.5 %own.1 = (bf16[1024,1024]{1,0:T(8,128)(2,1)S(1)}, s32[4,256]{1,0:T(4,128)S(1)}, f32[4,256]{1,0:T(4,128)S(1)}) custom-call(bf16[272,1024]{1,0:T(8,128)(2,1)} %get-tuple-element.20.refs_0_, bf16[272,1024]{1,0:T(8,128)(2,1)} %get-tuple-element.21.refs_1_, bf16[272,1024]{1,0:T(8,128)(2,1)} %get-tuple-element.22.refs_2_, bf16[272,1024]{1,0:T(8,128)(2,1)} %get-tuple-element.23.refs_3_), custom_call_target="tpu_custom_call" | custom-call | tf_op jit(solution)/shard_map/own/pallas_call | solution.py:115
  27.9 0.8 %collective-permute-done.4.refs_4_ = s32[3,256]{1,0:T(4,128)S(1)} collective-permute-done((s32[3,256]{1,0:T(4,128)S(1)}, s32[3,256]{1,0:T(4,128)S(1)}, u32[]{:S(2)}, u32[]{:S(2)}) %collective-permute-start.4) | collective-permute-done | bytes 3104 | tf_op jit(solution)/shard_map/ppermute | solution.py:149
  28.7 0.0 collective-permute-done.6.refs_6_
  28.7 0.0 collective-permute-done.3.refs_3_
  28.7 0.0 collective-permute-done.5.refs_5_
  28.7 1.7 %meet.1 = (f32[4,256]{1,0:T(4,128)S(1)}, f32[1,256]{1,0:T(1,128)S(1)}) custom-call(bf16[1024,1024]{1,0:T(8,128)(2,1)S(1)} %get-tuple-element.24.refs_0_, s32[4,256]{1,0:T(4,128)S(1)} %get-tuple-element.25.refs_1_, f32[4,256]{1,0:T(4,128)S(1)} %get-tuple-element.26.refs_2_, bf16[256,1024]{1,0:T(8,128)(2,1)S(1)} %collective-permute-done.3.refs_3_, ...), custom_call_target="tpu_custom_call" | custom-call | tf_op jit(solution)/shard_map/meet/pallas_call | solution.py:115
  30.4 0.1 collective-permute-start.7
  30.5 3.3 %collective-permute-start.9 = (f32[1,256]{1,0:T(1,128)S(1)}, f32[1,256]{1,0:T(1,128)S(1)}, u32[]{:S(2)}, u32[]{:S(2)}) collective-permute-start(f32[1,256]{1,0:T(1,128)S(1)} %get-tuple-element.28), channel_id=1, source_target_pairs={{8,0},{4,8},{12,4},{0,12},{9,1},{5,9},{13,5},{1,13},{10,2},{6,10},... | collective-permute-start | bytes 3080 | tf_op jit(solution)/shard_map/ppermute | solution.py:200
  33.8 0.0 collective-permute-done.7
  33.8 1.6 %collective-permute-start.8 = (f32[1,256]{1,0:T(1,128)S(1)}, f32[1,256]{1,0:T(1,128)S(1)}, u32[]{:S(2)}, u32[]{:S(2)}) collective-permute-start(f32[1,256]{1,0:T(1,128)S(1)} %slice.19), channel_id=1, source_target_pairs={{0,2},{2,0},{1,3},{3,1},{4,6},{6,4},{5,7},{7,5},{8,10},{10,8},{9,1... | collective-permute-start | bytes 3080 | tf_op jit(solution)/shard_map/ppermute | solution.py:208
  35.3 0.0 collective-permute-done.9
  35.3 2.1 %collective-permute-done.8 = f32[1,256]{1,0:T(1,128)S(1)} collective-permute-done((f32[1,256]{1,0:T(1,128)S(1)}, f32[1,256]{1,0:T(1,128)S(1)}, u32[]{:S(2)}, u32[]{:S(2)}) %collective-permute-start.8) | collective-permute-done | bytes 1056 | tf_op jit(solution)/shard_map/ppermute | solution.py:208
  37.4 0.6 %fusion.1 = f32[1,256]{1,0:T(1,128)} fusion(f32[1,256]{1,0:T(1,128)S(1)} %collective-permute-done.9, f32[1,256]{1,0:T(1,128)S(1)} %collective-permute-done.8, f32[2,256]{1,0:T(2,128)S(1)} %fusion), kind=kLoop, calls=%fused_computation.5 | loop fusion | flops 512 | bytes 4096 | tf_op jit(solution)/shard_map/max | solution.py:210
  (5 shorter events, 0.0 us)
Async XLA Ops:
  0.0 28.7 %collective-permute-start.3 = (bf16[256,1024]{1,0:T(8,128)(2,1)}, bf16[256,1024]{1,0:T(8,128)(2,1)S(1)}, u32[]{:S(2)}, u32[]{:S(2)}) collective-permute-start(bf16[256,1024]{1,0:T(8,128)(2,1)} %param.6), channel_id=1, source_target_pairs={{0,8},{8,4},{4,12},{12,0},{1,9},{9,5},{5,13},{13,1},{2,10},{10,6},... | collective-permute-start | bytes 1572872 | tf_op jit(solution)/shard_map/ppermute | solution.py:144
  4.0 24.7 %collective-permute-start.5 = (bf16[256,1024]{1,0:T(8,128)(2,1)}, bf16[256,1024]{1,0:T(8,128)(2,1)S(1)}, u32[]{:S(2)}, u32[]{:S(2)}) collective-permute-start(bf16[256,1024]{1,0:T(8,128)(2,1)} %param.6), channel_id=1, source_target_pairs={{0,4},{8,12},{4,0},{12,8},{1,5},{9,13},{5,1},{13,9},{2,6},{10,14},... | collective-permute-start | bytes 1572872 | tf_op jit(solution)/shard_map/ppermute | solution.py:145
  6.3 22.4 %collective-permute-start.4 = (s32[3,256]{1,0:T(4,128)S(1)}, s32[3,256]{1,0:T(4,128)S(1)}, u32[]{:S(2)}, u32[]{:S(2)}) collective-permute-start(s32[3,256]{1,0:T(4,128)S(1)} %pad_add_fusion), channel_id=1, source_target_pairs={{0,8},{8,4},{4,12},{12,0},{1,9},{9,5},{5,13},{13,1},{2,10},{10,6},... | collective-permute-start | bytes 9224 | tf_op jit(solution)/shard_map/ppermute | solution.py:149
  8.4 14.1 %collective-permute-start.1 = (bf16[272,1024]{1,0:T(8,128)(2,1)}, bf16[272,1024]{1,0:T(8,128)(2,1)}, u32[]{:S(2)}, u32[]{:S(2)}) collective-permute-start(bf16[272,1024]{1,0:T(8,128)(2,1)} %pack.1), channel_id=1, source_target_pairs={{0,2},{2,0},{1,3},{3,1},{4,6},{6,4},{5,7},{7,5},{8,10},{10,8},{9,1... | collective-permute-start | bytes 1671176 | tf_op jit(solution)/shard_map/cond/branch_1_fun/ppermute | solution.py:161
  10.1 12.4 %collective-permute-start = (bf16[272,1024]{1,0:T(8,128)(2,1)}, bf16[272,1024]{1,0:T(8,128)(2,1)}, u32[]{:S(2)}, u32[]{:S(2)}) collective-permute-start(bf16[272,1024]{1,0:T(8,128)(2,1)} %pack.1), channel_id=1, source_target_pairs={{0,1},{1,0},{2,3},{3,2},{4,5},{5,4},{6,7},{7,6},{8,9},{9,8},{10,11... | collective-permute-start | bytes 1671176 | tf_op jit(solution)/shard_map/cond/branch_1_fun/ppermute | solution.py:164
  22.5 2.3 %collective-permute-start.2 = (bf16[272,1024]{1,0:T(8,128)(2,1)}, bf16[272,1024]{1,0:T(8,128)(2,1)}, u32[]{:S(2)}, u32[]{:S(2)}) collective-permute-start(bf16[272,1024]{1,0:T(8,128)(2,1)} %collective-permute-done.1), channel_id=1, source_target_pairs={{0,1},{1,0},{2,3},{3,2},{4,5},{5,4},{6,7},{7,6},{8,9},{9,8},{10,11... | collective-permute-start | bytes 1671176 | tf_op jit(solution)/shard_map/cond/branch_1_fun/ppermute | solution.py:164
  24.8 3.9 %collective-permute-start.6 = (s32[3,256]{1,0:T(4,128)S(1)}, s32[3,256]{1,0:T(4,128)S(1)}, u32[]{:S(2)}, u32[]{:S(2)}) collective-permute-start(s32[3,256]{1,0:T(4,128)S(1)} %pad_add_fusion), channel_id=1, source_target_pairs={{0,4},{8,12},{4,0},{12,8},{1,5},{9,13},{5,1},{13,9},{2,6},{10,14},... | collective-permute-start | bytes 9224 | tf_op jit(solution)/shard_map/ppermute | solution.py:150
  30.4 3.4 %collective-permute-start.7 = (f32[2,256]{1,0:T(2,128)S(1)}, f32[2,256]{1,0:T(2,128)S(1)}, u32[]{:S(2)}, u32[]{:S(2)}) collective-permute-start(f32[2,256]{1,0:T(2,128)S(1)} %bitcast.11), channel_id=1, source_target_pairs={{0,1},{1,0},{2,3},{3,2},{4,5},{5,4},{6,7},{7,6},{8,9},{9,8},{10,11... | collective-permute-start | bytes 6152 | tf_op jit(solution)/shard_map/ppermute | solution.py:205
  30.5 4.9 %collective-permute-start.9 = (f32[1,256]{1,0:T(1,128)S(1)}, f32[1,256]{1,0:T(1,128)S(1)}, u32[]{:S(2)}, u32[]{:S(2)}) collective-permute-start(f32[1,256]{1,0:T(1,128)S(1)} %get-tuple-element.28), channel_id=1, source_target_pairs={{8,0},{4,8},{12,4},{0,12},{9,1},{5,9},{13,5},{1,13},{10,2},{6,10},... | collective-permute-start | bytes 3080 | tf_op jit(solution)/shard_map/ppermute | solution.py:200
  33.8 3.6 %collective-permute-start.8 = (f32[1,256]{1,0:T(1,128)S(1)}, f32[1,256]{1,0:T(1,128)S(1)}, u32[]{:S(2)}, u32[]{:S(2)}) collective-permute-start(f32[1,256]{1,0:T(1,128)S(1)} %slice.19), channel_id=1, source_target_pairs={{0,2},{2,0},{1,3},{3,1},{4,6},{6,4},{5,7},{7,5},{8,10},{10,8},{9,1... | collective-permute-start | bytes 3080 | tf_op jit(solution)/shard_map/ppermute | solution.py:208

commit v3 on v2

--- a/solution.py
+++ b/solution.py
@@ -200,12 +200,12 @@
             answers.append(lax.ppermute(back[0], "workers", home))
 
     kept = kept.reshape(n_team, n_sub, rows)
-    ends = kept[:, 0]
+    ends = kept[0]
+    for dt in range(1, n_team):
+        ends = jnp.maximum(ends, lax.ppermute(kept[dt], "team", shift(n_team, -dt)))
+    best = ends[0:1]
     for ds in range(1, n_sub):
-        ends = jnp.maximum(ends, lax.ppermute(kept[:, ds], "sub", shift(n_sub, -ds)))
-    best = ends[0:1]
-    for dt in range(1, n_team):
-        best = jnp.maximum(best, lax.ppermute(ends[dt : dt + 1], "team", shift(n_team, -dt)))
+        best = jnp.maximum(best, lax.ppermute(ends[ds : ds + 1], "sub", shift(n_sub, -ds)))
     for answer in answers:
         best = jnp.maximum(best, answer)
     return best.reshape(rows)

time: 38.2 us -> 37.2 us (0.974)
  waiting for transfers between devices: 17.6 us -> 16.7 us
    ppermute x2, waiting for transfers between devices: 2.08 us -> 0.01 us  [the longest x1 0.01 us: on_device(): ends = jnp.maximum(ends, lax.ppermute(kept[dt], 'team', shift(n_team, -dt)))]
    ppermute x1, waiting for transfers between devices: 0.01 us -> 1.21 us  [on_device(): answers.append(lax.ppermute(back[0], 'workers', home))]
where the time goes in v3:
time: 37.2 us; the launch traced here: 37 us
  waiting for transfers between devices  16.7 us (45%)
  starting transfers between devices  12.8 us (34%)
  Pallas kernels  6.17 us (17%)
  other arithmetic  1.29 us (3%)
    ppermute x1, waiting for transfers between devices, gather(): first = lax.ppermute(block, 'team', shift(n_team, dt)) if dt else block  12.4 us
    pallas_call x3, Pallas kernels, kernel(): pl.pallas_call(body, out_shape=out_shape, in_specs=[VMEM] * len(args), ou...  6.17 us
    ppermute x1, starting transfers between devices, on_device(): far = [lax.ppermute(embeddings, 'workers', turn) for turn in far_turns]  4.04 us
    ppermute x1, starting transfers between devices, on_device(): answers.append(lax.ppermute(back[0], 'workers', home))  3.23 us
    ppermute x2, waiting for transfers between devices, gather(): blocks.append(lax.ppermute(first, 'sub', shift(n_sub, ds)))  2.3 us
    ppermute x1, starting transfers between devices, gather(): first = lax.ppermute(block, 'team', shift(n_team, dt)) if dt else block  1.7 us
    ppermute x1, starting transfers between devices, on_device(): near = lax.ppermute(embeddings, 'workers', near_turn) if near_turn else None  1.58 us
    ppermute x1, starting transfers between devices, on_device(): ends = jnp.maximum(ends, lax.ppermute(kept[dt], 'team', shift(n_team, -dt)))  1.56 us
  transfers between devices with their start and end apart: 10, of which 4 were waited for; matrix products, arithmetic and copies ran while one was open for 2% of the time, Pallas kernels for 12%

profile of v3, /device:TPU:0, one launch (start us, length us, event | category | flops | bytes accessed | tf_op | source)
XLA Modules:
  0.0 37.0 jit_solution(8647212536325570019)
XLA Ops:
  0.0 4.0 %collective-permute-start.3 = (bf16[256,1024]{1,0:T(8,128)(2,1)}, bf16[256,1024]{1,0:T(8,128)(2,1)S(1)}, u32[]{:S(2)}, u32[]{:S(2)}) collective-permute-start(bf16[256,1024]{1,0:T(8,128)(2,1)} %param.6), channel_id=1, source_target_pairs={{0,8},{8,4},{4,12},{12,0},{1,9},{9,5},{5,13},{13,1},{2,10},{10,6},... | collective-permute-start | bytes 1572872 | tf_op jit(solution)/shard_map/ppermute | solution.py:144
  4.0 1.6 %collective-permute-start.5 = (bf16[256,1024]{1,0:T(8,128)(2,1)}, bf16[256,1024]{1,0:T(8,128)(2,1)S(1)}, u32[]{:S(2)}, u32[]{:S(2)}) collective-permute-start(bf16[256,1024]{1,0:T(8,128)(2,1)} %param.6), channel_id=1, source_target_pairs={{0,4},{8,12},{4,0},{12,8},{1,5},{9,13},{5,1},{13,9},{2,6},{10,14},... | collective-permute-start | bytes 1572872 | tf_op jit(solution)/shard_map/ppermute | solution.py:145
  5.6 0.7 %pad_add_fusion = s32[3,256]{1,0:T(4,128)S(1)} fusion(s32[1,256]{1,0:T(1,128)} %bitcast.4, s32[1,256]{1,0:T(1,128)} %bitcast.5, s32[1,256]{1,0:T(1,128)} %bitcast.6), kind=kLoop, calls=%fused_computation | loop fusion | flops 1536 | bytes 6144 | tf_op jit(solution)/shard_map/concatenate | solution.py:146
  6.3 0.0 collective-permute-start.4
  6.3 18.5 %conditional.1 = (bf16[272,1024]{1,0:T(8,128)(2,1)}, bf16[272,1024]{1,0:T(8,128)(2,1)}, bf16[272,1024]{1,0:T(8,128)(2,1)}, bf16[272,1024]{1,0:T(8,128)(2,1)}) conditional(s32[]{:T(128)} %convert_element_type.3, () %tuple.13, (bf16[256,1024]{1,0:T(8,128)(2,1)}, s32[3,256]{1,0:T(4,128)S(1)}) %tuple.14), branch_computations={%region_0.0_spmd, %region_1.0_spmd} | conditional | bytes 6684824 | solution.py:167
  6.3 2.0 %pack.1 = bf16[272,1024]{1,0:T(8,128)(2,1)} custom-call(bf16[256,1024]{1,0:T(8,128)(2,1)} %get-tuple-element.9.raw, s32[3,256]{1,0:T(4,128)S(1)} %get-tuple-element.10.ids), custom_call_target="tpu_custom_call" | custom-call | tf_op jit(solution)/shard_map/cond/branch_1_fun/pack/pallas_call | solution.py:115
  8.4 1.7 %collective-permute-start.1 = (bf16[272,1024]{1,0:T(8,128)(2,1)}, bf16[272,1024]{1,0:T(8,128)(2,1)}, u32[]{:S(2)}, u32[]{:S(2)}) collective-permute-start(bf16[272,1024]{1,0:T(8,128)(2,1)} %pack.1), channel_id=1, source_target_pairs={{0,2},{2,0},{1,3},{3,1},{4,6},{6,4},{5,7},{7,5},{8,10},{10,8},{9,1... | collective-permute-start | bytes 1671176 | tf_op jit(solution)/shard_map/cond/branch_1_fun/ppermute | solution.py:161
  10.1 0.0 collective-permute-start
  10.1 12.4 %collective-permute-done.1 = bf16[272,1024]{1,0:T(8,128)(2,1)} collective-permute-done((bf16[272,1024]{1,0:T(8,128)(2,1)}, bf16[272,1024]{1,0:T(8,128)(2,1)}, u32[]{:S(2)}, u32[]{:S(2)}) %collective-permute-start.1) | collective-permute-done | bytes 557088 | tf_op jit(solution)/shard_map/cond/branch_1_fun/ppermute | solution.py:161
  22.5 0.0 collective-permute-start.2
  22.5 0.0 collective-permute-done
  22.5 2.3 %collective-permute-done.2 = bf16[272,1024]{1,0:T(8,128)(2,1)} collective-permute-done((bf16[272,1024]{1,0:T(8,128)(2,1)}, bf16[272,1024]{1,0:T(8,128)(2,1)}, u32[]{:S(2)}, u32[]{:S(2)}) %collective-permute-start.2) | collective-permute-done | bytes 557088 | tf_op jit(solution)/shard_map/cond/branch_1_fun/ppermute | solution.py:164
  24.8 0.6 %collective-permute-start.6 = (s32[3,256]{1,0:T(4,128)S(1)}, s32[3,256]{1,0:T(4,128)S(1)}, u32[]{:S(2)}, u32[]{:S(2)}) collective-permute-start(s32[3,256]{1,0:T(4,128)S(1)} %pad_add_fusion), channel_id=1, source_target_pairs={{0,4},{8,12},{4,0},{12,8},{1,5},{9,13},{5,1},{13,9},{2,6},{10,14},... | collective-permute-start | bytes 9224 | tf_op jit(solution)/shard_map/ppermute | solution.py:150
  25.4 2.5 %own.1 = (bf16[1024,1024]{1,0:T(8,128)(2,1)S(1)}, s32[4,256]{1,0:T(4,128)S(1)}, f32[4,256]{1,0:T(4,128)S(1)}) custom-call(bf16[272,1024]{1,0:T(8,128)(2,1)} %get-tuple-element.20.refs_0_, bf16[272,1024]{1,0:T(8,128)(2,1)} %get-tuple-element.21.refs_1_, bf16[272,1024]{1,0:T(8,128)(2,1)} %get-tuple-element.22.refs_2_, bf16[272,1024]{1,0:T(8,128)(2,1)} %get-tuple-element.23.refs_3_), custom_call_target="tpu_custom_call" | custom-call | tf_op jit(solution)/shard_map/own/pallas_call | solution.py:115
  27.9 0.8 %collective-permute-done.4.refs_4_ = s32[3,256]{1,0:T(4,128)S(1)} collective-permute-done((s32[3,256]{1,0:T(4,128)S(1)}, s32[3,256]{1,0:T(4,128)S(1)}, u32[]{:S(2)}, u32[]{:S(2)}) %collective-permute-start.4) | collective-permute-done | bytes 3104 | tf_op jit(solution)/shard_map/ppermute | solution.py:149
  28.7 0.0 collective-permute-done.6.refs_6_
  28.7 0.0 collective-permute-done.3.refs_3_
  28.7 0.0 collective-permute-done.5.refs_5_
  28.7 1.7 %meet.1 = (f32[4,256]{1,0:T(4,128)S(1)}, f32[1,256]{1,0:T(1,128)S(1)}) custom-call(bf16[1024,1024]{1,0:T(8,128)(2,1)S(1)} %get-tuple-element.24.refs_0_, s32[4,256]{1,0:T(4,128)S(1)} %get-tuple-element.25.refs_1_, f32[4,256]{1,0:T(4,128)S(1)} %get-tuple-element.26.refs_2_, bf16[256,1024]{1,0:T(8,128)(2,1)S(1)} %collective-permute-done.3.refs_3_, ...), custom_call_target="tpu_custom_call" | custom-call | tf_op jit(solution)/shard_map/meet/pallas_call | solution.py:115
  30.4 1.6 %collective-permute-start.7 = (f32[2,256]{1,0:T(2,128)S(1)}, f32[2,256]{1,0:T(2,128)S(1)}, u32[]{:S(2)}, u32[]{:S(2)}) collective-permute-start(f32[2,256]{1,0:T(2,128)S(1)} %slice.15), channel_id=1, source_target_pairs={{0,2},{2,0},{1,3},{3,1},{4,6},{6,4},{5,7},{7,5},{8,10},{10,8},{9,1... | collective-permute-start | bytes 6152 | tf_op jit(solution)/shard_map/ppermute | solution.py:205
  31.9 3.2 %collective-permute-start.9 = (f32[1,256]{1,0:T(1,128)S(1)}, f32[1,256]{1,0:T(1,128)S(1)}, u32[]{:S(2)}, u32[]{:S(2)}) collective-permute-start(f32[1,256]{1,0:T(1,128)S(1)} %get-tuple-element.28), channel_id=1, source_target_pairs={{8,0},{4,8},{12,4},{0,12},{9,1},{5,9},{13,5},{1,13},{10,2},{6,10},... | collective-permute-start | bytes 3080 | tf_op jit(solution)/shard_map/ppermute | solution.py:200
  35.2 0.0 collective-permute-done.7
  35.2 0.1 collective-permute-start.8
  35.3 1.2 %collective-permute-done.9 = f32[1,256]{1,0:T(1,128)S(1)} collective-permute-done((f32[1,256]{1,0:T(1,128)S(1)}, f32[1,256]{1,0:T(1,128)S(1)}, u32[]{:S(2)}, u32[]{:S(2)}) %collective-permute-start.9) | collective-permute-done | bytes 1056 | tf_op jit(solution)/shard_map/ppermute | solution.py:200
  36.5 0.0 collective-permute-done.8
  36.5 0.6 %fusion = f32[1,256]{1,0:T(1,128)} fusion(f32[1,256]{1,0:T(1,128)S(1)} %collective-permute-done.9, f32[1,256]{1,0:T(1,128)S(1)} %collective-permute-done.8, f32[2,256]{1,0:T(2,128)S(1)} %slice_maximum_fusion), kind=kLoop, calls=%fused_computation.3 | loop fusion | flops 512 | bytes 4096 | tf_op jit(solution)/shard_map/max | solution.py:210
  (3 shorter events, 0.0 us)
Async XLA Ops:
  0.0 28.7 %collective-permute-start.3 = (bf16[256,1024]{1,0:T(8,128)(2,1)}, bf16[256,1024]{1,0:T(8,128)(2,1)S(1)}, u32[]{:S(2)}, u32[]{:S(2)}) collective-permute-start(bf16[256,1024]{1,0:T(8,128)(2,1)} %param.6), channel_id=1, source_target_pairs={{0,8},{8,4},{4,12},{12,0},{1,9},{9,5},{5,13},{13,1},{2,10},{10,6},... | collective-permute-start | bytes 1572872 | tf_op jit(solution)/shard_map/ppermute | solution.py:144
  4.0 24.7 %collective-permute-start.5 = (bf16[256,1024]{1,0:T(8,128)(2,1)}, bf16[256,1024]{1,0:T(8,128)(2,1)S(1)}, u32[]{:S(2)}, u32[]{:S(2)}) collective-permute-start(bf16[256,1024]{1,0:T(8,128)(2,1)} %param.6), channel_id=1, source_target_pairs={{0,4},{8,12},{4,0},{12,8},{1,5},{9,13},{5,1},{13,9},{2,6},{10,14},... | collective-permute-start | bytes 1572872 | tf_op jit(solution)/shard_map/ppermute | solution.py:145
  6.3 22.4 %collective-permute-start.4 = (s32[3,256]{1,0:T(4,128)S(1)}, s32[3,256]{1,0:T(4,128)S(1)}, u32[]{:S(2)}, u32[]{:S(2)}) collective-permute-start(s32[3,256]{1,0:T(4,128)S(1)} %pad_add_fusion), channel_id=1, source_target_pairs={{0,8},{8,4},{4,12},{12,0},{1,9},{9,5},{5,13},{13,1},{2,10},{10,6},... | collective-permute-start | bytes 9224 | tf_op jit(solution)/shard_map/ppermute | solution.py:149
  8.4 14.1 %collective-permute-start.1 = (bf16[272,1024]{1,0:T(8,128)(2,1)}, bf16[272,1024]{1,0:T(8,128)(2,1)}, u32[]{:S(2)}, u32[]{:S(2)}) collective-permute-start(bf16[272,1024]{1,0:T(8,128)(2,1)} %pack.1), channel_id=1, source_target_pairs={{0,2},{2,0},{1,3},{3,1},{4,6},{6,4},{5,7},{7,5},{8,10},{10,8},{9,1... | collective-permute-start | bytes 1671176 | tf_op jit(solution)/shard_map/cond/branch_1_fun/ppermute | solution.py:161
  10.1 12.4 %collective-permute-start = (bf16[272,1024]{1,0:T(8,128)(2,1)}, bf16[272,1024]{1,0:T(8,128)(2,1)}, u32[]{:S(2)}, u32[]{:S(2)}) collective-permute-start(bf16[272,1024]{1,0:T(8,128)(2,1)} %pack.1), channel_id=1, source_target_pairs={{0,1},{1,0},{2,3},{3,2},{4,5},{5,4},{6,7},{7,6},{8,9},{9,8},{10,11... | collective-permute-start | bytes 1671176 | tf_op jit(solution)/shard_map/cond/branch_1_fun/ppermute | solution.py:164
  22.5 2.3 %collective-permute-start.2 = (bf16[272,1024]{1,0:T(8,128)(2,1)}, bf16[272,1024]{1,0:T(8,128)(2,1)}, u32[]{:S(2)}, u32[]{:S(2)}) collective-permute-start(bf16[272,1024]{1,0:T(8,128)(2,1)} %collective-permute-done.1), channel_id=1, source_target_pairs={{0,1},{1,0},{2,3},{3,2},{4,5},{5,4},{6,7},{7,6},{8,9},{9,8},{10,11... | collective-permute-start | bytes 1671176 | tf_op jit(solution)/shard_map/cond/branch_1_fun/ppermute | solution.py:164
  24.8 3.9 %collective-permute-start.6 = (s32[3,256]{1,0:T(4,128)S(1)}, s32[3,256]{1,0:T(4,128)S(1)}, u32[]{:S(2)}, u32[]{:S(2)}) collective-permute-start(s32[3,256]{1,0:T(4,128)S(1)} %pad_add_fusion), channel_id=1, source_target_pairs={{0,4},{8,12},{4,0},{12,8},{1,5},{9,13},{5,1},{13,9},{2,6},{10,14},... | collective-permute-start | bytes 9224 | tf_op jit(solution)/shard_map/ppermute | solution.py:150
  30.4 4.8 %collective-permute-start.7 = (f32[2,256]{1,0:T(2,128)S(1)}, f32[2,256]{1,0:T(2,128)S(1)}, u32[]{:S(2)}, u32[]{:S(2)}) collective-permute-start(f32[2,256]{1,0:T(2,128)S(1)} %slice.15), channel_id=1, source_target_pairs={{0,2},{2,0},{1,3},{3,1},{4,6},{6,4},{5,7},{7,5},{8,10},{10,8},{9,1... | collective-permute-start | bytes 6152 | tf_op jit(solution)/shard_map/ppermute | solution.py:205
  31.9 4.5 %collective-permute-start.9 = (f32[1,256]{1,0:T(1,128)S(1)}, f32[1,256]{1,0:T(1,128)S(1)}, u32[]{:S(2)}, u32[]{:S(2)}) collective-permute-start(f32[1,256]{1,0:T(1,128)S(1)} %get-tuple-element.28), channel_id=1, source_target_pairs={{8,0},{4,8},{12,4},{0,12},{9,1},{5,9},{13,5},{1,13},{10,2},{6,10},... | collective-permute-start | bytes 3080 | tf_op jit(solution)/shard_map/ppermute | solution.py:200
  35.2 1.3 %collective-permute-start.8 = (f32[1,256]{1,0:T(1,128)S(1)}, f32[1,256]{1,0:T(1,128)S(1)}, u32[]{:S(2)}, u32[]{:S(2)}) collective-permute-start(f32[1,256]{1,0:T(1,128)S(1)} %slice.19), channel_id=1, source_target_pairs={{0,1},{1,0},{2,3},{3,2},{4,5},{5,4},{6,7},{7,6},{8,9},{9,8},{10,11... | collective-permute-start | bytes 3080 | tf_op jit(solution)/shard_map/ppermute | solution.py:208

commit v4 on v3

--- a/solution.py
+++ b/solution.py
@@ -10,6 +10,7 @@
 KC = 16
 EXTRA = 16
 VMEM = pl.BlockSpec(memory_space=pltpu.VMEM)
+HBM = pl.BlockSpec(memory_space=pl.ANY)
 
 
 def normalise(raw):
@@ -27,9 +28,9 @@
     return code_of(ids[0:1, :], ids[1:2, :], place // 256, place % 256)
 
 
-def code_at(block, rows):
-    last = block[rows : rows + EXTRA, :].astype(jnp.float32)[0:1, :].astype(jnp.int32)
-    return code_of(*[last[:, i * rows : (i + 1) * rows] for i in range(4)])
+def code_of_last(last, rows):
+    line = last.astype(jnp.float32)[0:1, :].astype(jnp.int32)
+    return code_of(*[line[:, i * rows : (i + 1) * rows] for i in range(4)])
 
 
 def as_column(row):
@@ -58,54 +59,75 @@
     block[rows : rows + EXTRA, :] = last.astype(jnp.bfloat16)
 
 
-def own_kernel(rows, *refs):
-    blocks, (plane, codes, kept) = refs[:-3], refs[-3:]
-    mine = blocks[0][0:rows, :]
-    column = as_column(code_at(blocks[0], rows))
+def load_kernel(rows, *refs):
+    *blocks, plane, codes, lasts, sems = refs
+    copies = [
+        pltpu.make_async_copy(b.at[rows : rows + EXTRA, :], lasts.at[i], sems.at[0, i])
+        for i, b in enumerate(blocks)
+    ] + [
+        pltpu.make_async_copy(
+            b.at[0:rows, :], plane.at[i * rows : (i + 1) * rows, :], sems.at[1, i]
+        )
+        for i, b in enumerate(blocks)
+    ]
+    for copy in copies:
+        copy.start()
+    for copy in copies:
+        copy.wait()
+    for i in range(len(blocks)):
+        codes[i : i + 1, :] = code_of_last(lasts[i], rows)
+
+
+def own_kernel(rows, n_plane, plane, codes, best):
+    mine, column = plane[0:rows, :], as_column(codes[0:1, :])
     found = jnp.full((rows, 128), -1.0, jnp.float32)
-    for index, block in enumerate(blocks):
-        here = block[0:rows, :]
-        code = code_at(block, rows)
-        plane[index * rows : (index + 1) * rows, :] = here
-        codes[index : index + 1, :] = code
-        scores = scores_of(mine, here)
+    for index in range(n_plane):
+        scores = scores_of(mine, plane[index * rows : (index + 1) * rows, :])
         for at in range(0, rows, 128):
-            other = code[:, at : at + 128]
+            other = codes[index : index + 1, at : at + 128]
             earlier = ((column ^ other) < 65536) & (column > other)
             found = jnp.maximum(found, jnp.where(earlier, scores[:, at : at + 128], -1.0))
-    kept[...] = jnp.full(kept.shape, -1.0, jnp.float32)
-    kept[0:1, :] = fold_rows(found)
-
-
-def meet_kernel(rows, n_plane, has_far, has_near, *refs):
-    (plane, codes, part), refs = refs[:3], list(refs[3:])
+    best[...] = fold_rows(found)
+
+
+def score_kernel(rows, n_plane, plane, came, scores):
+    came_rows = normalise(came[...])
+    for index in range(n_plane):
+        lanes = slice(index * rows, (index + 1) * rows)
+        scores[:, lanes] = scores_of(came_rows, plane[lanes, :])
+
+
+def meet_kernel(rows, n_plane, has_far, has_near, has_part, *refs):
+    plane, codes, *refs = refs
+    part = refs.pop(0) if has_part else None
     if has_far:
-        far, far_ids = refs.pop(0), refs.pop(0)
-        far_rows, far_column = normalise(far[...]), as_column(code_in(far_ids))
+        far_scores, far_ids = refs.pop(0), refs.pop(0)
+        far_column = as_column(code_in(far_ids))
         found = jnp.full((rows, 128), -1.0, jnp.float32)
     if has_near:
         near, near_ids = refs.pop(0), refs.pop(0)
         near_rows, near_column = normalise(near[...]), as_column(code_in(near_ids))
     kept = refs.pop(0)
     for index in range(n_plane):
-        here = plane[index * rows : (index + 1) * rows, :]
-        far_scores = scores_of(far_rows, here) if has_far else None
-        near_scores = scores_of(near_rows, here) if has_near else None
+        if has_near:
+            near_scores = scores_of(near_rows, plane[index * rows : (index + 1) * rows, :])
         for at in range(0, rows, 128):
             lanes = slice(at, at + 128)
             other = codes[index : index + 1, lanes]
             keep = jnp.full((rows, 128), -1.0, jnp.float32)
             if has_far:
-                shared = jnp.where((far_column ^ other) < 65536, far_scores[:, lanes], -1.0)
+                scores = far_scores[:, index * rows + at : index * rows + at + 128]
+                shared = jnp.where((far_column ^ other) < 65536, scores, -1.0)
                 later = far_column > other
                 found = jnp.maximum(found, jnp.where(later, shared, -1.0))
                 keep = jnp.where(later, -1.0, shared)
             if has_near:
                 earlier = ((near_column ^ other) < 65536) & (near_column < other)
                 keep = jnp.maximum(keep, jnp.where(earlier, near_scores[:, lanes], -1.0))
-            kept[index : index + 1, lanes] = jnp.maximum(
-                part[index : index + 1, lanes], jnp.max(keep, axis=0, keepdims=True)
-            )
+            keep = jnp.max(keep, axis=0, keepdims=True)
+            if has_part:
+                keep = jnp.maximum(keep, part[index : index + 1, lanes])
+            kept[index : index + 1, lanes] = keep
     if has_far:
         (back,) = refs
         back[...] = fold_rows(found)
@@ -169,35 +191,51 @@
         gather,
         lambda: (jnp.zeros((rows + EXTRA, width), jnp.bfloat16),) * n_plane,
     )
-    plane, codes, kept = kernel(
-        functools.partial(own_kernel, rows),
+    plane, codes = pl.pallas_call(
+        functools.partial(load_kernel, rows),
+        out_shape=(struct((n_plane * rows, width), jnp.bfloat16), struct((n_plane, rows), jnp.int32)),
+        in_specs=[HBM] * n_plane,
+        out_specs=(VMEM, VMEM),
+        scratch_shapes=[
+            pltpu.VMEM((n_plane, EXTRA, width), jnp.bfloat16),
+            pltpu.SemaphoreType.DMA((2, n_plane)),
+        ],
+        compiler_params=pltpu.CompilerParams(vmem_limit_bytes=40 * 1024 * 1024),
+        name="load",
+    )(*blocks)
+    (own,) = kernel(
+        functools.partial(own_kernel, rows, n_plane),
         "own",
-        (
-            struct((n_plane * rows, width), jnp.bfloat16),
-            struct((n_plane, rows), jnp.int32),
-            struct((n_plane, rows), jnp.float32),
-        ),
-        blocks,
-    )
-
-    answers = []
-    for index in range(max(len(far), 1)):
+        (struct((1, rows), jnp.float32),),
+        (plane, codes),
+    )
+    kept, answers = None, []
+    for index in range(max(len(far), 1 if near is not None else 0)):
         has_far, has_near = index < len(far), index == 0 and near is not None
-        if not has_far and not has_near:
-            break
-        came = (far[index], far_ids[index]) if has_far else ()
-        came += (near, near_ids) if has_near else ()
         out = (struct((n_plane, rows), jnp.float32),)
-        out += (struct((1, rows), jnp.float32),) if has_far else ()
+        args = (plane, codes) if kept is None else (plane, codes, kept)
+        if has_far:
+            (scores,) = kernel(
+                functools.partial(score_kernel, rows, n_plane),
+                "score",
+                (struct((rows, n_plane * rows), jnp.float32),),
+                (plane, far[index]),
+            )
+            args += (scores, far_ids[index])
+            out += (struct((1, rows), jnp.float32),)
+        if has_near:
+            args += (near, near_ids)
         kept, *back = kernel(
-            functools.partial(meet_kernel, rows, n_plane, has_far, has_near),
+            functools.partial(meet_kernel, rows, n_plane, has_far, has_near, kept is not None),
             "meet",
             out,
-            (plane, codes, kept, *came),
+            args,
         )
         if has_far:
             home = [(b, a) for a, b in far_turns[index]]
             answers.append(lax.ppermute(back[0], "workers", home))
+    if kept is None:
+        kept = jnp.full((n_plane, rows), -1.0, jnp.float32)
 
     kept = kept.reshape(n_team, n_sub, rows)
     ends = kept[0]
@@ -206,6 +244,7 @@
     best = ends[0:1]
     for ds in range(1, n_sub):
         best = jnp.maximum(best, lax.ppermute(ends[ds : ds + 1], "sub", shift(n_sub, -ds)))
+    best = jnp.maximum(best, own)
     for answer in answers:
         best = jnp.maximum(best, answer)
     return best.reshape(rows)

time: 37.2 us -> 36.7 us (0.987)
  waiting for transfers between devices: 16.7 us -> 15.8 us
    pallas_call x0 -> x1, Pallas kernels: none -> 1.69 us  [on_device(): pl.pallas_call(functools.partial(load_kernel, rows), out_shape=(struct((n...]
    pallas_call x3 -> x4, Pallas kernels: 6.17 us -> 4.83 us  [kernel(): pl.pallas_call(body, out_shape=out_shape, in_specs=[VMEM] * len(args), ou...]
    ppermute x1, waiting for transfers between devices: 1.21 us -> 0.3 us  [on_device(): answers.append(lax.ppermute(back[0], 'workers', home))]
  transfers between devices with their start and end apart: 10 -> 10, of which waited for: 4 -> 4; matrix products, arithmetic and copies ran while one was open for 2% -> 2% of each run, Pallas kernels for 12% -> 15%
where the time goes in v4:
time: 36.7 us; the launch traced here: 36.5 us
  waiting for transfers between devices  15.8 us (43%)
  starting transfers between devices  12.8 us (35%)
  Pallas kernels  6.52 us (18%)
  other arithmetic  1.29 us (4%)
    ppermute x1, waiting for transfers between devices, gather(): first = lax.ppermute(block, 'team', shift(n_team, dt)) if dt else block  12.4 us
    pallas_call x4, Pallas kernels, kernel(): pl.pallas_call(body, out_shape=out_shape, in_specs=[VMEM] * len(args), ou...  4.83 us
    ppermute x1, starting transfers between devices, on_device(): far = [lax.ppermute(embeddings, 'workers', turn) for turn in far_turns]  4.04 us
    ppermute x1, starting transfers between devices, on_device(): answers.append(lax.ppermute(back[0], 'workers', home))  3.23 us
    ppermute x2, waiting for transfers between devices, gather(): blocks.append(lax.ppermute(first, 'sub', shift(n_sub, ds)))  2.3 us
    ppermute x1, starting transfers between devices, gather(): first = lax.ppermute(block, 'team', shift(n_team, dt)) if dt else block  1.7 us
    pallas_call x1, Pallas kernels, on_device(): pl.pallas_call(functools.partial(load_kernel, rows), out_shape=(struct((n...  1.69 us
    ppermute x1, starting transfers between devices, on_device(): near = lax.ppermute(embeddings, 'workers', near_turn) if near_turn else None  1.58 us
  transfers between devices with their start and end apart: 10, of which 4 were waited for; matrix products, arithmetic and copies ran while one was open for 2% of the time, Pallas kernels for 15%

profile of v4, /device:TPU:0, one launch (start us, length us, event | category | flops | bytes accessed | tf_op | source)
XLA Modules:
  0.0 36.5 jit_solution(14697259589255449547)
XLA Ops:
  0.0 4.0 %collective-permute-start.3 = (bf16[256,1024]{1,0:T(8,128)(2,1)}, bf16[256,1024]{1,0:T(8,128)(2,1)S(1)}, u32[]{:S(2)}, u32[]{:S(2)}) collective-permute-start(bf16[256,1024]{1,0:T(8,128)(2,1)} %param.6), channel_id=1, source_target_pairs={{0,8},{8,4},{4,12},{12,0},{1,9},{9,5},{5,13},{13,1},{2,10},{10,6},... | collective-permute-start | bytes 1572872 | tf_op jit(solution)/shard_map/ppermute | solution.py:166
  4.0 1.6 %collective-permute-start.5 = (bf16[256,1024]{1,0:T(8,128)(2,1)}, bf16[256,1024]{1,0:T(8,128)(2,1)S(1)}, u32[]{:S(2)}, u32[]{:S(2)}) collective-permute-start(bf16[256,1024]{1,0:T(8,128)(2,1)} %param.6), channel_id=1, source_target_pairs={{0,4},{8,12},{4,0},{12,8},{1,5},{9,13},{5,1},{13,9},{2,6},{10,14},... | collective-permute-start | bytes 1572872 | tf_op jit(solution)/shard_map/ppermute | solution.py:167
  5.6 0.7 %pad_add_fusion = s32[3,256]{1,0:T(4,128)S(1)} fusion(s32[1,256]{1,0:T(1,128)} %bitcast.4, s32[1,256]{1,0:T(1,128)} %bitcast.5, s32[1,256]{1,0:T(1,128)} %bitcast.6), kind=kLoop, calls=%fused_computation | loop fusion | flops 1536 | bytes 6144 | tf_op jit(solution)/shard_map/concatenate | solution.py:168
  6.3 0.0 collective-permute-start.4
  6.3 18.5 %conditional.1 = (bf16[272,1024]{1,0:T(8,128)(2,1)}, bf16[272,1024]{1,0:T(8,128)(2,1)}, bf16[272,1024]{1,0:T(8,128)(2,1)}, bf16[272,1024]{1,0:T(8,128)(2,1)}) conditional(s32[]{:T(128)} %convert_element_type.3, () %tuple.13, (bf16[256,1024]{1,0:T(8,128)(2,1)}, s32[3,256]{1,0:T(4,128)S(1)}) %tuple.14), branch_computations={%region_0.0_spmd, %region_1.0_spmd} | conditional | bytes 6684824 | solution.py:189
  6.3 2.0 %pack.1 = bf16[272,1024]{1,0:T(8,128)(2,1)} custom-call(bf16[256,1024]{1,0:T(8,128)(2,1)} %get-tuple-element.9.raw, s32[3,256]{1,0:T(4,128)S(1)} %get-tuple-element.10.ids), custom_call_target="tpu_custom_call" | custom-call | tf_op jit(solution)/shard_map/cond/branch_1_fun/pack/pallas_call | solution.py:137
  8.4 1.7 %collective-permute-start.1 = (bf16[272,1024]{1,0:T(8,128)(2,1)}, bf16[272,1024]{1,0:T(8,128)(2,1)}, u32[]{:S(2)}, u32[]{:S(2)}) collective-permute-start(bf16[272,1024]{1,0:T(8,128)(2,1)} %pack.1), channel_id=1, source_target_pairs={{0,2},{2,0},{1,3},{3,1},{4,6},{6,4},{5,7},{7,5},{8,10},{10,8},{9,1... | collective-permute-start | bytes 1671176 | tf_op jit(solution)/shard_map/cond/branch_1_fun/ppermute | solution.py:183
  10.1 0.0 collective-permute-start
  10.1 12.4 %collective-permute-done.1 = bf16[272,1024]{1,0:T(8,128)(2,1)} collective-permute-done((bf16[272,1024]{1,0:T(8,128)(2,1)}, bf16[272,1024]{1,0:T(8,128)(2,1)}, u32[]{:S(2)}, u32[]{:S(2)}) %collective-permute-start.1) | collective-permute-done | bytes 557088 | tf_op jit(solution)/shard_map/cond/branch_1_fun/ppermute | solution.py:183
  22.5 0.0 collective-permute-start.2
  22.5 0.0 collective-permute-done
  22.5 2.3 %collective-permute-done.2 = bf16[272,1024]{1,0:T(8,128)(2,1)} collective-permute-done((bf16[272,1024]{1,0:T(8,128)(2,1)}, bf16[272,1024]{1,0:T(8,128)(2,1)}, u32[]{:S(2)}, u32[]{:S(2)}) %collective-permute-start.2) | collective-permute-done | bytes 557088 | tf_op jit(solution)/shard_map/cond/branch_1_fun/ppermute | solution.py:186
  24.8 0.6 %collective-permute-start.6 = (s32[3,256]{1,0:T(4,128)S(1)}, s32[3,256]{1,0:T(4,128)S(1)}, u32[]{:S(2)}, u32[]{:S(2)}) collective-permute-start(s32[3,256]{1,0:T(4,128)S(1)} %pad_add_fusion), channel_id=1, source_target_pairs={{0,4},{8,12},{4,0},{12,8},{1,5},{9,13},{5,1},{13,9},{2,6},{10,14},... | collective-permute-start | bytes 9224 | tf_op jit(solution)/shard_map/ppermute | solution.py:172
  25.4 1.7 %load.1 = (bf16[1024,1024]{1,0:T(8,128)(2,1)S(1)}, s32[4,256]{1,0:T(4,128)S(1)}) custom-call(bf16[272,1024]{1,0:T(8,128)(2,1)} %get-tuple-element.19.refs_0_, bf16[272,1024]{1,0:T(8,128)(2,1)} %get-tuple-element.20.refs_1_, bf16[272,1024]{1,0:T(8,128)(2,1)} %get-tuple-element.21.refs_2_, bf16[272,1024]{1,0:T(8,128)(2,1)} %get-tuple-element.22.refs_3_), custom_call_target="tpu_custom_call" | custom-call | tf_op jit(solution)/shard_map/load/pallas_call | solution.py:194
  27.1 0.0 collective-permute-done.3.came
  27.1 0.8 %score.1.refs_2_ = f32[256,1024]{1,0:T(8,128)S(1)} custom-call(bf16[1024,1024]{1,0:T(8,128)(2,1)S(1)} %get-tuple-element.23.plane.refs_0_, bf16[256,1024]{1,0:T(8,128)(2,1)S(1)} %collective-permute-done.3.came), custom_call_target="tpu_custom_call" | custom-call | tf_op jit(solution)/shard_map/score/pallas_call | solution.py:137
  27.9 0.8 %collective-permute-done.4.refs_3_ = s32[3,256]{1,0:T(4,128)S(1)} collective-permute-done((s32[3,256]{1,0:T(4,128)S(1)}, s32[3,256]{1,0:T(4,128)S(1)}, u32[]{:S(2)}, u32[]{:S(2)}) %collective-permute-start.4) | collective-permute-done | bytes 3104 | tf_op jit(solution)/shard_map/ppermute | solution.py:171
  28.7 0.0 collective-permute-done.6.refs_5_
  28.7 0.0 collective-permute-done.5.refs_4_
  28.7 1.1 %meet.1 = (f32[4,256]{1,0:T(4,128)S(1)}, f32[1,256]{1,0:T(1,128)S(1)}) custom-call(bf16[1024,1024]{1,0:T(8,128)(2,1)S(1)} %get-tuple-element.23.plane.refs_0_, s32[4,256]{1,0:T(4,128)S(1)} %get-tuple-element.24.refs_1_.codes, f32[256,1024]{1,0:T(8,128)S(1)} %score.1.refs_2_, s32[3,256]{1,0:T(4,128)S(1)} %collective-permute-done.4.refs_3_, ...), custom_call_target="tpu_custom_call" | custom-call | tf_op jit(solution)/shard_map/meet/pallas_call | solution.py:137
  29.8 1.6 %collective-permute-start.7 = (f32[2,256]{1,0:T(2,128)S(1)}, f32[2,256]{1,0:T(2,128)S(1)}, u32[]{:S(2)}, u32[]{:S(2)}) collective-permute-start(f32[2,256]{1,0:T(2,128)S(1)} %slice.15), channel_id=1, source_target_pairs={{0,2},{2,0},{1,3},{3,1},{4,6},{6,4},{5,7},{7,5},{8,10},{10,8},{9,1... | collective-permute-start | bytes 6152 | tf_op jit(solution)/shard_map/ppermute | solution.py:243
  31.4 3.2 %collective-permute-start.9 = (f32[1,256]{1,0:T(1,128)S(1)}, f32[1,256]{1,0:T(1,128)S(1)}, u32[]{:S(2)}, u32[]{:S(2)}) collective-permute-start(f32[1,256]{1,0:T(1,128)S(1)} %get-tuple-element.26), channel_id=1, source_target_pairs={{8,0},{4,8},{12,4},{0,12},{9,1},{5,9},{13,5},{1,13},{10,2},{6,10},... | collective-permute-start | bytes 3080 | tf_op jit(solution)/shard_map/ppermute | solution.py:236
  34.6 0.0 collective-permute-done.7
  34.6 0.1 collective-permute-start.8
  34.7 0.9 %own.1 = f32[1,256]{1,0:T(1,128)S(1)} custom-call(bf16[1024,1024]{1,0:T(8,128)(2,1)S(1)} %get-tuple-element.23.plane.refs_0_, s32[4,256]{1,0:T(4,128)S(1)} %get-tuple-element.24.refs_1_.codes), custom_call_target="tpu_custom_call" | custom-call | tf_op jit(solution)/shard_map/own/pallas_call | solution.py:137
  35.6 0.3 collective-permute-done.9
  35.9 0.0 collective-permute-done.8
  35.9 0.6 %fusion.1 = f32[1,256]{1,0:T(1,128)} fusion(f32[1,256]{1,0:T(1,128)S(1)} %collective-permute-done.9, f32[1,256]{1,0:T(1,128)S(1)} %own.1, f32[1,256]{1,0:T(1,128)S(1)} %collective-permute-done.8, f32[2,256]{1,0:T(2,128)S(1)} %slice_maximum_fusion), kind=kLoop, calls=%fused_computation.4 | loop fusion | flops 768 | bytes 5120 | tf_op jit(solution)/shard_map/max | solution.py:249
  (3 shorter events, 0.0 us)
Async XLA Ops:
  0.0 27.1 %collective-permute-start.3 = (bf16[256,1024]{1,0:T(8,128)(2,1)}, bf16[256,1024]{1,0:T(8,128)(2,1)S(1)}, u32[]{:S(2)}, u32[]{:S(2)}) collective-permute-start(bf16[256,1024]{1,0:T(8,128)(2,1)} %param.6), channel_id=1, source_target_pairs={{0,8},{8,4},{4,12},{12,0},{1,9},{9,5},{5,13},{13,1},{2,10},{10,6},... | collective-permute-start | bytes 1572872 | tf_op jit(solution)/shard_map/ppermute | solution.py:166
  4.0 24.7 %collective-permute-start.5 = (bf16[256,1024]{1,0:T(8,128)(2,1)}, bf16[256,1024]{1,0:T(8,128)(2,1)S(1)}, u32[]{:S(2)}, u32[]{:S(2)}) collective-permute-start(bf16[256,1024]{1,0:T(8,128)(2,1)} %param.6), channel_id=1, source_target_pairs={{0,4},{8,12},{4,0},{12,8},{1,5},{9,13},{5,1},{13,9},{2,6},{10,14},... | collective-permute-start | bytes 1572872 | tf_op jit(solution)/shard_map/ppermute | solution.py:167
  6.3 22.4 %collective-permute-start.4 = (s32[3,256]{1,0:T(4,128)S(1)}, s32[3,256]{1,0:T(4,128)S(1)}, u32[]{:S(2)}, u32[]{:S(2)}) collective-permute-start(s32[3,256]{1,0:T(4,128)S(1)} %pad_add_fusion), channel_id=1, source_target_pairs={{0,8},{8,4},{4,12},{12,0},{1,9},{9,5},{5,13},{13,1},{2,10},{10,6},... | collective-permute-start | bytes 9224 | tf_op jit(solution)/shard_map/ppermute | solution.py:171
  8.4 14.1 %collective-permute-start.1 = (bf16[272,1024]{1,0:T(8,128)(2,1)}, bf16[272,1024]{1,0:T(8,128)(2,1)}, u32[]{:S(2)}, u32[]{:S(2)}) collective-permute-start(bf16[272,1024]{1,0:T(8,128)(2,1)} %pack.1), channel_id=1, source_target_pairs={{0,2},{2,0},{1,3},{3,1},{4,6},{6,4},{5,7},{7,5},{8,10},{10,8},{9,1... | collective-permute-start | bytes 1671176 | tf_op jit(solution)/shard_map/cond/branch_1_fun/ppermute | solution.py:183
  10.1 12.4 %collective-permute-start = (bf16[272,1024]{1,0:T(8,128)(2,1)}, bf16[272,1024]{1,0:T(8,128)(2,1)}, u32[]{:S(2)}, u32[]{:S(2)}) collective-permute-start(bf16[272,1024]{1,0:T(8,128)(2,1)} %pack.1), channel_id=1, source_target_pairs={{0,1},{1,0},{2,3},{3,2},{4,5},{5,4},{6,7},{7,6},{8,9},{9,8},{10,11... | collective-permute-start | bytes 1671176 | tf_op jit(solution)/shard_map/cond/branch_1_fun/ppermute | solution.py:186
  22.5 2.3 %collective-permute-start.2 = (bf16[272,1024]{1,0:T(8,128)(2,1)}, bf16[272,1024]{1,0:T(8,128)(2,1)}, u32[]{:S(2)}, u32[]{:S(2)}) collective-permute-start(bf16[272,1024]{1,0:T(8,128)(2,1)} %collective-permute-done.1), channel_id=1, source_target_pairs={{0,1},{1,0},{2,3},{3,2},{4,5},{5,4},{6,7},{7,6},{8,9},{9,8},{10,11... | collective-permute-start | bytes 1671176 | tf_op jit(solution)/shard_map/cond/branch_1_fun/ppermute | solution.py:186
  24.8 3.9 %collective-permute-start.6 = (s32[3,256]{1,0:T(4,128)S(1)}, s32[3,256]{1,0:T(4,128)S(1)}, u32[]{:S(2)}, u32[]{:S(2)}) collective-permute-start(s32[3,256]{1,0:T(4,128)S(1)} %pad_add_fusion), channel_id=1, source_target_pairs={{0,4},{8,12},{4,0},{12,8},{1,5},{9,13},{5,1},{13,9},{2,6},{10,14},... | collective-permute-start | bytes 9224 | tf_op jit(solution)/shard_map/ppermute | solution.py:172
  29.8 4.8 %collective-permute-start.7 = (f32[2,256]{1,0:T(2,128)S(1)}, f32[2,256]{1,0:T(2,128)S(1)}, u32[]{:S(2)}, u32[]{:S(2)}) collective-permute-start(f32[2,256]{1,0:T(2,128)S(1)} %slice.15), channel_id=1, source_target_pairs={{0,2},{2,0},{1,3},{3,1},{4,6},{6,4},{5,7},{7,5},{8,10},{10,8},{9,1... | collective-permute-start | bytes 6152 | tf_op jit(solution)/shard_map/ppermute | solution.py:243
  31.4 4.5 %collective-permute-start.9 = (f32[1,256]{1,0:T(1,128)S(1)}, f32[1,256]{1,0:T(1,128)S(1)}, u32[]{:S(2)}, u32[]{:S(2)}) collective-permute-start(f32[1,256]{1,0:T(1,128)S(1)} %get-tuple-element.26), channel_id=1, source_target_pairs={{8,0},{4,8},{12,4},{0,12},{9,1},{5,9},{13,5},{1,13},{10,2},{6,10},... | collective-permute-start | bytes 3080 | tf_op jit(solution)/shard_map/ppermute | solution.py:236
  34.6 1.3 %collective-permute-start.8 = (f32[1,256]{1,0:T(1,128)S(1)}, f32[1,256]{1,0:T(1,128)S(1)}, u32[]{:S(2)}, u32[]{:S(2)}) collective-permute-start(f32[1,256]{1,0:T(1,128)S(1)} %slice.19), channel_id=1, source_target_pairs={{0,1},{1,0},{2,3},{3,2},{4,5},{5,4},{6,7},{7,6},{8,9},{9,8},{10,11... | collective-permute-start | bytes 3080 | tf_op jit(solution)/shard_map/ppermute | solution.py:246

commit v5 on v4

--- a/solution.py
+++ b/solution.py
@@ -91,46 +91,44 @@
 
 
 def score_kernel(rows, n_plane, plane, came, scores):
-    came_rows = normalise(came[...])
+    came_rows = came[...]
     for index in range(n_plane):
         lanes = slice(index * rows, (index + 1) * rows)
         scores[:, lanes] = scores_of(came_rows, plane[lanes, :])
 
 
-def meet_kernel(rows, n_plane, has_far, has_near, has_part, *refs):
+def meet_kernel(rows, n_plane, n_came, has_part, *refs):
     plane, codes, *refs = refs
     part = refs.pop(0) if has_part else None
-    if has_far:
-        far_scores, far_ids = refs.pop(0), refs.pop(0)
-        far_column = as_column(code_in(far_ids))
-        found = jnp.full((rows, 128), -1.0, jnp.float32)
-    if has_near:
-        near, near_ids = refs.pop(0), refs.pop(0)
-        near_rows, near_column = normalise(near[...]), as_column(code_in(near_ids))
-    kept = refs.pop(0)
+    scores, *refs = refs
+    columns = [as_column(code_in(refs.pop(0)))]
+    if n_came == 2:
+        packed = refs.pop(0)
+        came_rows = packed[0:rows, :]
+        columns.append(as_column(code_of_last(packed[rows : rows + EXTRA, :], rows)))
+    kept, back = refs
+    found = [jnp.full((rows, 128), -1.0, jnp.float32)] * n_came
     for index in range(n_plane):
-        if has_near:
-            near_scores = scores_of(near_rows, plane[index * rows : (index + 1) * rows, :])
+        block = slice(index * rows, (index + 1) * rows)
+        tables = [scores[:, block]]
+        if n_came == 2:
+            tables.append(scores_of(came_rows, plane[block, :]))
         for at in range(0, rows, 128):
             lanes = slice(at, at + 128)
             other = codes[index : index + 1, lanes]
-            keep = jnp.full((rows, 128), -1.0, jnp.float32)
-            if has_far:
-                scores = far_scores[:, index * rows + at : index * rows + at + 128]
-                shared = jnp.where((far_column ^ other) < 65536, scores, -1.0)
-                later = far_column > other
-                found = jnp.maximum(found, jnp.where(later, shared, -1.0))
-                keep = jnp.where(later, -1.0, shared)
-            if has_near:
-                earlier = ((near_column ^ other) < 65536) & (near_column < other)
-                keep = jnp.maximum(keep, jnp.where(earlier, near_scores[:, lanes], -1.0))
+            keep = None
+            for turn, (table, column) in enumerate(zip(tables, columns)):
+                shared = jnp.where((column ^ other) < 65536, table[:, lanes], -1.0)
+                later = column > other
+                found[turn] = jnp.maximum(found[turn], jnp.where(later, shared, -1.0))
+                kept_here = jnp.where(later, -1.0, shared)
+                keep = kept_here if keep is None else jnp.maximum(keep, kept_here)
             keep = jnp.max(keep, axis=0, keepdims=True)
             if has_part:
                 keep = jnp.maximum(keep, part[index : index + 1, lanes])
             kept[index : index + 1, lanes] = keep
-    if has_far:
-        (back,) = refs
-        back[...] = fold_rows(found)
+    for turn in range(n_came):
+        back[turn : turn + 1, :] = fold_rows(found[turn])
 
 
 def kernel(body, name, out_shape, args):
@@ -151,7 +149,7 @@
 def turns_of(n):
     half = n // 2
     line = [p // 2 + p % 2 * half for p in range(2 * half)] + list(range(2 * half, n))
-    turns = [[(line[p], line[(p + step) % n]) for p in range(n)] for step in range(1, half + 1)]
+    turns = [[(line[(p + step) % n], line[p]) for p in range(n)] for step in range(1, half + 1)]
     far = turns[: (n - 1) // 2]
     return far, turns[-1] if n % 2 == 0 else None
 
@@ -163,25 +161,43 @@
     struct = jax.ShapeDtypeStruct
     far_turns, near_turn = turns_of(n_work)
 
-    far = [lax.ppermute(embeddings, "workers", turn) for turn in far_turns]
-    near = lax.ppermute(embeddings, "workers", near_turn) if near_turn else None
+    axes = ("workers", "team", "sub")
+
+    def everywhere(turn_of):
+        return [
+            ((a * n_team + t) * n_sub + c, (b * n_team + t) * n_sub + c)
+            for t in range(n_team)
+            for c in range(n_sub)
+            for a, b in turn_of(c)
+        ]
+
+    turns = [everywhere(lambda c, turn=turn: turn) for turn in far_turns]
+    mixed = bool(far_turns) and near_turn is not None
+    if mixed:
+        turns[:1] = [
+            everywhere(lambda c: far_turns[0] if c % 2 else near_turn),
+            everywhere(lambda c: near_turn if c % 2 else far_turns[0]),
+        ]
+    elif near_turn is not None:
+        turns = [everywhere(lambda c: near_turn)]
     ids = jnp.concatenate(
         [owner_ids.reshape(1, rows), clusters.reshape(1, rows), priority.reshape(1, rows)], axis=0
     )
-    far_ids = [lax.ppermute(ids, "workers", turn) for turn in far_turns]
-    near_ids = lax.ppermute(ids, "workers", near_turn) if near_turn else None
+    whole = (struct((rows + EXTRA, width), jnp.bfloat16),)
+    (block,) = kernel(functools.partial(pack_kernel, rows), "pack", whole, (embeddings, ids))
+    came = [
+        lax.ppermute(block if mixed and i == 1 else embeddings, axes, turn)
+        for i, turn in enumerate(turns)
+    ]
+    came_ids = [
+        None if mixed and i == 1 else lax.ppermute(ids, axes, turn) for i, turn in enumerate(turns)
+    ]
 
     def gather():
-        (block,) = kernel(
-            functools.partial(pack_kernel, rows),
-            "pack",
-            (struct((rows + EXTRA, width), jnp.bfloat16),),
-            (embeddings, ids),
-        )
         blocks = []
         for dt in range(n_team):
             first = lax.ppermute(block, "team", shift(n_team, dt)) if dt else block
-            blocks.append(first)
+            blocks += [first] if dt else []
             for ds in range(1, n_sub):
                 blocks.append(lax.ppermute(first, "sub", shift(n_sub, ds)))
         return tuple(blocks)
@@ -189,8 +205,9 @@
     blocks = lax.cond(
         lax.axis_index("groups") < lax.axis_size("groups"),
         gather,
-        lambda: (jnp.zeros((rows + EXTRA, width), jnp.bfloat16),) * n_plane,
-    )
+        lambda: (jnp.zeros((rows + EXTRA, width), jnp.bfloat16),) * (n_plane - 1),
+    )
+    blocks = (block, *blocks)
     plane, codes = pl.pallas_call(
         functools.partial(load_kernel, rows),
         out_shape=(struct((n_plane * rows, width), jnp.bfloat16), struct((n_plane, rows), jnp.int32)),
@@ -210,30 +227,33 @@
         (plane, codes),
     )
     kept, answers = None, []
-    for index in range(max(len(far), 1 if near is not None else 0)):
-        has_far, has_near = index < len(far), index == 0 and near is not None
-        out = (struct((n_plane, rows), jnp.float32),)
+    steps = [[i] for i in range(len(turns))]
+    if mixed:
+        steps[:2] = [[0, 1]]
+    for number, step in enumerate(steps):
+        first, *second = step
+        (scores,) = kernel(
+            functools.partial(score_kernel, rows, n_plane),
+            "score",
+            (struct((rows, n_plane * rows), jnp.float32),),
+            (plane, normalise(came[first])),
+        )
         args = (plane, codes) if kept is None else (plane, codes, kept)
-        if has_far:
-            (scores,) = kernel(
-                functools.partial(score_kernel, rows, n_plane),
-                "score",
-                (struct((rows, n_plane * rows), jnp.float32),),
-                (plane, far[index]),
-            )
-            args += (scores, far_ids[index])
-            out += (struct((1, rows), jnp.float32),)
-        if has_near:
-            args += (near, near_ids)
-        kept, *back = kernel(
-            functools.partial(meet_kernel, rows, n_plane, has_far, has_near, kept is not None),
+        args += (scores, came_ids[first])
+        for turn in second:
+            args += (came[turn],)
+        kept, back = kernel(
+            functools.partial(meet_kernel, rows, n_plane, len(step), kept is not None),
             "meet",
-            out,
+            (struct((n_plane, rows), jnp.float32), struct((len(step), rows), jnp.float32)),
             args,
         )
-        if has_far:
-            home = [(b, a) for a, b in far_turns[index]]
-            answers.append(lax.ppermute(back[0], "workers", home))
+        if far_turns:
+            if second:
+                even = lax.axis_index("sub") % 2 == 0
+                back = jnp.where(even, back[1:2], back[0:1])
+            home = [(b, a) for a, b in far_turns[number]]
+            answers.append(lax.ppermute(back, "workers", home))
     if kept is None:
         kept = jnp.full((n_plane, rows), -1.0, jnp.float32)
 

time: 36.7 us -> 36 us (0.981)
  Pallas kernels: 6.52 us -> 4.47 us
  local copies, waits for them, and re-layouts: 0.01 us -> 1.05 us
  waiting for transfers between devices: 15.8 us -> 15.2 us
  starting transfers between devices: 12.8 us -> 13.3 us
    pallas_call x4, Pallas kernels: 4.83 us -> 2.95 us  [kernel(): pl.pallas_call(body, out_shape=out_shape, in_specs=[VMEM] * len(args), ou...]
    ppermute x1, waiting for transfers between devices: 12.4 us -> 10.8 us  [gather(): first = lax.ppermute(block, 'team', shift(n_team, dt)) if dt else block]
    unnamed x0 -> x2, local copies, waits for them, and re-layouts: none -> 1.04 us
    ppermute x5 -> x4, waiting for transfers between devices: 1.07 us -> 2.1 us  [the longest x1 1.75 us: on_device(): answers.append(lax.ppermute(back, 'workers', home))]
    ppermute x5 -> x4, starting transfers between devices: 9.46 us -> 10.2 us  [the longest x2 7.12 us: on_device(): lax.ppermute(block if mixed and i == 1 else embeddings, axes, turn)]
  transfers between devices with their start and end apart: 10 -> 9, of which waited for: 4 -> 4; matrix products, arithmetic and copies ran while one was open for 2% -> 3% of each run, Pallas kernels for 15% -> 9%
where the time goes in v5:
time: 36 us; the launch traced here: 35.8 us
  waiting for transfers between devices  15.2 us (42%)
  starting transfers between devices  13.3 us (37%)
  Pallas kernels  4.47 us (12%)
  other arithmetic  1.64 us (5%)
  local copies, waits for them, and re-layouts  1.05 us (3%)
    ppermute x1, waiting for transfers between devices, gather(): first = lax.ppermute(block, 'team', shift(n_team, dt)) if dt else block  10.8 us
    ppermute x2, starting transfers between devices, on_device(): lax.ppermute(block if mixed and i == 1 else embeddings, axes, turn)  7.12 us
    ppermute x1, starting transfers between devices, on_device(): answers.append(lax.ppermute(back, 'workers', home))  3.08 us
    pallas_call x4, Pallas kernels, kernel(): pl.pallas_call(body, out_shape=out_shape, in_specs=[VMEM] * len(args), ou...  2.95 us
    ppermute x2, waiting for transfers between devices, gather(): blocks.append(lax.ppermute(first, 'sub', shift(n_sub, ds)))  2.3 us
    ppermute x1, waiting for transfers between devices, on_device(): answers.append(lax.ppermute(back, 'workers', home))  1.75 us
    ppermute x1, starting transfers between devices, on_device(): ends = jnp.maximum(ends, lax.ppermute(kept[dt], 'team', shift(n_team, -dt)))  1.55 us
    pallas_call x1, Pallas kernels, on_device(): pl.pallas_call(functools.partial(load_kernel, rows), out_shape=(struct((n...  1.53 us
  transfers between devices with their start and end apart: 9, of which 4 were waited for; matrix products, arithmetic and copies ran while one was open for 3% of the time, Pallas kernels for 9%

profile of v5, /device:TPU:0, one launch (start us, length us, event | category | flops | bytes accessed | tf_op | source)
XLA Modules:
  0.0 35.8 jit_solution(9983764891803303408)
XLA Ops:
  0.0 3.0 %collective-permute-start.3 = (bf16[256,1024]{1,0:T(8,128)(2,1)}, bf16[256,1024]{1,0:T(8,128)(2,1)S(1)}, u32[]{:S(2)}, u32[]{:S(2)}) collective-permute-start(bf16[256,1024]{1,0:T(8,128)(2,1)} %raw.1), channel_id=1, source_target_pairs={{4,0},{12,8},{0,4},{8,12},{9,1},{5,9},{13,5},{1,13},{6,2},{14,10},... | collective-permute-start | bytes 1572872 | tf_op jit(solution)/shard_map/ppermute | solution.py:189
  3.0 0.7 %pad_add_fusion.ids = s32[3,256]{1,0:T(4,128)S(1)} fusion(s32[1,256]{1,0:T(1,128)} %bitcast.4, s32[1,256]{1,0:T(1,128)} %bitcast.5, s32[1,256]{1,0:T(1,128)} %bitcast.6), kind=kLoop, calls=%fused_computation.4 | loop fusion | flops 1536 | bytes 6144 | tf_op jit(solution)/shard_map/concatenate | solution.py:183
  3.7 0.0 collective-permute-start.4
  3.7 0.0 copy-start
  3.8 1.0 %copy-done = bf16[256,1024]{1,0:T(8,128)(2,1)S(1)} copy-done((bf16[256,1024]{1,0:T(8,128)(2,1)S(1)}, bf16[256,1024]{1,0:T(8,128)(2,1)}, u32[]{:S(2)}) %copy-start) | copy-done | bytes 524312
  4.8 0.2 pack.1.refs_0_
  5.0 4.1 %collective-permute-start.5 = (bf16[272,1024]{1,0:T(8,128)(2,1)S(1)}, bf16[272,1024]{1,0:T(8,128)(2,1)S(1)}, u32[]{:S(2)}, u32[]{:S(2)}) collective-permute-start(bf16[272,1024]{1,0:T(8,128)(2,1)S(1)} %pack.1.refs_0_), channel_id=1, source_target_pairs={{8,0},{4,8},{12,4},{0,12},{5,1},{13,9},{1,5},{9,13},{10,2},{6,10},... | collective-permute-start | bytes 1671176 | tf_op jit(solution)/shard_map/ppermute | solution.py:189
  9.1 14.6 %conditional.1 = (bf16[272,1024]{1,0:T(8,128)(2,1)}, bf16[272,1024]{1,0:T(8,128)(2,1)}, bf16[272,1024]{1,0:T(8,128)(2,1)}) conditional(s32[]{:T(128)} %convert_element_type.9, () %tuple.13, bf16[272,1024]{1,0:T(8,128)(2,1)S(1)} %pack.1.refs_0_), branch_computations={%region_0.0_spmd, %region_1.0_spmd} | conditional | bytes 6684816 | solution.py:205
  9.1 1.5 %collective-permute-start.1 = (bf16[272,1024]{1,0:T(8,128)(2,1)S(1)}, bf16[272,1024]{1,0:T(8,128)(2,1)}, u32[]{:S(2)}, u32[]{:S(2)}) collective-permute-start(bf16[272,1024]{1,0:T(8,128)(2,1)S(1)} %param.1), channel_id=1, source_target_pairs={{0,2},{2,0},{1,3},{3,1},{4,6},{6,4},{5,7},{7,5},{8,10},{10,8},{9,1... | collective-permute-start | bytes 1671176 | tf_op jit(solution)/shard_map/cond/branch_1_fun/ppermute | solution.py:199
  10.6 0.0 collective-permute-start
  10.6 10.8 %collective-permute-done.1 = bf16[272,1024]{1,0:T(8,128)(2,1)} collective-permute-done((bf16[272,1024]{1,0:T(8,128)(2,1)S(1)}, bf16[272,1024]{1,0:T(8,128)(2,1)}, u32[]{:S(2)}, u32[]{:S(2)}) %collective-permute-start.1) | collective-permute-done | bytes 557088 | tf_op jit(solution)/shard_map/cond/branch_1_fun/ppermute | solution.py:199
  21.4 0.0 collective-permute-start.2
  21.4 0.0 collective-permute-done
  21.4 2.3 %collective-permute-done.2 = bf16[272,1024]{1,0:T(8,128)(2,1)} collective-permute-done((bf16[272,1024]{1,0:T(8,128)(2,1)}, bf16[272,1024]{1,0:T(8,128)(2,1)}, u32[]{:S(2)}, u32[]{:S(2)}) %collective-permute-start.2) | collective-permute-done | bytes 557088 | tf_op jit(solution)/shard_map/cond/branch_1_fun/ppermute | solution.py:202
  23.7 1.5 %load.1 = (bf16[1024,1024]{1,0:T(8,128)(2,1)S(1)}, s32[4,256]{1,0:T(4,128)S(1)}) custom-call(bf16[272,1024]{1,0:T(8,128)(2,1)S(1)} %pack.1.refs_0_, bf16[272,1024]{1,0:T(8,128)(2,1)} %get-tuple-element.13.refs_1_, bf16[272,1024]{1,0:T(8,128)(2,1)} %get-tuple-element.14.refs_2_, bf16[272,1024]{1,0:T(8,128)(2,1)} %get-tuple-element.15.refs_3_), custom_call_target="tpu_custom_call" | custom-call | tf_op jit(solution)/shard_map/load/pallas_call | solution.py:211
  25.2 0.0 collective-permute-done.3
  25.2 0.2 fusion
  25.4 0.2 fusion.1.came
  25.6 0.7 %score.1.refs_2_ = f32[256,1024]{1,0:T(8,128)S(1)} custom-call(bf16[1024,1024]{1,0:T(8,128)(2,1)S(1)} %get-tuple-element.16.plane.refs_0_, bf16[256,1024]{1,0:T(8,128)(2,1)S(1)} %fusion.1.came), custom_call_target="tpu_custom_call" | custom-call | tf_op jit(solution)/shard_map/score/pallas_call | solution.py:135
  26.4 0.0 collective-permute-done.4.refs_3_
  26.4 0.3 collective-permute-done.5.refs_4_
  26.7 1.1 %meet.1 = (f32[4,256]{1,0:T(4,128)S(1)}, f32[2,256]{1,0:T(2,128)S(1)}) custom-call(bf16[1024,1024]{1,0:T(8,128)(2,1)S(1)} %get-tuple-element.16.plane.refs_0_, s32[4,256]{1,0:T(4,128)S(1)} %get-tuple-element.17.refs_1_.codes, f32[256,1024]{1,0:T(8,128)S(1)} %score.1.refs_2_, s32[3,256]{1,0:T(4,128)S(1)} %collective-permute-done.4.refs_3_, ...), custom_call_target="tpu_custom_call" | custom-call | tf_op jit(solution)/shard_map/meet/pallas_call | solution.py:135
  27.8 1.6 %collective-permute-start.6 = (f32[2,256]{1,0:T(2,128)S(1)}, f32[2,256]{1,0:T(2,128)S(1)}, u32[]{:S(2)}, u32[]{:S(2)}) collective-permute-start(f32[2,256]{1,0:T(2,128)S(1)} %slice.21), channel_id=1, source_target_pairs={{0,2},{2,0},{1,3},{3,1},{4,6},{6,4},{5,7},{7,5},{8,10},{10,8},{9,1... | collective-permute-start | bytes 6152 | tf_op jit(solution)/shard_map/ppermute | solution.py:263
  29.4 3.1 %collective-permute-start.8 = (f32[1,256]{1,0:T(1,128)S(1)}, f32[1,256]{1,0:T(1,128)S(1)}, u32[]{:S(2)}, u32[]{:S(2)}) collective-permute-start(f32[1,256]{1,0:T(1,128)S(1)} %broadcast_select_fusion), channel_id=1, source_target_pairs={{0,8},{8,4},{4,12},{12,0},{1,9},{9,5},{5,13},{13,1},{2,10},{10,6},... | collective-permute-start | bytes 3080 | tf_op jit(solution)/shard_map/ppermute | solution.py:256
  32.5 0.0 collective-permute-done.6
  32.5 0.1 collective-permute-start.7
  32.6 0.9 %own.1 = f32[1,256]{1,0:T(1,128)S(1)} custom-call(bf16[1024,1024]{1,0:T(8,128)(2,1)S(1)} %get-tuple-element.16.plane.refs_0_, s32[4,256]{1,0:T(4,128)S(1)} %get-tuple-element.17.refs_1_.codes), custom_call_target="tpu_custom_call" | custom-call | tf_op jit(solution)/shard_map/own/pallas_call | solution.py:135
  33.5 1.8 %collective-permute-done.8 = f32[1,256]{1,0:T(1,128)S(1)} collective-permute-done((f32[1,256]{1,0:T(1,128)S(1)}, f32[1,256]{1,0:T(1,128)S(1)}, u32[]{:S(2)}, u32[]{:S(2)}) %collective-permute-start.8) | collective-permute-done | bytes 1056 | tf_op jit(solution)/shard_map/ppermute | solution.py:256
  35.2 0.0 collective-permute-done.7
  35.2 0.6 %fusion.3 = f32[1,256]{1,0:T(1,128)} fusion(f32[1,256]{1,0:T(1,128)S(1)} %collective-permute-done.8, f32[1,256]{1,0:T(1,128)S(1)} %own.1, f32[1,256]{1,0:T(1,128)S(1)} %collective-permute-done.7, f32[2,256]{1,0:T(2,128)S(1)} %slice_maximum_fusion), kind=kLoop, calls=%fused_computation.9 | loop fusion | flops 768 | bytes 5120 | tf_op jit(solution)/shard_map/max | solution.py:269
  (5 shorter events, 0.0 us)
Async XLA Ops:
  0.0 25.2 %collective-permute-start.3 = (bf16[256,1024]{1,0:T(8,128)(2,1)}, bf16[256,1024]{1,0:T(8,128)(2,1)S(1)}, u32[]{:S(2)}, u32[]{:S(2)}) collective-permute-start(bf16[256,1024]{1,0:T(8,128)(2,1)} %raw.1), channel_id=1, source_target_pairs={{4,0},{12,8},{0,4},{8,12},{9,1},{5,9},{13,5},{1,13},{6,2},{14,10},... | collective-permute-start | bytes 1572872 | tf_op jit(solution)/shard_map/ppermute | solution.py:189
  3.7 22.6 %collective-permute-start.4 = (s32[3,256]{1,0:T(4,128)S(1)}, s32[3,256]{1,0:T(4,128)S(1)}, u32[]{:S(2)}, u32[]{:S(2)}) collective-permute-start(s32[3,256]{1,0:T(4,128)S(1)} %pad_add_fusion.ids), channel_id=1, source_target_pairs={{4,0},{12,8},{0,4},{8,12},{9,1},{5,9},{13,5},{1,13},{6,2},{14,10},... | collective-permute-start | bytes 9224 | tf_op jit(solution)/shard_map/ppermute | solution.py:193
  3.7 1.0 %copy-start = (bf16[256,1024]{1,0:T(8,128)(2,1)S(1)}, bf16[256,1024]{1,0:T(8,128)(2,1)}, u32[]{:S(2)}) copy-start(bf16[256,1024]{1,0:T(8,128)(2,1)} %raw.1) | copy-start | bytes 1572868
  5.0 21.7 %collective-permute-start.5 = (bf16[272,1024]{1,0:T(8,128)(2,1)S(1)}, bf16[272,1024]{1,0:T(8,128)(2,1)S(1)}, u32[]{:S(2)}, u32[]{:S(2)}) collective-permute-start(bf16[272,1024]{1,0:T(8,128)(2,1)S(1)} %pack.1.refs_0_), channel_id=1, source_target_pairs={{8,0},{4,8},{12,4},{0,12},{5,1},{13,9},{1,5},{9,13},{10,2},{6,10},... | collective-permute-start | bytes 1671176 | tf_op jit(solution)/shard_map/ppermute | solution.py:189
  9.1 12.3 %collective-permute-start.1 = (bf16[272,1024]{1,0:T(8,128)(2,1)S(1)}, bf16[272,1024]{1,0:T(8,128)(2,1)}, u32[]{:S(2)}, u32[]{:S(2)}) collective-permute-start(bf16[272,1024]{1,0:T(8,128)(2,1)S(1)} %param.1), channel_id=1, source_target_pairs={{0,2},{2,0},{1,3},{3,1},{4,6},{6,4},{5,7},{7,5},{8,10},{10,8},{9,1... | collective-permute-start | bytes 1671176 | tf_op jit(solution)/shard_map/cond/branch_1_fun/ppermute | solution.py:199
  10.6 10.8 %collective-permute-start = (bf16[272,1024]{1,0:T(8,128)(2,1)S(1)}, bf16[272,1024]{1,0:T(8,128)(2,1)}, u32[]{:S(2)}, u32[]{:S(2)}) collective-permute-start(bf16[272,1024]{1,0:T(8,128)(2,1)S(1)} %param.1), channel_id=1, source_target_pairs={{0,1},{1,0},{2,3},{3,2},{4,5},{5,4},{6,7},{7,6},{8,9},{9,8},{10,11... | collective-permute-start | bytes 1671176 | tf_op jit(solution)/shard_map/cond/branch_1_fun/ppermute | solution.py:202
  21.4 2.3 %collective-permute-start.2 = (bf16[272,1024]{1,0:T(8,128)(2,1)}, bf16[272,1024]{1,0:T(8,128)(2,1)}, u32[]{:S(2)}, u32[]{:S(2)}) collective-permute-start(bf16[272,1024]{1,0:T(8,128)(2,1)} %collective-permute-done.1), channel_id=1, source_target_pairs={{0,1},{1,0},{2,3},{3,2},{4,5},{5,4},{6,7},{7,6},{8,9},{9,8},{10,11... | collective-permute-start | bytes 1671176 | tf_op jit(solution)/shard_map/cond/branch_1_fun/ppermute | solution.py:202
  27.8 4.6 %collective-permute-start.6 = (f32[2,256]{1,0:T(2,128)S(1)}, f32[2,256]{1,0:T(2,128)S(1)}, u32[]{:S(2)}, u32[]{:S(2)}) collective-permute-start(f32[2,256]{1,0:T(2,128)S(1)} %slice.21), channel_id=1, source_target_pairs={{0,2},{2,0},{1,3},{3,1},{4,6},{6,4},{5,7},{7,5},{8,10},{10,8},{9,1... | collective-permute-start | bytes 6152 | tf_op jit(solution)/shard_map/ppermute | solution.py:263
  29.4 5.8 %collective-permute-start.8 = (f32[1,256]{1,0:T(1,128)S(1)}, f32[1,256]{1,0:T(1,128)S(1)}, u32[]{:S(2)}, u32[]{:S(2)}) collective-permute-start(f32[1,256]{1,0:T(1,128)S(1)} %broadcast_select_fusion), channel_id=1, source_target_pairs={{0,8},{8,4},{4,12},{12,0},{1,9},{9,5},{5,13},{13,1},{2,10},{10,6},... | collective-permute-start | bytes 3080 | tf_op jit(solution)/shard_map/ppermute | solution.py:256
  32.5 2.7 %collective-permute-start.7 = (f32[1,256]{1,0:T(1,128)S(1)}, f32[1,256]{1,0:T(1,128)S(1)}, u32[]{:S(2)}, u32[]{:S(2)}) collective-permute-start(f32[1,256]{1,0:T(1,128)S(1)} %slice.27), channel_id=1, source_target_pairs={{0,1},{1,0},{2,3},{3,2},{4,5},{5,4},{6,7},{7,6},{8,9},{9,8},{10,11... | collective-permute-start | bytes 3080 | tf_op jit(solution)/shard_map/ppermute | solution.py:266

commit v6 on v5

--- a/solution.py
+++ b/solution.py
@@ -8,7 +8,7 @@
 from jax.sharding import PartitionSpec as P
 
 KC = 16
-EXTRA = 16
+EXTRA = 8
 VMEM = pl.BlockSpec(memory_space=pltpu.VMEM)
 HBM = pl.BlockSpec(memory_space=pl.ANY)
 
@@ -55,34 +55,27 @@
     line = jnp.concatenate(line, axis=1).astype(jnp.float32)
     first = lax.broadcasted_iota(jnp.int32, (EXTRA, width), 0) == 0
     last = jnp.where(first, jnp.broadcast_to(line, (EXTRA, width)), 0.0)
-    block[0:rows, :] = normalise(raw[...])
-    block[rows : rows + EXTRA, :] = last.astype(jnp.bfloat16)
+    block[...] = jnp.concatenate([normalise(raw[...]), last.astype(jnp.bfloat16)], axis=0)
 
 
 def load_kernel(rows, *refs):
-    *blocks, plane, codes, lasts, sems = refs
+    *blocks, plane, codes, sems = refs
     copies = [
-        pltpu.make_async_copy(b.at[rows : rows + EXTRA, :], lasts.at[i], sems.at[0, i])
-        for i, b in enumerate(blocks)
-    ] + [
-        pltpu.make_async_copy(
-            b.at[0:rows, :], plane.at[i * rows : (i + 1) * rows, :], sems.at[1, i]
-        )
-        for i, b in enumerate(blocks)
+        pltpu.make_async_copy(block, plane.at[i], sems.at[i]) for i, block in enumerate(blocks)
     ]
     for copy in copies:
         copy.start()
     for copy in copies:
         copy.wait()
     for i in range(len(blocks)):
-        codes[i : i + 1, :] = code_of_last(lasts[i], rows)
+        codes[i : i + 1, :] = code_of_last(plane[i][rows : rows + EXTRA, :], rows)
 
 
 def own_kernel(rows, n_plane, plane, codes, best):
-    mine, column = plane[0:rows, :], as_column(codes[0:1, :])
+    mine, column = plane[0, 0:rows, :], as_column(codes[0:1, :])
     found = jnp.full((rows, 128), -1.0, jnp.float32)
     for index in range(n_plane):
-        scores = scores_of(mine, plane[index * rows : (index + 1) * rows, :])
+        scores = scores_of(mine, plane[index, 0:rows, :])
         for at in range(0, rows, 128):
             other = codes[index : index + 1, at : at + 128]
             earlier = ((column ^ other) < 65536) & (column > other)
@@ -94,7 +87,7 @@
     came_rows = came[...]
     for index in range(n_plane):
         lanes = slice(index * rows, (index + 1) * rows)
-        scores[:, lanes] = scores_of(came_rows, plane[lanes, :])
+        scores[:, lanes] = scores_of(came_rows, plane[index, 0:rows, :])
 
 
 def meet_kernel(rows, n_plane, n_came, has_part, *refs):
@@ -105,14 +98,14 @@
     if n_came == 2:
         packed = refs.pop(0)
         came_rows = packed[0:rows, :]
-        columns.append(as_column(code_of_last(packed[rows : rows + EXTRA, :], rows)))
+        columns.append(as_column(code_of_last(packed[...][rows : rows + EXTRA, :], rows)))
     kept, back = refs
     found = [jnp.full((rows, 128), -1.0, jnp.float32)] * n_came
     for index in range(n_plane):
         block = slice(index * rows, (index + 1) * rows)
         tables = [scores[:, block]]
         if n_came == 2:
-            tables.append(scores_of(came_rows, plane[block, :]))
+            tables.append(scores_of(came_rows, plane[index, 0:rows, :]))
         for at in range(0, rows, 128):
             lanes = slice(at, at + 128)
             other = codes[index : index + 1, lanes]
@@ -210,13 +203,13 @@
     blocks = (block, *blocks)
     plane, codes = pl.pallas_call(
         functools.partial(load_kernel, rows),
-        out_shape=(struct((n_plane * rows, width), jnp.bfloat16), struct((n_plane, rows), jnp.int32)),
+        out_shape=(
+            struct((n_plane, rows + EXTRA, width), jnp.bfloat16),
+            struct((n_plane, rows), jnp.int32),
+        ),
         in_specs=[HBM] * n_plane,
         out_specs=(VMEM, VMEM),
-        scratch_shapes=[
-            pltpu.VMEM((n_plane, EXTRA, width), jnp.bfloat16),
-            pltpu.SemaphoreType.DMA((2, n_plane)),
-        ],
+        scratch_shapes=[pltpu.SemaphoreType.DMA((n_plane,))],
         compiler_params=pltpu.CompilerParams(vmem_limit_bytes=40 * 1024 * 1024),
         name="load",
     )(*blocks)

time: 36 us -> 35.7 us (level)
  no operation moved by 1% of the time
where the time goes in v6:
time: 35.7 us; the launch traced here: 35.5 us
  waiting for transfers between devices  14.9 us (42%)
  starting transfers between devices  13.3 us (37%)
  Pallas kernels  4.44 us (12%)
  other arithmetic  1.64 us (5%)
  local copies, waits for them, and re-layouts  1.05 us (3%)
    ppermute x1, waiting for transfers between devices, gather(): first = lax.ppermute(block, 'team', shift(n_team, dt)) if dt else block  10.5 us
    ppermute x2, starting transfers between devices, on_device(): lax.ppermute(block if mixed and i == 1 else embeddings, axes, turn)  7.12 us
    ppermute x1, starting transfers between devices, on_device(): answers.append(lax.ppermute(back, 'workers', home))  3.08 us
    pallas_call x4, Pallas kernels, kernel(): pl.pallas_call(body, out_shape=out_shape, in_specs=[VMEM] * len(args), ou...  2.95 us
    ppermute x2, waiting for transfers between devices, gather(): blocks.append(lax.ppermute(first, 'sub', shift(n_sub, ds)))  2.27 us
    ppermute x1, waiting for transfers between devices, on_device(): answers.append(lax.ppermute(back, 'workers', home))  1.75 us
    ppermute x1, starting transfers between devices, on_device(): ends = jnp.maximum(ends, lax.ppermute(kept[dt], 'team', shift(n_team, -dt)))  1.55 us
    ppermute x1, starting transfers between devices, gather(): first = lax.ppermute(block, 'team', shift(n_team, dt)) if dt else block  1.49 us
  transfers between devices with their start and end apart: 9, of which 4 were waited for; matrix products, arithmetic and copies ran while one was open for 3% of the time, Pallas kernels for 9%

profile of v6, /device:TPU:0, one launch (start us, length us, event | category | flops | bytes accessed | tf_op | source)
XLA Modules:
  0.0 35.5 jit_solution(2633920153365867675)
XLA Ops:
  0.0 3.0 %collective-permute-start.3 = (bf16[256,1024]{1,0:T(8,128)(2,1)}, bf16[256,1024]{1,0:T(8,128)(2,1)S(1)}, u32[]{:S(2)}, u32[]{:S(2)}) collective-permute-start(bf16[256,1024]{1,0:T(8,128)(2,1)} %raw.1), channel_id=1, source_target_pairs={{4,0},{12,8},{0,4},{8,12},{9,1},{5,9},{13,5},{1,13},{6,2},{14,10},... | collective-permute-start | bytes 1572872 | tf_op jit(solution)/shard_map/ppermute | solution.py:182
  3.0 0.7 %pad_add_fusion.ids = s32[3,256]{1,0:T(4,128)S(1)} fusion(s32[1,256]{1,0:T(1,128)} %bitcast.4, s32[1,256]{1,0:T(1,128)} %bitcast.5, s32[1,256]{1,0:T(1,128)} %bitcast.6), kind=kLoop, calls=%fused_computation.4 | loop fusion | flops 1536 | bytes 6144 | tf_op jit(solution)/shard_map/concatenate | solution.py:176
  3.7 0.0 collective-permute-start.4
  3.7 0.0 copy-start
  3.8 1.0 %copy-done = bf16[256,1024]{1,0:T(8,128)(2,1)S(1)} copy-done((bf16[256,1024]{1,0:T(8,128)(2,1)S(1)}, bf16[256,1024]{1,0:T(8,128)(2,1)}, u32[]{:S(2)}) %copy-start) | copy-done | bytes 524312
  4.8 0.2 pack.1.refs_0_
  5.0 4.1 %collective-permute-start.5 = (bf16[264,1024]{1,0:T(8,128)(2,1)S(1)}, bf16[264,1024]{1,0:T(8,128)(2,1)S(1)}, u32[]{:S(2)}, u32[]{:S(2)}) collective-permute-start(bf16[264,1024]{1,0:T(8,128)(2,1)S(1)} %pack.1.refs_0_), channel_id=1, source_target_pairs={{8,0},{4,8},{12,4},{0,12},{5,1},{13,9},{1,5},{9,13},{10,2},{6,10},... | collective-permute-start | bytes 1622024 | tf_op jit(solution)/shard_map/ppermute | solution.py:182
  9.1 14.2 %conditional.1 = (bf16[264,1024]{1,0:T(8,128)(2,1)}, bf16[264,1024]{1,0:T(8,128)(2,1)}, bf16[264,1024]{1,0:T(8,128)(2,1)}) conditional(s32[]{:T(128)} %convert_element_type.9, () %tuple.13, bf16[264,1024]{1,0:T(8,128)(2,1)S(1)} %pack.1.refs_0_), branch_computations={%region_0.0_spmd, %region_1.0_spmd} | conditional | bytes 6488208 | solution.py:198
  9.1 1.5 %collective-permute-start.1 = (bf16[264,1024]{1,0:T(8,128)(2,1)S(1)}, bf16[264,1024]{1,0:T(8,128)(2,1)}, u32[]{:S(2)}, u32[]{:S(2)}) collective-permute-start(bf16[264,1024]{1,0:T(8,128)(2,1)S(1)} %param.1), channel_id=1, source_target_pairs={{0,2},{2,0},{1,3},{3,1},{4,6},{6,4},{5,7},{7,5},{8,10},{10,8},{9,1... | collective-permute-start | bytes 1622024 | tf_op jit(solution)/shard_map/cond/branch_1_fun/ppermute | solution.py:192
  10.6 0.0 collective-permute-start
  10.6 10.5 %collective-permute-done.1 = bf16[264,1024]{1,0:T(8,128)(2,1)} collective-permute-done((bf16[264,1024]{1,0:T(8,128)(2,1)S(1)}, bf16[264,1024]{1,0:T(8,128)(2,1)}, u32[]{:S(2)}, u32[]{:S(2)}) %collective-permute-start.1) | collective-permute-done | bytes 540704 | tf_op jit(solution)/shard_map/cond/branch_1_fun/ppermute | solution.py:192
  21.1 0.0 collective-permute-start.2
  21.1 0.0 collective-permute-done
  21.1 2.3 %collective-permute-done.2 = bf16[264,1024]{1,0:T(8,128)(2,1)} collective-permute-done((bf16[264,1024]{1,0:T(8,128)(2,1)}, bf16[264,1024]{1,0:T(8,128)(2,1)}, u32[]{:S(2)}, u32[]{:S(2)}) %collective-permute-start.2) | collective-permute-done | bytes 540704 | tf_op jit(solution)/shard_map/cond/branch_1_fun/ppermute | solution.py:195
  23.3 1.5 %load.1 = (bf16[4,264,1024]{2,1,0:T(8,128)(2,1)S(1)}, s32[4,256]{1,0:T(4,128)S(1)}) custom-call(bf16[264,1024]{1,0:T(8,128)(2,1)S(1)} %pack.1.refs_0_, bf16[264,1024]{1,0:T(8,128)(2,1)} %get-tuple-element.13.refs_1_, bf16[264,1024]{1,0:T(8,128)(2,1)} %get-tuple-element.14.refs_2_, bf16[264,1024]{1,0:T(8,128)(2,1)} %get-tuple-element.15.refs_3_), custom_call_target="tpu_custom_call" | custom-call | tf_op jit(solution)/shard_map/load/pallas_call | solution.py:204
  24.8 0.0 collective-permute-done.3
  24.8 0.2 fusion
  25.0 0.2 fusion.1.came
  25.2 0.7 %score.1.refs_2_ = f32[256,1024]{1,0:T(8,128)S(1)} custom-call(bf16[4,264,1024]{2,1,0:T(8,128)(2,1)S(1)} %get-tuple-element.16.plane.refs_0_, bf16[256,1024]{1,0:T(8,128)(2,1)S(1)} %fusion.1.came), custom_call_target="tpu_custom_call" | custom-call | tf_op jit(solution)/shard_map/score/pallas_call | solution.py:128
  25.9 0.0 collective-permute-done.4.refs_3_
  26.0 0.4 %collective-permute-done.5.refs_4_ = bf16[264,1024]{1,0:T(8,128)(2,1)S(1)} collective-permute-done((bf16[264,1024]{1,0:T(8,128)(2,1)S(1)}, bf16[264,1024]{1,0:T(8,128)(2,1)S(1)}, u32[]{:S(2)}, u32[]{:S(2)}) %collective-permute-start.5) | collective-permute-done | bytes 540704 | tf_op jit(solution)/shard_map/ppermute | solution.py:182
  26.3 1.1 %meet.1 = (f32[4,256]{1,0:T(4,128)S(1)}, f32[2,256]{1,0:T(2,128)S(1)}) custom-call(bf16[4,264,1024]{2,1,0:T(8,128)(2,1)S(1)} %get-tuple-element.16.plane.refs_0_, s32[4,256]{1,0:T(4,128)S(1)} %get-tuple-element.17.refs_1_.codes, f32[256,1024]{1,0:T(8,128)S(1)} %score.1.refs_2_, s32[3,256]{1,0:T(4,128)S(1)} %collective-permute-done.4.refs_3_, ...), custom_call_target="tpu_custom_call" | custom-call | tf_op jit(solution)/shard_map/meet/pallas_call | solution.py:128
  27.5 1.6 %collective-permute-start.6 = (f32[2,256]{1,0:T(2,128)S(1)}, f32[2,256]{1,0:T(2,128)S(1)}, u32[]{:S(2)}, u32[]{:S(2)}) collective-permute-start(f32[2,256]{1,0:T(2,128)S(1)} %slice.21), channel_id=1, source_target_pairs={{0,2},{2,0},{1,3},{3,1},{4,6},{6,4},{5,7},{7,5},{8,10},{10,8},{9,1... | collective-permute-start | bytes 6152 | tf_op jit(solution)/shard_map/ppermute | solution.py:256
  29.1 3.1 %collective-permute-start.8 = (f32[1,256]{1,0:T(1,128)S(1)}, f32[1,256]{1,0:T(1,128)S(1)}, u32[]{:S(2)}, u32[]{:S(2)}) collective-permute-start(f32[1,256]{1,0:T(1,128)S(1)} %broadcast_select_fusion), channel_id=1, source_target_pairs={{0,8},{8,4},{4,12},{12,0},{1,9},{9,5},{5,13},{13,1},{2,10},{10,6},... | collective-permute-start | bytes 3080 | tf_op jit(solution)/shard_map/ppermute | solution.py:249
  32.1 0.0 collective-permute-done.6
  32.2 0.1 collective-permute-start.7
  32.2 0.9 %own.1 = f32[1,256]{1,0:T(1,128)S(1)} custom-call(bf16[4,264,1024]{2,1,0:T(8,128)(2,1)S(1)} %get-tuple-element.16.plane.refs_0_, s32[4,256]{1,0:T(4,128)S(1)} %get-tuple-element.17.refs_1_.codes), custom_call_target="tpu_custom_call" | custom-call | tf_op jit(solution)/shard_map/own/pallas_call | solution.py:128
  33.1 1.8 %collective-permute-done.8 = f32[1,256]{1,0:T(1,128)S(1)} collective-permute-done((f32[1,256]{1,0:T(1,128)S(1)}, f32[1,256]{1,0:T(1,128)S(1)}, u32[]{:S(2)}, u32[]{:S(2)}) %collective-permute-start.8) | collective-permute-done | bytes 1056 | tf_op jit(solution)/shard_map/ppermute | solution.py:249
  34.9 0.0 collective-permute-done.7
  34.9 0.6 %fusion.3 = f32[1,256]{1,0:T(1,128)} fusion(f32[1,256]{1,0:T(1,128)S(1)} %collective-permute-done.8, f32[1,256]{1,0:T(1,128)S(1)} %own.1, f32[1,256]{1,0:T(1,128)S(1)} %collective-permute-done.7, f32[2,256]{1,0:T(2,128)S(1)} %slice_maximum_fusion), kind=kLoop, calls=%fused_computation.9 | loop fusion | flops 768 | bytes 5120 | tf_op jit(solution)/shard_map/max | solution.py:262
  (5 shorter events, 0.0 us)
Async XLA Ops:
  0.0 24.8 %collective-permute-start.3 = (bf16[256,1024]{1,0:T(8,128)(2,1)}, bf16[256,1024]{1,0:T(8,128)(2,1)S(1)}, u32[]{:S(2)}, u32[]{:S(2)}) collective-permute-start(bf16[256,1024]{1,0:T(8,128)(2,1)} %raw.1), channel_id=1, source_target_pairs={{4,0},{12,8},{0,4},{8,12},{9,1},{5,9},{13,5},{1,13},{6,2},{14,10},... | collective-permute-start | bytes 1572872 | tf_op jit(solution)/shard_map/ppermute | solution.py:182
  3.7 22.2 %collective-permute-start.4 = (s32[3,256]{1,0:T(4,128)S(1)}, s32[3,256]{1,0:T(4,128)S(1)}, u32[]{:S(2)}, u32[]{:S(2)}) collective-permute-start(s32[3,256]{1,0:T(4,128)S(1)} %pad_add_fusion.ids), channel_id=1, source_target_pairs={{4,0},{12,8},{0,4},{8,12},{9,1},{5,9},{13,5},{1,13},{6,2},{14,10},... | collective-permute-start | bytes 9224 | tf_op jit(solution)/shard_map/ppermute | solution.py:186
  3.7 1.0 %copy-start = (bf16[256,1024]{1,0:T(8,128)(2,1)S(1)}, bf16[256,1024]{1,0:T(8,128)(2,1)}, u32[]{:S(2)}) copy-start(bf16[256,1024]{1,0:T(8,128)(2,1)} %raw.1) | copy-start | bytes 1572868
  5.0 21.4 %collective-permute-start.5 = (bf16[264,1024]{1,0:T(8,128)(2,1)S(1)}, bf16[264,1024]{1,0:T(8,128)(2,1)S(1)}, u32[]{:S(2)}, u32[]{:S(2)}) collective-permute-start(bf16[264,1024]{1,0:T(8,128)(2,1)S(1)} %pack.1.refs_0_), channel_id=1, source_target_pairs={{8,0},{4,8},{12,4},{0,12},{5,1},{13,9},{1,5},{9,13},{10,2},{6,10},... | collective-permute-start | bytes 1622024 | tf_op jit(solution)/shard_map/ppermute | solution.py:182
  9.1 12.0 %collective-permute-start.1 = (bf16[264,1024]{1,0:T(8,128)(2,1)S(1)}, bf16[264,1024]{1,0:T(8,128)(2,1)}, u32[]{:S(2)}, u32[]{:S(2)}) collective-permute-start(bf16[264,1024]{1,0:T(8,128)(2,1)S(1)} %param.1), channel_id=1, source_target_pairs={{0,2},{2,0},{1,3},{3,1},{4,6},{6,4},{5,7},{7,5},{8,10},{10,8},{9,1... | collective-permute-start | bytes 1622024 | tf_op jit(solution)/shard_map/cond/branch_1_fun/ppermute | solution.py:192
  10.6 10.5 %collective-permute-start = (bf16[264,1024]{1,0:T(8,128)(2,1)S(1)}, bf16[264,1024]{1,0:T(8,128)(2,1)}, u32[]{:S(2)}, u32[]{:S(2)}) collective-permute-start(bf16[264,1024]{1,0:T(8,128)(2,1)S(1)} %param.1), channel_id=1, source_target_pairs={{0,1},{1,0},{2,3},{3,2},{4,5},{5,4},{6,7},{7,6},{8,9},{9,8},{10,11... | collective-permute-start | bytes 1622024 | tf_op jit(solution)/shard_map/cond/branch_1_fun/ppermute | solution.py:195
  21.1 2.3 %collective-permute-start.2 = (bf16[264,1024]{1,0:T(8,128)(2,1)}, bf16[264,1024]{1,0:T(8,128)(2,1)}, u32[]{:S(2)}, u32[]{:S(2)}) collective-permute-start(bf16[264,1024]{1,0:T(8,128)(2,1)} %collective-permute-done.1), channel_id=1, source_target_pairs={{0,1},{1,0},{2,3},{3,2},{4,5},{5,4},{6,7},{7,6},{8,9},{9,8},{10,11... | collective-permute-start | bytes 1622024 | tf_op jit(solution)/shard_map/cond/branch_1_fun/ppermute | solution.py:195
  27.5 4.6 %collective-permute-start.6 = (f32[2,256]{1,0:T(2,128)S(1)}, f32[2,256]{1,0:T(2,128)S(1)}, u32[]{:S(2)}, u32[]{:S(2)}) collective-permute-start(f32[2,256]{1,0:T(2,128)S(1)} %slice.21), channel_id=1, source_target_pairs={{0,2},{2,0},{1,3},{3,1},{4,6},{6,4},{5,7},{7,5},{8,10},{10,8},{9,1... | collective-permute-start | bytes 6152 | tf_op jit(solution)/shard_map/ppermute | solution.py:256
  29.1 5.8 %collective-permute-start.8 = (f32[1,256]{1,0:T(1,128)S(1)}, f32[1,256]{1,0:T(1,128)S(1)}, u32[]{:S(2)}, u32[]{:S(2)}) collective-permute-start(f32[1,256]{1,0:T(1,128)S(1)} %broadcast_select_fusion), channel_id=1, source_target_pairs={{0,8},{8,4},{4,12},{12,0},{1,9},{9,5},{5,13},{13,1},{2,10},{10,6},... | collective-permute-start | bytes 3080 | tf_op jit(solution)/shard_map/ppermute | solution.py:249
  32.2 2.7 %collective-permute-start.7 = (f32[1,256]{1,0:T(1,128)S(1)}, f32[1,256]{1,0:T(1,128)S(1)}, u32[]{:S(2)}, u32[]{:S(2)}) collective-permute-start(f32[1,256]{1,0:T(1,128)S(1)} %slice.27), channel_id=1, source_target_pairs={{0,1},{1,0},{2,3},{3,2},{4,5},{5,4},{6,7},{7,6},{8,9},{9,8},{10,11... | collective-permute-start | bytes 3080 | tf_op jit(solution)/shard_map/ppermute | solution.py:259

commit v7 on v6

--- a/solution.py
+++ b/solution.py
@@ -90,7 +90,7 @@
         scores[:, lanes] = scores_of(came_rows, plane[index, 0:rows, :])
 
 
-def meet_kernel(rows, n_plane, n_came, has_part, *refs):
+def meet_kernel(rows, places, n_came, has_part, *refs):
     plane, codes, *refs = refs
     part = refs.pop(0) if has_part else None
     scores, *refs = refs
@@ -101,7 +101,7 @@
         columns.append(as_column(code_of_last(packed[...][rows : rows + EXTRA, :], rows)))
     kept, back = refs
     found = [jnp.full((rows, 128), -1.0, jnp.float32)] * n_came
-    for index in range(n_plane):
+    for index, place in enumerate(places):
         block = slice(index * rows, (index + 1) * rows)
         tables = [scores[:, block]]
         if n_came == 2:
@@ -118,8 +118,8 @@
                 keep = kept_here if keep is None else jnp.maximum(keep, kept_here)
             keep = jnp.max(keep, axis=0, keepdims=True)
             if has_part:
-                keep = jnp.maximum(keep, part[index : index + 1, lanes])
-            kept[index : index + 1, lanes] = keep
+                keep = jnp.maximum(keep, part[place : place + 1, lanes])
+            kept[place : place + 1, lanes] = keep
     for turn in range(n_came):
         back[turn : turn + 1, :] = fold_rows(found[turn])
 
@@ -219,6 +219,7 @@
         (struct((1, rows), jnp.float32),),
         (plane, codes),
     )
+    places = [ds * n_team + dt for dt in range(n_team) for ds in range(n_sub)]
     kept, answers = None, []
     steps = [[i] for i in range(len(turns))]
     if mixed:
@@ -236,7 +237,7 @@
         for turn in second:
             args += (came[turn],)
         kept, back = kernel(
-            functools.partial(meet_kernel, rows, n_plane, len(step), kept is not None),
+            functools.partial(meet_kernel, rows, places, len(step), kept is not None),
             "meet",
             (struct((n_plane, rows), jnp.float32), struct((len(step), rows), jnp.float32)),
             args,
@@ -250,13 +251,13 @@
     if kept is None:
         kept = jnp.full((n_plane, rows), -1.0, jnp.float32)
 
-    kept = kept.reshape(n_team, n_sub, rows)
+    kept = kept.reshape(n_sub, n_team, rows)
     ends = kept[0]
+    for ds in range(1, n_sub):
+        ends = jnp.maximum(ends, lax.ppermute(kept[ds], "sub", shift(n_sub, -ds)))
+    best = ends[0:1]
     for dt in range(1, n_team):
-        ends = jnp.maximum(ends, lax.ppermute(kept[dt], "team", shift(n_team, -dt)))
-    best = ends[0:1]
-    for ds in range(1, n_sub):
-        best = jnp.maximum(best, lax.ppermute(ends[ds : ds + 1], "sub", shift(n_sub, -ds)))
+        best = jnp.maximum(best, lax.ppermute(ends[dt : dt + 1], "team", shift(n_team, -dt)))
     best = jnp.maximum(best, own)
     for answer in answers:
         best = jnp.maximum(best, answer)

time: 35.7 us -> 35.6 us (level)
  waiting for transfers between devices: 14.9 us -> 14.3 us
  starting transfers between devices: 13.3 us -> 13.8 us
    ppermute x2, starting transfers between devices: 1.62 us -> 2.78 us  [the longest x1 1.56 us: on_device(): lax.ppermute(ends[dt:dt + 1], 'team', shift(n_team, -dt))]
    ppermute x1, waiting for transfers between devices: 1.75 us -> 0.7 us  [on_device(): answers.append(lax.ppermute(back, 'workers', home))]
    ppermute x1, starting transfers between devices: 3.08 us -> 2.43 us  [on_device(): answers.append(lax.ppermute(back, 'workers', home))]
    ppermute x2, waiting for transfers between devices: 0.01 us -> 0.48 us  [the longest x1 0.47 us: on_device(): lax.ppermute(ends[dt:dt + 1], 'team', shift(n_team, -dt))]
  transfers between devices with their start and end apart: 9 -> 9, of which waited for: 4 -> 5; matrix products, arithmetic and copies ran while one was open for 3% -> 3% of each run, Pallas kernels for 9% -> 9%
where the time goes in v7:
time: 35.6 us; the launch traced here: 35.4 us
  waiting for transfers between devices  14.3 us (40%)
  starting transfers between devices  13.8 us (39%)
  Pallas kernels  4.44 us (12%)
  other arithmetic  1.64 us (5%)
  local copies, waits for them, and re-layouts  1.05 us (3%)
    ppermute x1, waiting for transfers between devices, gather(): first = lax.ppermute(block, 'team', shift(n_team, dt)) if dt else block  10.5 us
    ppermute x2, starting transfers between devices, on_device(): lax.ppermute(block if mixed and i == 1 else embeddings, axes, turn)  7.12 us
    pallas_call x4, Pallas kernels, kernel(): pl.pallas_call(body, out_shape=out_shape, in_specs=[VMEM] * len(args), ou...  2.95 us
    ppermute x1, starting transfers between devices, on_device(): answers.append(lax.ppermute(back, 'workers', home))  2.43 us
    ppermute x2, waiting for transfers between devices, gather(): blocks.append(lax.ppermute(first, 'sub', shift(n_sub, ds)))  2.27 us
    ppermute x1, starting transfers between devices, on_device(): lax.ppermute(ends[dt:dt + 1], 'team', shift(n_team, -dt))  1.56 us
    ppermute x1, starting transfers between devices, gather(): first = lax.ppermute(block, 'team', shift(n_team, dt)) if dt else block  1.49 us
    pallas_call x1, Pallas kernels, on_device(): pl.pallas_call(functools.partial(load_kernel, rows), out_shape=(struct((n...  1.49 us
  transfers between devices with their start and end apart: 9, of which 5 were waited for; matrix products, arithmetic and copies ran while one was open for 3% of the time, Pallas kernels for 9%

profile of v7, /device:TPU:0, one launch (start us, length us, event | category | flops | bytes accessed | tf_op | source)
XLA Modules:
  0.0 35.4 jit_solution(8589850869401066178)
XLA Ops:
  0.0 3.0 %collective-permute-start.3 = (bf16[256,1024]{1,0:T(8,128)(2,1)}, bf16[256,1024]{1,0:T(8,128)(2,1)S(1)}, u32[]{:S(2)}, u32[]{:S(2)}) collective-permute-start(bf16[256,1024]{1,0:T(8,128)(2,1)} %raw.1), channel_id=1, source_target_pairs={{4,0},{12,8},{0,4},{8,12},{9,1},{5,9},{13,5},{1,13},{6,2},{14,10},... | collective-permute-start | bytes 1572872 | tf_op jit(solution)/shard_map/ppermute | solution.py:182
  3.0 0.7 %pad_add_fusion.ids = s32[3,256]{1,0:T(4,128)S(1)} fusion(s32[1,256]{1,0:T(1,128)} %bitcast.4, s32[1,256]{1,0:T(1,128)} %bitcast.5, s32[1,256]{1,0:T(1,128)} %bitcast.6), kind=kLoop, calls=%fused_computation.4 | loop fusion | flops 1536 | bytes 6144 | tf_op jit(solution)/shard_map/concatenate | solution.py:176
  3.7 0.0 collective-permute-start.4
  3.7 0.0 copy-start
  3.8 1.0 %copy-done = bf16[256,1024]{1,0:T(8,128)(2,1)S(1)} copy-done((bf16[256,1024]{1,0:T(8,128)(2,1)S(1)}, bf16[256,1024]{1,0:T(8,128)(2,1)}, u32[]{:S(2)}) %copy-start) | copy-done | bytes 524312
  4.8 0.2 pack.1.refs_0_
  5.0 4.1 %collective-permute-start.5 = (bf16[264,1024]{1,0:T(8,128)(2,1)S(1)}, bf16[264,1024]{1,0:T(8,128)(2,1)S(1)}, u32[]{:S(2)}, u32[]{:S(2)}) collective-permute-start(bf16[264,1024]{1,0:T(8,128)(2,1)S(1)} %pack.1.refs_0_), channel_id=1, source_target_pairs={{8,0},{4,8},{12,4},{0,12},{5,1},{13,9},{1,5},{9,13},{10,2},{6,10},... | collective-permute-start | bytes 1622024 | tf_op jit(solution)/shard_map/ppermute | solution.py:182
  9.1 14.2 %conditional.1 = (bf16[264,1024]{1,0:T(8,128)(2,1)}, bf16[264,1024]{1,0:T(8,128)(2,1)}, bf16[264,1024]{1,0:T(8,128)(2,1)}) conditional(s32[]{:T(128)} %convert_element_type.9, () %tuple.13, bf16[264,1024]{1,0:T(8,128)(2,1)S(1)} %pack.1.refs_0_), branch_computations={%region_0.0_spmd, %region_1.0_spmd} | conditional | bytes 6488208 | solution.py:198
  9.1 1.5 %collective-permute-start.1 = (bf16[264,1024]{1,0:T(8,128)(2,1)S(1)}, bf16[264,1024]{1,0:T(8,128)(2,1)}, u32[]{:S(2)}, u32[]{:S(2)}) collective-permute-start(bf16[264,1024]{1,0:T(8,128)(2,1)S(1)} %param.1), channel_id=1, source_target_pairs={{0,2},{2,0},{1,3},{3,1},{4,6},{6,4},{5,7},{7,5},{8,10},{10,8},{9,1... | collective-permute-start | bytes 1622024 | tf_op jit(solution)/shard_map/cond/branch_1_fun/ppermute | solution.py:192
  10.6 0.0 collective-permute-start
  10.6 10.5 %collective-permute-done.1 = bf16[264,1024]{1,0:T(8,128)(2,1)} collective-permute-done((bf16[264,1024]{1,0:T(8,128)(2,1)S(1)}, bf16[264,1024]{1,0:T(8,128)(2,1)}, u32[]{:S(2)}, u32[]{:S(2)}) %collective-permute-start.1) | collective-permute-done | bytes 540704 | tf_op jit(solution)/shard_map/cond/branch_1_fun/ppermute | solution.py:192
  21.1 0.0 collective-permute-start.2
  21.1 0.0 collective-permute-done
  21.1 2.3 %collective-permute-done.2 = bf16[264,1024]{1,0:T(8,128)(2,1)} collective-permute-done((bf16[264,1024]{1,0:T(8,128)(2,1)}, bf16[264,1024]{1,0:T(8,128)(2,1)}, u32[]{:S(2)}, u32[]{:S(2)}) %collective-permute-start.2) | collective-permute-done | bytes 540704 | tf_op jit(solution)/shard_map/cond/branch_1_fun/ppermute | solution.py:195
  23.3 1.5 %load.1 = (bf16[4,264,1024]{2,1,0:T(8,128)(2,1)S(1)}, s32[4,256]{1,0:T(4,128)S(1)}) custom-call(bf16[264,1024]{1,0:T(8,128)(2,1)S(1)} %pack.1.refs_0_, bf16[264,1024]{1,0:T(8,128)(2,1)} %get-tuple-element.13.refs_1_, bf16[264,1024]{1,0:T(8,128)(2,1)} %get-tuple-element.14.refs_2_, bf16[264,1024]{1,0:T(8,128)(2,1)} %get-tuple-element.15.refs_3_), custom_call_target="tpu_custom_call" | custom-call | tf_op jit(solution)/shard_map/load/pallas_call | solution.py:204
  24.8 0.0 collective-permute-done.3
  24.8 0.2 fusion
  25.0 0.2 fusion.1.came
  25.2 0.7 %score.1.refs_2_ = f32[256,1024]{1,0:T(8,128)S(1)} custom-call(bf16[4,264,1024]{2,1,0:T(8,128)(2,1)S(1)} %get-tuple-element.16.plane.refs_0_, bf16[256,1024]{1,0:T(8,128)(2,1)S(1)} %fusion.1.came), custom_call_target="tpu_custom_call" | custom-call | tf_op jit(solution)/shard_map/score/pallas_call | solution.py:128
  25.9 0.0 collective-permute-done.4.refs_3_
  26.0 0.4 %collective-permute-done.5.refs_4_ = bf16[264,1024]{1,0:T(8,128)(2,1)S(1)} collective-permute-done((bf16[264,1024]{1,0:T(8,128)(2,1)S(1)}, bf16[264,1024]{1,0:T(8,128)(2,1)S(1)}, u32[]{:S(2)}, u32[]{:S(2)}) %collective-permute-start.5) | collective-permute-done | bytes 540704 | tf_op jit(solution)/shard_map/ppermute | solution.py:182
  26.3 1.1 %meet.1 = (f32[4,256]{1,0:T(4,128)S(1)}, f32[2,256]{1,0:T(2,128)S(1)}) custom-call(bf16[4,264,1024]{2,1,0:T(8,128)(2,1)S(1)} %get-tuple-element.16.plane.refs_0_, s32[4,256]{1,0:T(4,128)S(1)} %get-tuple-element.17.refs_1_.codes, f32[256,1024]{1,0:T(8,128)S(1)} %score.1.refs_2_, s32[3,256]{1,0:T(4,128)S(1)} %collective-permute-done.4.refs_3_, ...), custom_call_target="tpu_custom_call" | custom-call | tf_op jit(solution)/shard_map/meet/pallas_call | solution.py:128
  27.5 1.2 %collective-permute-start.6 = (f32[2,256]{1,0:T(2,128)S(1)}, f32[2,256]{1,0:T(2,128)S(1)}, u32[]{:S(2)}, u32[]{:S(2)}) collective-permute-start(f32[2,256]{1,0:T(2,128)S(1)} %slice.21), channel_id=1, source_target_pairs={{0,1},{1,0},{2,3},{3,2},{4,5},{5,4},{6,7},{7,6},{8,9},{9,8},{10,11... | collective-permute-start | bytes 6152 | tf_op jit(solution)/shard_map/ppermute | solution.py:257
  28.7 2.4 %collective-permute-start.8 = (f32[1,256]{1,0:T(1,128)S(1)}, f32[1,256]{1,0:T(1,128)S(1)}, u32[]{:S(2)}, u32[]{:S(2)}) collective-permute-start(f32[1,256]{1,0:T(1,128)S(1)} %broadcast_select_fusion), channel_id=1, source_target_pairs={{0,8},{8,4},{4,12},{12,0},{1,9},{9,5},{5,13},{13,1},{2,10},{10,6},... | collective-permute-start | bytes 3080 | tf_op jit(solution)/shard_map/ppermute | solution.py:250
  31.2 0.0 collective-permute-done.6
  31.2 1.6 %collective-permute-start.7 = (f32[1,256]{1,0:T(1,128)S(1)}, f32[1,256]{1,0:T(1,128)S(1)}, u32[]{:S(2)}, u32[]{:S(2)}) collective-permute-start(f32[1,256]{1,0:T(1,128)S(1)} %slice.27), channel_id=1, source_target_pairs={{0,2},{2,0},{1,3},{3,1},{4,6},{6,4},{5,7},{7,5},{8,10},{10,8},{9,1... | collective-permute-start | bytes 3080 | tf_op jit(solution)/shard_map/ppermute | solution.py:260
  32.7 0.9 %own.1 = f32[1,256]{1,0:T(1,128)S(1)} custom-call(bf16[4,264,1024]{2,1,0:T(8,128)(2,1)S(1)} %get-tuple-element.16.plane.refs_0_, s32[4,256]{1,0:T(4,128)S(1)} %get-tuple-element.17.refs_1_.codes), custom_call_target="tpu_custom_call" | custom-call | tf_op jit(solution)/shard_map/own/pallas_call | solution.py:128
  33.6 0.7 %collective-permute-done.8 = f32[1,256]{1,0:T(1,128)S(1)} collective-permute-done((f32[1,256]{1,0:T(1,128)S(1)}, f32[1,256]{1,0:T(1,128)S(1)}, u32[]{:S(2)}, u32[]{:S(2)}) %collective-permute-start.8) | collective-permute-done | bytes 1056 | tf_op jit(solution)/shard_map/ppermute | solution.py:250
  34.3 0.5 %collective-permute-done.7 = f32[1,256]{1,0:T(1,128)S(1)} collective-permute-done((f32[1,256]{1,0:T(1,128)S(1)}, f32[1,256]{1,0:T(1,128)S(1)}, u32[]{:S(2)}, u32[]{:S(2)}) %collective-permute-start.7) | collective-permute-done | bytes 1056 | tf_op jit(solution)/shard_map/ppermute | solution.py:260
  34.8 0.6 %fusion.3 = f32[1,256]{1,0:T(1,128)} fusion(f32[1,256]{1,0:T(1,128)S(1)} %collective-permute-done.8, f32[1,256]{1,0:T(1,128)S(1)} %own.1, f32[1,256]{1,0:T(1,128)S(1)} %collective-permute-done.7, f32[2,256]{1,0:T(2,128)S(1)} %slice_maximum_fusion), kind=kLoop, calls=%fused_computation.9 | loop fusion | flops 768 | bytes 5120 | tf_op jit(solution)/shard_map/max | solution.py:263
  (5 shorter events, 0.0 us)
Async XLA Ops:
  0.0 24.8 %collective-permute-start.3 = (bf16[256,1024]{1,0:T(8,128)(2,1)}, bf16[256,1024]{1,0:T(8,128)(2,1)S(1)}, u32[]{:S(2)}, u32[]{:S(2)}) collective-permute-start(bf16[256,1024]{1,0:T(8,128)(2,1)} %raw.1), channel_id=1, source_target_pairs={{4,0},{12,8},{0,4},{8,12},{9,1},{5,9},{13,5},{1,13},{6,2},{14,10},... | collective-permute-start | bytes 1572872 | tf_op jit(solution)/shard_map/ppermute | solution.py:182
  3.7 22.2 %collective-permute-start.4 = (s32[3,256]{1,0:T(4,128)S(1)}, s32[3,256]{1,0:T(4,128)S(1)}, u32[]{:S(2)}, u32[]{:S(2)}) collective-permute-start(s32[3,256]{1,0:T(4,128)S(1)} %pad_add_fusion.ids), channel_id=1, source_target_pairs={{4,0},{12,8},{0,4},{8,12},{9,1},{5,9},{13,5},{1,13},{6,2},{14,10},... | collective-permute-start | bytes 9224 | tf_op jit(solution)/shard_map/ppermute | solution.py:186
  3.7 1.0 %copy-start = (bf16[256,1024]{1,0:T(8,128)(2,1)S(1)}, bf16[256,1024]{1,0:T(8,128)(2,1)}, u32[]{:S(2)}) copy-start(bf16[256,1024]{1,0:T(8,128)(2,1)} %raw.1) | copy-start | bytes 1572868
  5.0 21.4 %collective-permute-start.5 = (bf16[264,1024]{1,0:T(8,128)(2,1)S(1)}, bf16[264,1024]{1,0:T(8,128)(2,1)S(1)}, u32[]{:S(2)}, u32[]{:S(2)}) collective-permute-start(bf16[264,1024]{1,0:T(8,128)(2,1)S(1)} %pack.1.refs_0_), channel_id=1, source_target_pairs={{8,0},{4,8},{12,4},{0,12},{5,1},{13,9},{1,5},{9,13},{10,2},{6,10},... | collective-permute-start | bytes 1622024 | tf_op jit(solution)/shard_map/ppermute | solution.py:182
  9.1 12.0 %collective-permute-start.1 = (bf16[264,1024]{1,0:T(8,128)(2,1)S(1)}, bf16[264,1024]{1,0:T(8,128)(2,1)}, u32[]{:S(2)}, u32[]{:S(2)}) collective-permute-start(bf16[264,1024]{1,0:T(8,128)(2,1)S(1)} %param.1), channel_id=1, source_target_pairs={{0,2},{2,0},{1,3},{3,1},{4,6},{6,4},{5,7},{7,5},{8,10},{10,8},{9,1... | collective-permute-start | bytes 1622024 | tf_op jit(solution)/shard_map/cond/branch_1_fun/ppermute | solution.py:192
  10.6 10.5 %collective-permute-start = (bf16[264,1024]{1,0:T(8,128)(2,1)S(1)}, bf16[264,1024]{1,0:T(8,128)(2,1)}, u32[]{:S(2)}, u32[]{:S(2)}) collective-permute-start(bf16[264,1024]{1,0:T(8,128)(2,1)S(1)} %param.1), channel_id=1, source_target_pairs={{0,1},{1,0},{2,3},{3,2},{4,5},{5,4},{6,7},{7,6},{8,9},{9,8},{10,11... | collective-permute-start | bytes 1622024 | tf_op jit(solution)/shard_map/cond/branch_1_fun/ppermute | solution.py:195
  21.1 2.3 %collective-permute-start.2 = (bf16[264,1024]{1,0:T(8,128)(2,1)}, bf16[264,1024]{1,0:T(8,128)(2,1)}, u32[]{:S(2)}, u32[]{:S(2)}) collective-permute-start(bf16[264,1024]{1,0:T(8,128)(2,1)} %collective-permute-done.1), channel_id=1, source_target_pairs={{0,1},{1,0},{2,3},{3,2},{4,5},{5,4},{6,7},{7,6},{8,9},{9,8},{10,11... | collective-permute-start | bytes 1622024 | tf_op jit(solution)/shard_map/cond/branch_1_fun/ppermute | solution.py:195
  27.5 3.7 %collective-permute-start.6 = (f32[2,256]{1,0:T(2,128)S(1)}, f32[2,256]{1,0:T(2,128)S(1)}, u32[]{:S(2)}, u32[]{:S(2)}) collective-permute-start(f32[2,256]{1,0:T(2,128)S(1)} %slice.21), channel_id=1, source_target_pairs={{0,1},{1,0},{2,3},{3,2},{4,5},{5,4},{6,7},{7,6},{8,9},{9,8},{10,11... | collective-permute-start | bytes 6152 | tf_op jit(solution)/shard_map/ppermute | solution.py:257
  28.7 5.6 %collective-permute-start.8 = (f32[1,256]{1,0:T(1,128)S(1)}, f32[1,256]{1,0:T(1,128)S(1)}, u32[]{:S(2)}, u32[]{:S(2)}) collective-permute-start(f32[1,256]{1,0:T(1,128)S(1)} %broadcast_select_fusion), channel_id=1, source_target_pairs={{0,8},{8,4},{4,12},{12,0},{1,9},{9,5},{5,13},{13,1},{2,10},{10,6},... | collective-permute-start | bytes 3080 | tf_op jit(solution)/shard_map/ppermute | solution.py:250
  31.2 3.6 %collective-permute-start.7 = (f32[1,256]{1,0:T(1,128)S(1)}, f32[1,256]{1,0:T(1,128)S(1)}, u32[]{:S(2)}, u32[]{:S(2)}) collective-permute-start(f32[1,256]{1,0:T(1,128)S(1)} %slice.27), channel_id=1, source_target_pairs={{0,2},{2,0},{1,3},{3,1},{4,6},{6,4},{5,7},{7,5},{8,10},{10,8},{9,1... | collective-permute-start | bytes 3080 | tf_op jit(solution)/shard_map/ppermute | solution.py:260

commit v8 on v7

--- a/solution.py
+++ b/solution.py
@@ -90,38 +90,47 @@
         scores[:, lanes] = scores_of(came_rows, plane[index, 0:rows, :])
 
 
-def meet_kernel(rows, places, n_came, has_part, *refs):
+def meet_kernel(rows, places, n_came, has_part, odd, *refs):
     plane, codes, *refs = refs
     part = refs.pop(0) if has_part else None
-    scores, *refs = refs
-    columns = [as_column(code_in(refs.pop(0)))]
-    if n_came == 2:
-        packed = refs.pop(0)
-        came_rows = packed[0:rows, :]
-        columns.append(as_column(code_of_last(packed[...][rows : rows + EXTRA, :], rows)))
+    scores, ids, *refs = refs
+    packed = refs.pop(0) if n_came == 2 else None
     kept, back = refs
-    found = [jnp.full((rows, 128), -1.0, jnp.float32)] * n_came
-    for index, place in enumerate(places):
-        block = slice(index * rows, (index + 1) * rows)
-        tables = [scores[:, block]]
+
+    def meet(far):
+        columns = [as_column(code_in(ids))]
         if n_came == 2:
-            tables.append(scores_of(came_rows, plane[index, 0:rows, :]))
-        for at in range(0, rows, 128):
-            lanes = slice(at, at + 128)
-            other = codes[index : index + 1, lanes]
-            keep = None
-            for turn, (table, column) in enumerate(zip(tables, columns)):
-                shared = jnp.where((column ^ other) < 65536, table[:, lanes], -1.0)
-                later = column > other
-                found[turn] = jnp.maximum(found[turn], jnp.where(later, shared, -1.0))
-                kept_here = jnp.where(later, -1.0, shared)
-                keep = kept_here if keep is None else jnp.maximum(keep, kept_here)
-            keep = jnp.max(keep, axis=0, keepdims=True)
-            if has_part:
-                keep = jnp.maximum(keep, part[place : place + 1, lanes])
-            kept[place : place + 1, lanes] = keep
-    for turn in range(n_came):
-        back[turn : turn + 1, :] = fold_rows(found[turn])
+            came_rows = packed[0:rows, :]
+            columns.append(as_column(code_of_last(packed[...][rows : rows + EXTRA, :], rows)))
+        found = jnp.full((rows, 128), -1.0, jnp.float32)
+        for index, place in enumerate(places):
+            tables = [scores[:, index * rows : (index + 1) * rows]]
+            if n_came == 2:
+                tables.append(scores_of(came_rows, plane[index, 0:rows, :]))
+            for at in range(0, rows, 128):
+                lanes = slice(at, at + 128)
+                other = codes[index : index + 1, lanes]
+                keep = jnp.full((rows, 128), -1.0, jnp.float32)
+                for turn, (table, column) in enumerate(zip(tables, columns)):
+                    same, later = (column ^ other) < 65536, column > other
+                    if turn == far:
+                        shared = jnp.where(same, table[:, lanes], -1.0)
+                        found = jnp.maximum(found, jnp.where(later, shared, -1.0))
+                        keep = jnp.maximum(keep, jnp.where(later, -1.0, shared))
+                    else:
+                        earlier = same & (column < other)
+                        keep = jnp.maximum(keep, jnp.where(earlier, table[:, lanes], -1.0))
+                keep = jnp.max(keep, axis=0, keepdims=True)
+                if has_part:
+                    keep = jnp.maximum(keep, part[place : place + 1, lanes])
+                kept[place : place + 1, lanes] = keep
+        back[...] = fold_rows(found)
+
+    if n_came == 1:
+        meet(0)
+    else:
+        pl.when(odd[0] != 0)(lambda: meet(0))
+        pl.when(odd[0] == 0)(lambda: meet(1))
 
 
 def kernel(body, name, out_shape, args):
@@ -236,16 +245,15 @@
         args += (scores, came_ids[first])
         for turn in second:
             args += (came[turn],)
-        kept, back = kernel(
+        kept, back = pl.pallas_call(
             functools.partial(meet_kernel, rows, places, len(step), kept is not None),
-            "meet",
-            (struct((n_plane, rows), jnp.float32), struct((len(step), rows), jnp.float32)),
-            args,
-        )
+            out_shape=(struct((n_plane, rows), jnp.float32), struct((1, rows), jnp.float32)),
+            in_specs=[pl.BlockSpec(memory_space=pltpu.SMEM)] + [VMEM] * len(args),
+            out_specs=(VMEM, VMEM),
+            compiler_params=pltpu.CompilerParams(vmem_limit_bytes=40 * 1024 * 1024),
+            name="meet",
+        )(lax.axis_index("sub").reshape(1) % 2, *args)
         if far_turns:
-            if second:
-                even = lax.axis_index("sub") % 2 == 0
-                back = jnp.where(even, back[1:2], back[0:1])
             home = [(b, a) for a, b in far_turns[number]]
             answers.append(lax.ppermute(back, "workers", home))
     if kept is None:

time: 35.6 us -> 35.5 us (level)
    pallas_call x0 -> x1, Pallas kernels: none -> 1.14 us  [on_device(): pl.pallas_call(functools.partial(meet_kernel, rows, places, len(step), ke...]
    pallas_call x4 -> x3, Pallas kernels: 2.95 us -> 1.82 us  [kernel(): pl.pallas_call(body, out_shape=out_shape, in_specs=[VMEM] * len(args), ou...]
where the time goes in v8:
time: 35.5 us; the launch traced here: 35.3 us
  waiting for transfers between devices  14.3 us (40%)
  starting transfers between devices  13.7 us (39%)
  Pallas kernels  4.45 us (13%)
  other arithmetic  1.64 us (5%)
  local copies, waits for them, and re-layouts  1.05 us (3%)
    ppermute x1, waiting for transfers between devices, gather(): first = lax.ppermute(block, 'team', shift(n_team, dt)) if dt else block  10.5 us
    ppermute x2, starting transfers between devices, on_device(): lax.ppermute(block if mixed and i == 1 else embeddings, axes, turn)  7.12 us
    ppermute x1, starting transfers between devices, on_device(): answers.append(lax.ppermute(back, 'workers', home))  2.42 us
    ppermute x2, waiting for transfers between devices, gather(): blocks.append(lax.ppermute(first, 'sub', shift(n_sub, ds)))  2.27 us
    pallas_call x3, Pallas kernels, kernel(): pl.pallas_call(body, out_shape=out_shape, in_specs=[VMEM] * len(args), ou...  1.82 us
    ppermute x1, starting transfers between devices, on_device(): lax.ppermute(ends[dt:dt + 1], 'team', shift(n_team, -dt))  1.56 us
    ppermute x1, starting transfers between devices, gather(): first = lax.ppermute(block, 'team', shift(n_team, dt)) if dt else block  1.49 us
    pallas_call x1, Pallas kernels, on_device(): pl.pallas_call(functools.partial(load_kernel, rows), out_shape=(struct((n...  1.49 us
  transfers between devices with their start and end apart: 9, of which 5 were waited for; matrix products, arithmetic and copies ran while one was open for 3% of the time, Pallas kernels for 9%

profile of v8, /device:TPU:0, one launch (start us, length us, event | category | flops | bytes accessed | tf_op | source)
XLA Modules:
  0.0 35.3 jit_solution(7780785754159644979)
XLA Ops:
  0.0 3.0 %collective-permute-start.3 = (bf16[256,1024]{1,0:T(8,128)(2,1)}, bf16[256,1024]{1,0:T(8,128)(2,1)S(1)}, u32[]{:S(2)}, u32[]{:S(2)}) collective-permute-start(bf16[256,1024]{1,0:T(8,128)(2,1)} %raw.1), channel_id=1, source_target_pairs={{4,0},{12,8},{0,4},{8,12},{9,1},{5,9},{13,5},{1,13},{6,2},{14,10},... | collective-permute-start | bytes 1572872 | tf_op jit(solution)/shard_map/ppermute | solution.py:191
  3.0 0.7 %pad_add_fusion.ids = s32[3,256]{1,0:T(4,128)S(1)} fusion(s32[1,256]{1,0:T(1,128)} %bitcast.5, s32[1,256]{1,0:T(1,128)} %bitcast.6, s32[1,256]{1,0:T(1,128)} %bitcast.7), kind=kLoop, calls=%fused_computation.4 | loop fusion | flops 1536 | bytes 6144 | tf_op jit(solution)/shard_map/concatenate | solution.py:185
  3.7 0.0 collective-permute-start.4
  3.7 0.0 copy-start
  3.8 1.0 %copy-done = bf16[256,1024]{1,0:T(8,128)(2,1)S(1)} copy-done((bf16[256,1024]{1,0:T(8,128)(2,1)S(1)}, bf16[256,1024]{1,0:T(8,128)(2,1)}, u32[]{:S(2)}) %copy-start) | copy-done | bytes 524312
  4.8 0.2 pack.1.refs_0_
  5.0 4.1 %collective-permute-start.5 = (bf16[264,1024]{1,0:T(8,128)(2,1)S(1)}, bf16[264,1024]{1,0:T(8,128)(2,1)S(1)}, u32[]{:S(2)}, u32[]{:S(2)}) collective-permute-start(bf16[264,1024]{1,0:T(8,128)(2,1)S(1)} %pack.1.refs_0_), channel_id=1, source_target_pairs={{8,0},{4,8},{12,4},{0,12},{5,1},{13,9},{1,5},{9,13},{10,2},{6,10},... | collective-permute-start | bytes 1622024 | tf_op jit(solution)/shard_map/ppermute | solution.py:191
  9.1 14.2 %conditional.1 = (bf16[264,1024]{1,0:T(8,128)(2,1)}, bf16[264,1024]{1,0:T(8,128)(2,1)}, bf16[264,1024]{1,0:T(8,128)(2,1)}) conditional(s32[]{:T(128)} %convert_element_type.9, () %tuple.13, bf16[264,1024]{1,0:T(8,128)(2,1)S(1)} %pack.1.refs_0_), branch_computations={%region_0.0_spmd, %region_1.0_spmd} | conditional | bytes 6488208 | solution.py:207
  9.1 1.5 %collective-permute-start.1 = (bf16[264,1024]{1,0:T(8,128)(2,1)S(1)}, bf16[264,1024]{1,0:T(8,128)(2,1)}, u32[]{:S(2)}, u32[]{:S(2)}) collective-permute-start(bf16[264,1024]{1,0:T(8,128)(2,1)S(1)} %param.1), channel_id=1, source_target_pairs={{0,2},{2,0},{1,3},{3,1},{4,6},{6,4},{5,7},{7,5},{8,10},{10,8},{9,1... | collective-permute-start | bytes 1622024 | tf_op jit(solution)/shard_map/cond/branch_1_fun/ppermute | solution.py:201
  10.6 0.0 collective-permute-start
  10.6 10.5 %collective-permute-done.1 = bf16[264,1024]{1,0:T(8,128)(2,1)} collective-permute-done((bf16[264,1024]{1,0:T(8,128)(2,1)S(1)}, bf16[264,1024]{1,0:T(8,128)(2,1)}, u32[]{:S(2)}, u32[]{:S(2)}) %collective-permute-start.1) | collective-permute-done | bytes 540704 | tf_op jit(solution)/shard_map/cond/branch_1_fun/ppermute | solution.py:201
  21.1 0.0 collective-permute-start.2
  21.1 0.0 collective-permute-done
  21.1 2.3 %collective-permute-done.2 = bf16[264,1024]{1,0:T(8,128)(2,1)} collective-permute-done((bf16[264,1024]{1,0:T(8,128)(2,1)}, bf16[264,1024]{1,0:T(8,128)(2,1)}, u32[]{:S(2)}, u32[]{:S(2)}) %collective-permute-start.2) | collective-permute-done | bytes 540704 | tf_op jit(solution)/shard_map/cond/branch_1_fun/ppermute | solution.py:204
  23.3 1.5 %load.1 = (bf16[4,264,1024]{2,1,0:T(8,128)(2,1)S(1)}, s32[4,256]{1,0:T(4,128)S(1)}) custom-call(bf16[264,1024]{1,0:T(8,128)(2,1)S(1)} %pack.1.refs_0_, bf16[264,1024]{1,0:T(8,128)(2,1)} %get-tuple-element.13.refs_1_, bf16[264,1024]{1,0:T(8,128)(2,1)} %get-tuple-element.14.refs_2_, bf16[264,1024]{1,0:T(8,128)(2,1)} %get-tuple-element.15.refs_3_), custom_call_target="tpu_custom_call" | custom-call | tf_op jit(solution)/shard_map/load/pallas_call | solution.py:213
  24.8 0.0 collective-permute-done.3
  24.8 0.2 fusion
  25.0 0.2 fusion.1.came
  25.2 0.7 %score.1.refs_2_ = f32[256,1024]{1,0:T(8,128)S(1)} custom-call(bf16[4,264,1024]{2,1,0:T(8,128)(2,1)S(1)} %get-tuple-element.16.plane.refs_0_, bf16[256,1024]{1,0:T(8,128)(2,1)S(1)} %fusion.1.came), custom_call_target="tpu_custom_call" | custom-call | tf_op jit(solution)/shard_map/score/pallas_call | solution.py:137
  25.9 0.0 collective-permute-done.4.refs_3_
  26.0 0.4 %collective-permute-done.5.refs_4_ = bf16[264,1024]{1,0:T(8,128)(2,1)S(1)} collective-permute-done((bf16[264,1024]{1,0:T(8,128)(2,1)S(1)}, bf16[264,1024]{1,0:T(8,128)(2,1)S(1)}, u32[]{:S(2)}, u32[]{:S(2)}) %collective-permute-start.5) | collective-permute-done | bytes 540704 | tf_op jit(solution)/shard_map/ppermute | solution.py:191
  26.3 1.1 %meet.1 = (f32[4,256]{1,0:T(4,128)S(1)}, f32[1,256]{1,0:T(1,128)S(1)}) custom-call(s32[1]{0:T(128)S(6)} %select_n.7.odd, bf16[4,264,1024]{2,1,0:T(8,128)(2,1)S(1)} %get-tuple-element.16.plane.refs_0_, s32[4,256]{1,0:T(4,128)S(1)} %get-tuple-element.17.refs_1_.codes, f32[256,1024]{1,0:T(8,128)S(1)} %score.1.refs_2_, ...), custom_call_target="tpu_custom_call" | custom-call | tf_op jit(solution)/shard_map/meet/pallas_call | solution.py:248
  27.5 1.1 %collective-permute-start.6 = (f32[2,256]{1,0:T(2,128)S(1)}, f32[2,256]{1,0:T(2,128)S(1)}, u32[]{:S(2)}, u32[]{:S(2)}) collective-permute-start(f32[2,256]{1,0:T(2,128)S(1)} %slice.15), channel_id=1, source_target_pairs={{0,1},{1,0},{2,3},{3,2},{4,5},{5,4},{6,7},{7,6},{8,9},{9,8},{10,11... | collective-permute-start | bytes 6152 | tf_op jit(solution)/shard_map/ppermute | solution.py:265
  28.6 2.4 %collective-permute-start.8 = (f32[1,256]{1,0:T(1,128)S(1)}, f32[1,256]{1,0:T(1,128)S(1)}, u32[]{:S(2)}, u32[]{:S(2)}) collective-permute-start(f32[1,256]{1,0:T(1,128)S(1)} %get-tuple-element.19), channel_id=1, source_target_pairs={{0,8},{8,4},{4,12},{12,0},{1,9},{9,5},{5,13},{13,1},{2,10},{10,6},... | collective-permute-start | bytes 3080 | tf_op jit(solution)/shard_map/ppermute | solution.py:258
  31.1 0.0 collective-permute-done.6
  31.1 1.6 %collective-permute-start.7 = (f32[1,256]{1,0:T(1,128)S(1)}, f32[1,256]{1,0:T(1,128)S(1)}, u32[]{:S(2)}, u32[]{:S(2)}) collective-permute-start(f32[1,256]{1,0:T(1,128)S(1)} %slice.19), channel_id=1, source_target_pairs={{0,2},{2,0},{1,3},{3,1},{4,6},{6,4},{5,7},{7,5},{8,10},{10,8},{9,1... | collective-permute-start | bytes 3080 | tf_op jit(solution)/shard_map/ppermute | solution.py:268
  32.6 0.9 %own.1 = f32[1,256]{1,0:T(1,128)S(1)} custom-call(bf16[4,264,1024]{2,1,0:T(8,128)(2,1)S(1)} %get-tuple-element.16.plane.refs_0_, s32[4,256]{1,0:T(4,128)S(1)} %get-tuple-element.17.refs_1_.codes), custom_call_target="tpu_custom_call" | custom-call | tf_op jit(solution)/shard_map/own/pallas_call | solution.py:137
  33.5 0.7 %collective-permute-done.8 = f32[1,256]{1,0:T(1,128)S(1)} collective-permute-done((f32[1,256]{1,0:T(1,128)S(1)}, f32[1,256]{1,0:T(1,128)S(1)}, u32[]{:S(2)}, u32[]{:S(2)}) %collective-permute-start.8) | collective-permute-done | bytes 1056 | tf_op jit(solution)/shard_map/ppermute | solution.py:258
  34.2 0.5 %collective-permute-done.7 = f32[1,256]{1,0:T(1,128)S(1)} collective-permute-done((f32[1,256]{1,0:T(1,128)S(1)}, f32[1,256]{1,0:T(1,128)S(1)}, u32[]{:S(2)}, u32[]{:S(2)}) %collective-permute-start.7) | collective-permute-done | bytes 1056 | tf_op jit(solution)/shard_map/ppermute | solution.py:268
  34.7 0.6 %fusion.3 = f32[1,256]{1,0:T(1,128)} fusion(f32[1,256]{1,0:T(1,128)S(1)} %collective-permute-done.8, f32[1,256]{1,0:T(1,128)S(1)} %own.1, f32[1,256]{1,0:T(1,128)S(1)} %collective-permute-done.7, f32[2,256]{1,0:T(2,128)S(1)} %slice_maximum_fusion), kind=kLoop, calls=%fused_computation.8 | loop fusion | flops 768 | bytes 5120 | tf_op jit(solution)/shard_map/max | solution.py:271
  (4 shorter events, 0.0 us)
Async XLA Ops:
  0.0 24.8 %collective-permute-start.3 = (bf16[256,1024]{1,0:T(8,128)(2,1)}, bf16[256,1024]{1,0:T(8,128)(2,1)S(1)}, u32[]{:S(2)}, u32[]{:S(2)}) collective-permute-start(bf16[256,1024]{1,0:T(8,128)(2,1)} %raw.1), channel_id=1, source_target_pairs={{4,0},{12,8},{0,4},{8,12},{9,1},{5,9},{13,5},{1,13},{6,2},{14,10},... | collective-permute-start | bytes 1572872 | tf_op jit(solution)/shard_map/ppermute | solution.py:191
  3.7 22.2 %collective-permute-start.4 = (s32[3,256]{1,0:T(4,128)S(1)}, s32[3,256]{1,0:T(4,128)S(1)}, u32[]{:S(2)}, u32[]{:S(2)}) collective-permute-start(s32[3,256]{1,0:T(4,128)S(1)} %pad_add_fusion.ids), channel_id=1, source_target_pairs={{4,0},{12,8},{0,4},{8,12},{9,1},{5,9},{13,5},{1,13},{6,2},{14,10},... | collective-permute-start | bytes 9224 | tf_op jit(solution)/shard_map/ppermute | solution.py:195
  3.7 1.0 %copy-start = (bf16[256,1024]{1,0:T(8,128)(2,1)S(1)}, bf16[256,1024]{1,0:T(8,128)(2,1)}, u32[]{:S(2)}) copy-start(bf16[256,1024]{1,0:T(8,128)(2,1)} %raw.1) | copy-start | bytes 1572868
  5.0 21.4 %collective-permute-start.5 = (bf16[264,1024]{1,0:T(8,128)(2,1)S(1)}, bf16[264,1024]{1,0:T(8,128)(2,1)S(1)}, u32[]{:S(2)}, u32[]{:S(2)}) collective-permute-start(bf16[264,1024]{1,0:T(8,128)(2,1)S(1)} %pack.1.refs_0_), channel_id=1, source_target_pairs={{8,0},{4,8},{12,4},{0,12},{5,1},{13,9},{1,5},{9,13},{10,2},{6,10},... | collective-permute-start | bytes 1622024 | tf_op jit(solution)/shard_map/ppermute | solution.py:191
  9.1 12.0 %collective-permute-start.1 = (bf16[264,1024]{1,0:T(8,128)(2,1)S(1)}, bf16[264,1024]{1,0:T(8,128)(2,1)}, u32[]{:S(2)}, u32[]{:S(2)}) collective-permute-start(bf16[264,1024]{1,0:T(8,128)(2,1)S(1)} %param.1), channel_id=1, source_target_pairs={{0,2},{2,0},{1,3},{3,1},{4,6},{6,4},{5,7},{7,5},{8,10},{10,8},{9,1... | collective-permute-start | bytes 1622024 | tf_op jit(solution)/shard_map/cond/branch_1_fun/ppermute | solution.py:201
  10.6 10.5 %collective-permute-start = (bf16[264,1024]{1,0:T(8,128)(2,1)S(1)}, bf16[264,1024]{1,0:T(8,128)(2,1)}, u32[]{:S(2)}, u32[]{:S(2)}) collective-permute-start(bf16[264,1024]{1,0:T(8,128)(2,1)S(1)} %param.1), channel_id=1, source_target_pairs={{0,1},{1,0},{2,3},{3,2},{4,5},{5,4},{6,7},{7,6},{8,9},{9,8},{10,11... | collective-permute-start | bytes 1622024 | tf_op jit(solution)/shard_map/cond/branch_1_fun/ppermute | solution.py:204
  21.1 2.3 %collective-permute-start.2 = (bf16[264,1024]{1,0:T(8,128)(2,1)}, bf16[264,1024]{1,0:T(8,128)(2,1)}, u32[]{:S(2)}, u32[]{:S(2)}) collective-permute-start(bf16[264,1024]{1,0:T(8,128)(2,1)} %collective-permute-done.1), channel_id=1, source_target_pairs={{0,1},{1,0},{2,3},{3,2},{4,5},{5,4},{6,7},{7,6},{8,9},{9,8},{10,11... | collective-permute-start | bytes 1622024 | tf_op jit(solution)/shard_map/cond/branch_1_fun/ppermute | solution.py:204
  27.5 3.6 %collective-permute-start.6 = (f32[2,256]{1,0:T(2,128)S(1)}, f32[2,256]{1,0:T(2,128)S(1)}, u32[]{:S(2)}, u32[]{:S(2)}) collective-permute-start(f32[2,256]{1,0:T(2,128)S(1)} %slice.15), channel_id=1, source_target_pairs={{0,1},{1,0},{2,3},{3,2},{4,5},{5,4},{6,7},{7,6},{8,9},{9,8},{10,11... | collective-permute-start | bytes 6152 | tf_op jit(solution)/shard_map/ppermute | solution.py:265
  28.6 5.6 %collective-permute-start.8 = (f32[1,256]{1,0:T(1,128)S(1)}, f32[1,256]{1,0:T(1,128)S(1)}, u32[]{:S(2)}, u32[]{:S(2)}) collective-permute-start(f32[1,256]{1,0:T(1,128)S(1)} %get-tuple-element.19), channel_id=1, source_target_pairs={{0,8},{8,4},{4,12},{12,0},{1,9},{9,5},{5,13},{13,1},{2,10},{10,6},... | collective-permute-start | bytes 3080 | tf_op jit(solution)/shard_map/ppermute | solution.py:258
  31.1 3.6 %collective-permute-start.7 = (f32[1,256]{1,0:T(1,128)S(1)}, f32[1,256]{1,0:T(1,128)S(1)}, u32[]{:S(2)}, u32[]{:S(2)}) collective-permute-start(f32[1,256]{1,0:T(1,128)S(1)} %slice.19), channel_id=1, source_target_pairs={{0,2},{2,0},{1,3},{3,1},{4,6},{6,4},{5,7},{7,5},{8,10},{10,8},{9,1... | collective-permute-start | bytes 3080 | tf_op jit(solution)/shard_map/ppermute | solution.py:268

commit v9 on v8

--- a/solution.py
+++ b/solution.py
@@ -90,7 +90,7 @@
         scores[:, lanes] = scores_of(came_rows, plane[index, 0:rows, :])
 
 
-def meet_kernel(rows, places, n_came, has_part, odd, *refs):
+def meet_kernel(rows, n_plane, n_came, has_part, odd, *refs):
     plane, codes, *refs = refs
     part = refs.pop(0) if has_part else None
     scores, ids, *refs = refs
@@ -103,7 +103,7 @@
             came_rows = packed[0:rows, :]
             columns.append(as_column(code_of_last(packed[...][rows : rows + EXTRA, :], rows)))
         found = jnp.full((rows, 128), -1.0, jnp.float32)
-        for index, place in enumerate(places):
+        for index in range(n_plane):
             tables = [scores[:, index * rows : (index + 1) * rows]]
             if n_came == 2:
                 tables.append(scores_of(came_rows, plane[index, 0:rows, :]))
@@ -122,8 +122,8 @@
                         keep = jnp.maximum(keep, jnp.where(earlier, table[:, lanes], -1.0))
                 keep = jnp.max(keep, axis=0, keepdims=True)
                 if has_part:
-                    keep = jnp.maximum(keep, part[place : place + 1, lanes])
-                kept[place : place + 1, lanes] = keep
+                    keep = jnp.maximum(keep, part[index : index + 1, lanes])
+                kept[index : index + 1, lanes] = keep
         back[...] = fold_rows(found)
 
     if n_came == 1:
@@ -228,7 +228,6 @@
         (struct((1, rows), jnp.float32),),
         (plane, codes),
     )
-    places = [ds * n_team + dt for dt in range(n_team) for ds in range(n_sub)]
     kept, answers = None, []
     steps = [[i] for i in range(len(turns))]
     if mixed:
@@ -246,7 +245,7 @@
         for turn in second:
             args += (came[turn],)
         kept, back = pl.pallas_call(
-            functools.partial(meet_kernel, rows, places, len(step), kept is not None),
+            functools.partial(meet_kernel, rows, n_plane, len(step), kept is not None),
             out_shape=(struct((n_plane, rows), jnp.float32), struct((1, rows), jnp.float32)),
             in_specs=[pl.BlockSpec(memory_space=pltpu.SMEM)] + [VMEM] * len(args),
             out_specs=(VMEM, VMEM),
@@ -259,13 +258,13 @@
     if kept is None:
         kept = jnp.full((n_plane, rows), -1.0, jnp.float32)
 
-    kept = kept.reshape(n_sub, n_team, rows)
+    kept = kept.reshape(n_team, n_sub, rows)
     ends = kept[0]
+    for dt in range(1, n_team):
+        ends = jnp.maximum(ends, lax.ppermute(kept[dt], "team", shift(n_team, -dt)))
+    best = ends[0:1]
     for ds in range(1, n_sub):
-        ends = jnp.maximum(ends, lax.ppermute(kept[ds], "sub", shift(n_sub, -ds)))
-    best = ends[0:1]
-    for dt in range(1, n_team):
-        best = jnp.maximum(best, lax.ppermute(ends[dt : dt + 1], "team", shift(n_team, -dt)))
+        best = jnp.maximum(best, lax.ppermute(ends[ds : ds + 1], "sub", shift(n_sub, -ds)))
     best = jnp.maximum(best, own)
     for answer in answers:
         best = jnp.maximum(best, answer)

time: 35.5 us -> 35.7 us (level)
  waiting for transfers between devices: 14.3 us -> 14.9 us
  starting transfers between devices: 13.7 us -> 13.3 us
    ppermute x2, starting transfers between devices: 2.69 us -> 1.62 us  [the longest x1 1.55 us: on_device(): ends = jnp.maximum(ends, lax.ppermute(kept[dt], 'team', shift(n_team, -dt)))]
    ppermute x1, waiting for transfers between devices: 0.7 us -> 1.75 us  [on_device(): answers.append(lax.ppermute(back, 'workers', home))]
    ppermute x1, starting transfers between devices: 2.42 us -> 3.08 us  [on_device(): answers.append(lax.ppermute(back, 'workers', home))]
    ppermute x2, waiting for transfers between devices: 0.47 us -> 0.01 us  [the longest x1 0.01 us: on_device(): ends = jnp.maximum(ends, lax.ppermute(kept[dt], 'team', shift(n_team, -dt)))]
  transfers between devices with their start and end apart: 9 -> 9, of which waited for: 5 -> 4; matrix products, arithmetic and copies ran while one was open for 3% -> 3% of each run, Pallas kernels for 9% -> 9%
where the time goes in v9:
time: 35.7 us; the launch traced here: 35.5 us
  waiting for transfers between devices  14.9 us (42%)
  starting transfers between devices  13.3 us (37%)
  Pallas kernels  4.45 us (12%)
  other arithmetic  1.64 us (5%)
  local copies, waits for them, and re-layouts  1.05 us (3%)
    ppermute x1, waiting for transfers between devices, gather(): first = lax.ppermute(block, 'team', shift(n_team, dt)) if dt else block  10.5 us
    ppermute x2, starting transfers between devices, on_device(): lax.ppermute(block if mixed and i == 1 else embeddings, axes, turn)  7.12 us
    ppermute x1, starting transfers between devices, on_device(): answers.append(lax.ppermute(back, 'workers', home))  3.08 us
    ppermute x2, waiting for transfers between devices, gather(): blocks.append(lax.ppermute(first, 'sub', shift(n_sub, ds)))  2.27 us
    pallas_call x3, Pallas kernels, kernel(): pl.pallas_call(body, out_shape=out_shape, in_specs=[VMEM] * len(args), ou...  1.83 us
    ppermute x1, waiting for transfers between devices, on_device(): answers.append(lax.ppermute(back, 'workers', home))  1.75 us
    ppermute x1, starting transfers between devices, on_device(): ends = jnp.maximum(ends, lax.ppermute(kept[dt], 'team', shift(n_team, -dt)))  1.55 us
    ppermute x1, starting transfers between devices, gather(): first = lax.ppermute(block, 'team', shift(n_team, dt)) if dt else block  1.49 us
  transfers between devices with their start and end apart: 9, of which 4 were waited for; matrix products, arithmetic and copies ran while one was open for 3% of the time, Pallas kernels for 9%

profile of v9, /device:TPU:0, one launch (start us, length us, event | category | flops | bytes accessed | tf_op | source)
XLA Modules:
  0.0 35.5 jit_solution(5866606121868317652)
XLA Ops:
  0.0 3.0 %collective-permute-start.3 = (bf16[256,1024]{1,0:T(8,128)(2,1)}, bf16[256,1024]{1,0:T(8,128)(2,1)S(1)}, u32[]{:S(2)}, u32[]{:S(2)}) collective-permute-start(bf16[256,1024]{1,0:T(8,128)(2,1)} %raw.1), channel_id=1, source_target_pairs={{4,0},{12,8},{0,4},{8,12},{9,1},{5,9},{13,5},{1,13},{6,2},{14,10},... | collective-permute-start | bytes 1572872 | tf_op jit(solution)/shard_map/ppermute | solution.py:191
  3.0 0.7 %pad_add_fusion.ids = s32[3,256]{1,0:T(4,128)S(1)} fusion(s32[1,256]{1,0:T(1,128)} %bitcast.5, s32[1,256]{1,0:T(1,128)} %bitcast.6, s32[1,256]{1,0:T(1,128)} %bitcast.7), kind=kLoop, calls=%fused_computation.4 | loop fusion | flops 1536 | bytes 6144 | tf_op jit(solution)/shard_map/concatenate | solution.py:185
  3.7 0.0 collective-permute-start.4
  3.7 0.0 copy-start
  3.8 1.0 %copy-done = bf16[256,1024]{1,0:T(8,128)(2,1)S(1)} copy-done((bf16[256,1024]{1,0:T(8,128)(2,1)S(1)}, bf16[256,1024]{1,0:T(8,128)(2,1)}, u32[]{:S(2)}) %copy-start) | copy-done | bytes 524312
  4.8 0.2 pack.1.refs_0_
  5.0 4.1 %collective-permute-start.5 = (bf16[264,1024]{1,0:T(8,128)(2,1)S(1)}, bf16[264,1024]{1,0:T(8,128)(2,1)S(1)}, u32[]{:S(2)}, u32[]{:S(2)}) collective-permute-start(bf16[264,1024]{1,0:T(8,128)(2,1)S(1)} %pack.1.refs_0_), channel_id=1, source_target_pairs={{8,0},{4,8},{12,4},{0,12},{5,1},{13,9},{1,5},{9,13},{10,2},{6,10},... | collective-permute-start | bytes 1622024 | tf_op jit(solution)/shard_map/ppermute | solution.py:191
  9.1 14.2 %conditional.1 = (bf16[264,1024]{1,0:T(8,128)(2,1)}, bf16[264,1024]{1,0:T(8,128)(2,1)}, bf16[264,1024]{1,0:T(8,128)(2,1)}) conditional(s32[]{:T(128)} %convert_element_type.9, () %tuple.13, bf16[264,1024]{1,0:T(8,128)(2,1)S(1)} %pack.1.refs_0_), branch_computations={%region_0.0_spmd, %region_1.0_spmd} | conditional | bytes 6488208 | solution.py:207
  9.1 1.5 %collective-permute-start.1 = (bf16[264,1024]{1,0:T(8,128)(2,1)S(1)}, bf16[264,1024]{1,0:T(8,128)(2,1)}, u32[]{:S(2)}, u32[]{:S(2)}) collective-permute-start(bf16[264,1024]{1,0:T(8,128)(2,1)S(1)} %param.1), channel_id=1, source_target_pairs={{0,2},{2,0},{1,3},{3,1},{4,6},{6,4},{5,7},{7,5},{8,10},{10,8},{9,1... | collective-permute-start | bytes 1622024 | tf_op jit(solution)/shard_map/cond/branch_1_fun/ppermute | solution.py:201
  10.6 0.0 collective-permute-start
  10.6 10.5 %collective-permute-done.1 = bf16[264,1024]{1,0:T(8,128)(2,1)} collective-permute-done((bf16[264,1024]{1,0:T(8,128)(2,1)S(1)}, bf16[264,1024]{1,0:T(8,128)(2,1)}, u32[]{:S(2)}, u32[]{:S(2)}) %collective-permute-start.1) | collective-permute-done | bytes 540704 | tf_op jit(solution)/shard_map/cond/branch_1_fun/ppermute | solution.py:201
  21.1 0.0 collective-permute-start.2
  21.1 0.0 collective-permute-done
  21.1 2.3 %collective-permute-done.2 = bf16[264,1024]{1,0:T(8,128)(2,1)} collective-permute-done((bf16[264,1024]{1,0:T(8,128)(2,1)}, bf16[264,1024]{1,0:T(8,128)(2,1)}, u32[]{:S(2)}, u32[]{:S(2)}) %collective-permute-start.2) | collective-permute-done | bytes 540704 | tf_op jit(solution)/shard_map/cond/branch_1_fun/ppermute | solution.py:204
  23.3 1.5 %load.1 = (bf16[4,264,1024]{2,1,0:T(8,128)(2,1)S(1)}, s32[4,256]{1,0:T(4,128)S(1)}) custom-call(bf16[264,1024]{1,0:T(8,128)(2,1)S(1)} %pack.1.refs_0_, bf16[264,1024]{1,0:T(8,128)(2,1)} %get-tuple-element.13.refs_1_, bf16[264,1024]{1,0:T(8,128)(2,1)} %get-tuple-element.14.refs_2_, bf16[264,1024]{1,0:T(8,128)(2,1)} %get-tuple-element.15.refs_3_), custom_call_target="tpu_custom_call" | custom-call | tf_op jit(solution)/shard_map/load/pallas_call | solution.py:213
  24.8 0.0 collective-permute-done.3
  24.8 0.2 fusion
  25.0 0.2 fusion.1.came
  25.2 0.7 %score.1.refs_2_ = f32[256,1024]{1,0:T(8,128)S(1)} custom-call(bf16[4,264,1024]{2,1,0:T(8,128)(2,1)S(1)} %get-tuple-element.16.plane.refs_0_, bf16[256,1024]{1,0:T(8,128)(2,1)S(1)} %fusion.1.came), custom_call_target="tpu_custom_call" | custom-call | tf_op jit(solution)/shard_map/score/pallas_call | solution.py:137
  25.9 0.0 collective-permute-done.4.refs_3_
  26.0 0.4 %collective-permute-done.5.refs_4_ = bf16[264,1024]{1,0:T(8,128)(2,1)S(1)} collective-permute-done((bf16[264,1024]{1,0:T(8,128)(2,1)S(1)}, bf16[264,1024]{1,0:T(8,128)(2,1)S(1)}, u32[]{:S(2)}, u32[]{:S(2)}) %collective-permute-start.5) | collective-permute-done | bytes 540704 | tf_op jit(solution)/shard_map/ppermute | solution.py:191
  26.3 1.1 %meet.1 = (f32[4,256]{1,0:T(4,128)S(1)}, f32[1,256]{1,0:T(1,128)S(1)}) custom-call(s32[1]{0:T(128)S(6)} %select_n.7.odd, bf16[4,264,1024]{2,1,0:T(8,128)(2,1)S(1)} %get-tuple-element.16.plane.refs_0_, s32[4,256]{1,0:T(4,128)S(1)} %get-tuple-element.17.refs_1_.codes, f32[256,1024]{1,0:T(8,128)S(1)} %score.1.refs_2_, ...), custom_call_target="tpu_custom_call" | custom-call | tf_op jit(solution)/shard_map/meet/pallas_call | solution.py:247
  27.5 1.6 %collective-permute-start.6 = (f32[2,256]{1,0:T(2,128)S(1)}, f32[2,256]{1,0:T(2,128)S(1)}, u32[]{:S(2)}, u32[]{:S(2)}) collective-permute-start(f32[2,256]{1,0:T(2,128)S(1)} %slice.15), channel_id=1, source_target_pairs={{0,2},{2,0},{1,3},{3,1},{4,6},{6,4},{5,7},{7,5},{8,10},{10,8},{9,1... | collective-permute-start | bytes 6152 | tf_op jit(solution)/shard_map/ppermute | solution.py:264
  29.1 3.1 %collective-permute-start.8 = (f32[1,256]{1,0:T(1,128)S(1)}, f32[1,256]{1,0:T(1,128)S(1)}, u32[]{:S(2)}, u32[]{:S(2)}) collective-permute-start(f32[1,256]{1,0:T(1,128)S(1)} %get-tuple-element.19), channel_id=1, source_target_pairs={{0,8},{8,4},{4,12},{12,0},{1,9},{9,5},{5,13},{13,1},{2,10},{10,6},... | collective-permute-start | bytes 3080 | tf_op jit(solution)/shard_map/ppermute | solution.py:257
  32.1 0.0 collective-permute-done.6
  32.2 0.1 collective-permute-start.7
  32.2 0.9 %own.1 = f32[1,256]{1,0:T(1,128)S(1)} custom-call(bf16[4,264,1024]{2,1,0:T(8,128)(2,1)S(1)} %get-tuple-element.16.plane.refs_0_, s32[4,256]{1,0:T(4,128)S(1)} %get-tuple-element.17.refs_1_.codes), custom_call_target="tpu_custom_call" | custom-call | tf_op jit(solution)/shard_map/own/pallas_call | solution.py:137
  33.1 1.7 %collective-permute-done.8 = f32[1,256]{1,0:T(1,128)S(1)} collective-permute-done((f32[1,256]{1,0:T(1,128)S(1)}, f32[1,256]{1,0:T(1,128)S(1)}, u32[]{:S(2)}, u32[]{:S(2)}) %collective-permute-start.8) | collective-permute-done | bytes 1056 | tf_op jit(solution)/shard_map/ppermute | solution.py:257
  34.9 0.0 collective-permute-done.7
  34.9 0.6 %fusion.3 = f32[1,256]{1,0:T(1,128)} fusion(f32[1,256]{1,0:T(1,128)S(1)} %collective-permute-done.8, f32[1,256]{1,0:T(1,128)S(1)} %own.1, f32[1,256]{1,0:T(1,128)S(1)} %collective-permute-done.7, f32[2,256]{1,0:T(2,128)S(1)} %slice_maximum_fusion), kind=kLoop, calls=%fused_computation.8 | loop fusion | flops 768 | bytes 5120 | tf_op jit(solution)/shard_map/max | solution.py:270
  (4 shorter events, 0.0 us)
Async XLA Ops:
  0.0 24.8 %collective-permute-start.3 = (bf16[256,1024]{1,0:T(8,128)(2,1)}, bf16[256,1024]{1,0:T(8,128)(2,1)S(1)}, u32[]{:S(2)}, u32[]{:S(2)}) collective-permute-start(bf16[256,1024]{1,0:T(8,128)(2,1)} %raw.1), channel_id=1, source_target_pairs={{4,0},{12,8},{0,4},{8,12},{9,1},{5,9},{13,5},{1,13},{6,2},{14,10},... | collective-permute-start | bytes 1572872 | tf_op jit(solution)/shard_map/ppermute | solution.py:191
  3.7 22.2 %collective-permute-start.4 = (s32[3,256]{1,0:T(4,128)S(1)}, s32[3,256]{1,0:T(4,128)S(1)}, u32[]{:S(2)}, u32[]{:S(2)}) collective-permute-start(s32[3,256]{1,0:T(4,128)S(1)} %pad_add_fusion.ids), channel_id=1, source_target_pairs={{4,0},{12,8},{0,4},{8,12},{9,1},{5,9},{13,5},{1,13},{6,2},{14,10},... | collective-permute-start | bytes 9224 | tf_op jit(solution)/shard_map/ppermute | solution.py:195
  3.7 1.0 %copy-start = (bf16[256,1024]{1,0:T(8,128)(2,1)S(1)}, bf16[256,1024]{1,0:T(8,128)(2,1)}, u32[]{:S(2)}) copy-start(bf16[256,1024]{1,0:T(8,128)(2,1)} %raw.1) | copy-start | bytes 1572868
  5.0 21.4 %collective-permute-start.5 = (bf16[264,1024]{1,0:T(8,128)(2,1)S(1)}, bf16[264,1024]{1,0:T(8,128)(2,1)S(1)}, u32[]{:S(2)}, u32[]{:S(2)}) collective-permute-start(bf16[264,1024]{1,0:T(8,128)(2,1)S(1)} %pack.1.refs_0_), channel_id=1, source_target_pairs={{8,0},{4,8},{12,4},{0,12},{5,1},{13,9},{1,5},{9,13},{10,2},{6,10},... | collective-permute-start | bytes 1622024 | tf_op jit(solution)/shard_map/ppermute | solution.py:191
  9.1 12.0 %collective-permute-start.1 = (bf16[264,1024]{1,0:T(8,128)(2,1)S(1)}, bf16[264,1024]{1,0:T(8,128)(2,1)}, u32[]{:S(2)}, u32[]{:S(2)}) collective-permute-start(bf16[264,1024]{1,0:T(8,128)(2,1)S(1)} %param.1), channel_id=1, source_target_pairs={{0,2},{2,0},{1,3},{3,1},{4,6},{6,4},{5,7},{7,5},{8,10},{10,8},{9,1... | collective-permute-start | bytes 1622024 | tf_op jit(solution)/shard_map/cond/branch_1_fun/ppermute | solution.py:201
  10.6 10.5 %collective-permute-start = (bf16[264,1024]{1,0:T(8,128)(2,1)S(1)}, bf16[264,1024]{1,0:T(8,128)(2,1)}, u32[]{:S(2)}, u32[]{:S(2)}) collective-permute-start(bf16[264,1024]{1,0:T(8,128)(2,1)S(1)} %param.1), channel_id=1, source_target_pairs={{0,1},{1,0},{2,3},{3,2},{4,5},{5,4},{6,7},{7,6},{8,9},{9,8},{10,11... | collective-permute-start | bytes 1622024 | tf_op jit(solution)/shard_map/cond/branch_1_fun/ppermute | solution.py:204
  21.1 2.3 %collective-permute-start.2 = (bf16[264,1024]{1,0:T(8,128)(2,1)}, bf16[264,1024]{1,0:T(8,128)(2,1)}, u32[]{:S(2)}, u32[]{:S(2)}) collective-permute-start(bf16[264,1024]{1,0:T(8,128)(2,1)} %collective-permute-done.1), channel_id=1, source_target_pairs={{0,1},{1,0},{2,3},{3,2},{4,5},{5,4},{6,7},{7,6},{8,9},{9,8},{10,11... | collective-permute-start | bytes 1622024 | tf_op jit(solution)/shard_map/cond/branch_1_fun/ppermute | solution.py:204
  27.5 4.6 %collective-permute-start.6 = (f32[2,256]{1,0:T(2,128)S(1)}, f32[2,256]{1,0:T(2,128)S(1)}, u32[]{:S(2)}, u32[]{:S(2)}) collective-permute-start(f32[2,256]{1,0:T(2,128)S(1)} %slice.15), channel_id=1, source_target_pairs={{0,2},{2,0},{1,3},{3,1},{4,6},{6,4},{5,7},{7,5},{8,10},{10,8},{9,1... | collective-permute-start | bytes 6152 | tf_op jit(solution)/shard_map/ppermute | solution.py:264
  29.1 5.8 %collective-permute-start.8 = (f32[1,256]{1,0:T(1,128)S(1)}, f32[1,256]{1,0:T(1,128)S(1)}, u32[]{:S(2)}, u32[]{:S(2)}) collective-permute-start(f32[1,256]{1,0:T(1,128)S(1)} %get-tuple-element.19), channel_id=1, source_target_pairs={{0,8},{8,4},{4,12},{12,0},{1,9},{9,5},{5,13},{13,1},{2,10},{10,6},... | collective-permute-start | bytes 3080 | tf_op jit(solution)/shard_map/ppermute | solution.py:257
  32.2 2.7 %collective-permute-start.7 = (f32[1,256]{1,0:T(1,128)S(1)}, f32[1,256]{1,0:T(1,128)S(1)}, u32[]{:S(2)}, u32[]{:S(2)}) collective-permute-start(f32[1,256]{1,0:T(1,128)S(1)} %slice.19), channel_id=1, source_target_pairs={{0,1},{1,0},{2,3},{3,2},{4,5},{5,4},{6,7},{7,6},{8,9},{9,8},{10,11... | collective-permute-start | bytes 3080 | tf_op jit(solution)/shard_map/ppermute | solution.py:267
